TPU v7x, 32 devices: a whole 2x2x4 slice. The times are simulated.
32 devices in a mesh: group: 2 (over x), seq: 16 (over z, y, core).
Axes of the slice: x: 2, y: 2, z: 4, core: 2. Of those that a mesh axis runs over, the one named last changes fastest.
Arguments:
- query: bfloat16 [8192, 2048], P(('group', 'seq')), parts along dimension 0, may hold values from -6 to 6
- key_in: bfloat16 [8192, 2048], P(('group', 'seq')), parts along dimension 0, may hold values from -6 to 6
- value: bfloat16 [8192, 2048], P(('group', 'seq')), parts along dimension 0, may hold values from -6 to 6
- d_out: bfloat16 [8192, 2048], P(('group', 'seq')), parts along dimension 0, may hold values from -6 to 6
Outputs:
- output: bfloat16 [8192, 2048], P(('group', 'seq')), parts along dimension 0
- d_query: bfloat16 [8192, 2048], P(('group', 'seq')), parts along dimension 0
- d_key: bfloat16 [8192, 2048], P(('group', 'seq')), parts along dimension 0
- d_value: bfloat16 [8192, 2048], P(('group', 'seq')), parts along dimension 0
There are 2 independent parts, one for each index of `group`. A program takes and returns all parts, laid end to end along the dimension named above; each array names one. Nothing has to cross between parts.
All inputs are finite; a program needn't handle non-finite values.
Results may differ from a plain program's by a relative error of at most 0.0059.
Values sent between devices are 32-bit elements; how exact they have to be, the bound alone decides.
No kernel may reach another device: no remote copies, remote signals or barrier semaphores. Data moves between devices by JAX's collectives and lax.ppermute only.
A program may use at most 320 MiB of HBM per device.

v0:
```python
import jax
import jax.numpy as jnp
from jax import lax
from jax.sharding import PartitionSpec as P

H = 16
DH = 128


def carried_in(array, axis, combine, identity, reverse):
    length, place = (lax.axis_size(axis), lax.axis_index(axis))
    everything = lax.all_gather(array, axis)
    start = jnp.broadcast_to(jnp.asarray(identity, array.dtype), array.shape)

    def lap(k, before):
        at = length - 1 - k if reverse else k
        reached = at > place if reverse else at < place
        new = combine(before, everything[at])
        return jnp.where(reached, new, before)

    return lax.fori_loop(0, length, lap, start)


def add_states(earlier, later):
    return jax.tree.map(lambda first, second: first + second, earlier, later)


def body(query, key_in, value, d_out):
    count = query.shape[0]
    heads = H
    width = DH
    shape = (count, heads, width)
    qblk = query.reshape(shape)
    kblk = key_in.reshape(shape)
    vblk = value.reshape(shape)
    where = lax.axis_index("seq") * count + lax.iota(jnp.int32, count)
    rscale = 1.0 / jnp.sqrt(width * (where.astype(jnp.float32) + 1.0))
    scaled = (d_out.reshape(shape).astype(jnp.float32) * rscale[:, None, None]).astype(jnp.bfloat16)
    local_kv = jnp.einsum("thd,the->hde", kblk, vblk, preferred_element_type=jnp.float32)
    local_qg = jnp.einsum("thd,the->hde", qblk, scaled, preferred_element_type=jnp.float32)
    zeros_state = jnp.zeros_like(local_kv)
    before_kv = carried_in(local_kv, "seq", add_states, zeros_state, False)
    after_qg = carried_in(local_qg, "seq", add_states, zeros_state, True)
    kv_state = before_kv.astype(jnp.bfloat16)
    grad_state = after_qg.astype(jnp.bfloat16)
    rows_idx = lax.broadcasted_iota(jnp.int32, (count, count), 0)
    cols_idx = lax.broadcasted_iota(jnp.int32, (count, count), 1)
    causal = (cols_idx <= rows_idx)[None, :, :]
    raw_scores = jnp.einsum("thd,shd->hts", qblk, kblk, preferred_element_type=jnp.float32)
    scores = jnp.where(causal, raw_scores, 0.0).astype(jnp.bfloat16)
    mixed = jnp.einsum("hts,shd->thd", scores, vblk, preferred_element_type=jnp.float32)
    mixed = mixed + jnp.einsum("thd,hde->the", qblk, kv_state, preferred_element_type=jnp.float32)
    output = (mixed * rscale[:, None, None]).astype(jnp.bfloat16)
    raw_back = jnp.einsum("the,she->hts", scaled, vblk, preferred_element_type=jnp.float32)
    back = jnp.where(causal, raw_back, 0.0).astype(jnp.bfloat16)
    d_query = jnp.einsum("hts,shd->thd", back, kblk, preferred_element_type=jnp.float32)
    d_query = d_query + jnp.einsum(
        "the,hde->thd", scaled, kv_state, preferred_element_type=jnp.float32
    )
    d_key = jnp.einsum("hts,thd->shd", back, qblk, preferred_element_type=jnp.float32)
    d_key = d_key + jnp.einsum("she,hde->shd", vblk, grad_state, preferred_element_type=jnp.float32)
    d_value = jnp.einsum("hts,the->she", scores, scaled, preferred_element_type=jnp.float32)
    d_value = d_value + jnp.einsum(
        "shd,hde->she", kblk, grad_state, preferred_element_type=jnp.float32
    )
    flat = (count, heads * width)
    return (
        output.reshape(flat),
        d_query.astype(jnp.bfloat16).reshape(flat),
        d_key.astype(jnp.bfloat16).reshape(flat),
        d_value.astype(jnp.bfloat16).reshape(flat),
    )


def solution(mesh):
    in_specs = (
        P(("group", "seq"), None),
        P(("group", "seq"), None),
        P(("group", "seq"), None),
        P(("group", "seq"), None),
    )
    out_specs = (
        P(("group", "seq"), None),
        P(("group", "seq"), None),
        P(("group", "seq"), None),
        P(("group", "seq"), None),
    )
    return jax.shard_map(body, mesh=mesh, in_specs=in_specs, out_specs=out_specs, check_vma=False)
```

profile of v0, /device:TPU:0, one launch (start us, length us, event | category | flops | bytes accessed | tf_op | source)
XLA Modules:
  0.0 317.7 jit_solution(13159309231180458982)
XLA Ops:
  11.6 1.6 copy.37
  13.2 1.9 multiply_convert_fusion
  17.9 2.2 select_convert_fusion
  21.4 2.2 fusion.31
  23.6 1.9 fusion.12
  25.5 1.8 fusion.32
  27.3 2.2 fusion.4
  29.4 111.3 %all-gather.5.cloned.1.call-done = f32[256,128,128]{2,1,0:T(8,128)} async-done(((f32[16,128,128]{2,1,0:T(8,128)}), f32[256,128,128]{2,1,0:T(8,128)}) %all-gather.5.cloned.1.call-update) | async-done | bytes 16777232 | tf_op jit(solution)/shard_map/all_gather | solution.py:12
  140.8 26.0 %while.30 = (s32[]{:T(128)}, f32[16,128,128]{2,1,0:T(8,128)S(1)}, s32[]{:T(128)}, f32[16,16,128,128]{3,2,1,0:T(8,128)}, s32[]{:T(128)}, /*index=5*/s32[]{:T(128)}) while((s32[]{:T(128)}, f32[16,128,128]{2,1,0:T(8,128)S(1)}, s32[]{:T(128)}, f32[16,16,128,128]{3,2,1,0:T(8,128)}, s32[]{:T(128)}, /*index=5*/s32[]{:T(128)}) %tuple.85), condition=%wide.region_1.2_spmd.clone, body=%wide.region_0.1_spmd.clone.sunk | while | flops 786436 | bytes 3145821 | solution.py:21
  142.4 1.6 add_select_fusion.4
  144.0 1.6 add_select_fusion.4
  145.6 1.6 add_select_fusion.4
  147.2 1.6 add_select_fusion.4
  148.8 1.7 add_select_fusion.4
  150.6 1.6 add_select_fusion.4
  152.2 1.6 add_select_fusion.4
  157.1 1.6 add_select_fusion.4
  158.7 1.6 add_select_fusion.4
  160.3 1.6 add_select_fusion.4
  161.9 1.6 add_select_fusion.4
  163.6 1.6 add_select_fusion.4
  165.2 1.6 add_select_fusion.4
  166.8 3.3 %fusion.1 = bf16[256,16,128]{0,2,1:T(8,128)(2,1)} fusion(f32[16,256,128]{1,2,0:T(8,128)} %fusion.31, bf16[256,16,128]{0,2,1:T(8,128)(2,1)} %copy-done.1, f32[16,128,128]{2,1,0:T(8,128)S(1)} %get-tuple-element.193), kind=kOutput, calls=%fused_computation.7 | convolution fusion | flops 135528448 | bytes 5242880 | tf_op jit(solution)/shard_map/the,hde->thd/dot_general | solution.py:57
  170.1 2.3 copy.49
  172.4 96.2 %all-gather.7.cloned.1.call-done = f32[256,128,128]{2,1,0:T(8,128)} async-done(((f32[16,128,128]{2,1,0:T(8,128)}), f32[256,128,128]{2,1,0:T(8,128)}) %all-gather.7.cloned.1.call-update) | async-done | bytes 16777232 | tf_op jit(solution)/shard_map/all_gather | solution.py:12
  268.6 25.9 %while.31 = (s32[]{:T(128)}, f32[16,128,128]{2,1,0:T(8,128)S(1)}, s32[]{:T(128)}, f32[16,16,128,128]{3,2,1,0:T(8,128)}, s32[]{:T(128)}, /*index=5*/s32[]{:T(128)}, s32[]{:T(128)}, s32[]{:T(128)}) while((s32[]{:T(128)}, f32[16,128,128]{2,1,0:T(8,128)S(1)}, s32[]{:T(128)}, f32[16,16,128,128]{3,2,1,0:T(8,128)}, s32[]{:T(128)}, ...), condition=%wide.region_3.4_spmd.clone, body=%wide.region_2.3_spmd.clone.sunk | while | flops 786440 | bytes 3145883 | solution.py:21
  294.5 3.0 fusion
  297.5 2.3 copy.50
  299.8 3.4 %add_convert_fusion = bf16[16,128,256]{2,1,0:T(8,128)(2,1)} fusion(f32[16,128,256]{2,1,0:T(8,128)} %fusion.32, f32[16,128,128]{2,1,0:T(8,128)S(1)} %get-tuple-element.194, bf16[256,2048]{1,0:T(8,128)(2,1)} %param.9), kind=kOutput, calls=%fused_computation.11 | convolution fusion | flops 135528448 | bytes 5242880 | tf_op jit(solution)/shard_map/shd,hde->she/dot_general | solution.py:63
  303.2 2.4 copy.51
  305.5 3.1 fusion.3
  308.6 2.3 copy.48
  (53 shorter events, 38.6 us)
Async XLA Ops:
  7.2 2.4 copy-start
  7.2 133.6 %all-gather.5.cloned.1.call-start = ((), (), s32[]{:S(2)}) async-start(), calls=%async_computation | async-start | bytes 17825792 | tf_op jit(solution)/shard_map/all_gather | solution.py:12
  9.6 1.4 copy-start.3
  9.6 2.0 copy-start.9
  11.0 257.6 %all-gather.7.cloned.1.call-start = ((), (), s32[]{:S(2)}) async-start(), calls=%async_computation.1 | async-start | bytes 17825792 | tf_op jit(solution)/shard_map/all_gather | solution.py:12
  13.2 2.9 copy-start.5
  15.1 1.0 copy-start.1
  17.9 2.2 copy-start.6
  17.9 2.2 copy-start.8
  20.1 1.3 copy-start.4
  23.6 1.9 copy-start.2
  303.1 2.4 copy-start.7
Sparse Core Ops, SparseCore 0:
  11.1 129.5 all-gather.4
  143.5 125.0 all-gather.6
where the time goes:
time: 319 us; the launch traced here: 318 us
  waiting for transfers between devices  208 us (65%)
  other arithmetic  53 us (17%)
  matrix products  25.5 us (8%)
  local copies, waits for them, and re-layouts  16.5 us (5%)
  between operations  14.2 us (4%)
    all_gather x2, waiting for transfers between devices, carried_in(): everything = lax.all_gather(array, axis)  208 us
    select_n x32, other arithmetic, lap(): return jnp.where(reached, new, before)  51.1 us
    unnamed x25, local copies, waits for them, and re-layouts  12.8 us
  transfers between devices with their start and end apart: 2, of which 2 were waited for; matrix products, arithmetic and copies ran while one was open for 15% of the time, Pallas kernels for 0%

commit v1 on v0

v1 whole, which is shorter than its diff:
```python
import functools

import jax
import jax.numpy as jnp
from jax import lax
from jax.experimental import pallas as pl
from jax.experimental.pallas import tpu as pltpu
from jax.sharding import PartitionSpec as P

DH = 128
F32 = jnp.float32
BF16 = jnp.bfloat16

CORE, ROW, EVEN, EARLY_KV, START = range(5)


def rows_scale(start, count):
    where = start + lax.broadcasted_iota(jnp.int32, (count, DH), 0)
    return 1.0 / jnp.sqrt(DH * (where.astype(F32) + 1.0))


def dot(a, b, ca, cb):
    return lax.dot_general(a, b, (((ca,), (cb,)), ((), ())), preferred_element_type=F32)


def states_kernel(info, *refs):
    ins, outs = refs[:8], refs[8:12]
    count = ins[0].shape[0]
    scale = rows_scale(info[START], count)
    even = info[EVEN] == 1
    for side in range(2):
        q, k, v, d = ins[4 * side : 4 * side + 4]
        first, second = outs[2 * side : 2 * side + 2]
        for i in range(first.shape[0]):
            cols = slice(i * DH, (i + 1) * DH)
            scaled = (d[:, cols].astype(F32) * scale).astype(BF16)
            kv = dot(k[:, cols], v[:, cols], 0, 0)
            qg = dot(q[:, cols], scaled, 0, 0)
            first[i] = jnp.where(even, kv, qg)
            second[i] = jnp.where(even, qg, kv)


def local_states(info, query, key_in, value, d_out):
    count, width = query.shape
    heads = width // DH
    half, two = heads // 2, 2
    steps = half // two

    def at(side):
        def index(g, info):
            core = info[CORE] if side == 0 else 1 - info[CORE]
            part = g // (steps // 2)
            row = jnp.where(part == 0, info[ROW], 1 - info[ROW])
            return 0, core * steps + row * (steps // 2) + g % (steps // 2)

        return pl.BlockSpec((count, two * DH), index)

    out = pl.BlockSpec((two, DH, DH), lambda g, info: (g, 0, 0))
    args = (query, key_in, value, d_out)
    return pl.pallas_call(
        states_kernel,
        out_shape=[jax.ShapeDtypeStruct((half, DH, DH), F32)] * 4,
        grid_spec=pltpu.PrefetchScalarGridSpec(
            num_scalar_prefetch=1,
            grid=(steps,),
            in_specs=[at(0)] * 4 + [at(1)] * 4,
            out_specs=[out] * 4,
        ),
        compiler_params=pltpu.CompilerParams(vmem_limit_bytes=16 * 2**20),
        name="states",
    )(info, *args, *args)


def final_kernel(info, q, k, v, d, *refs):
    early, late = refs[0:4], refs[4:8]
    o_ref, dq_ref, dk_ref, dv_ref = refs[8:12]
    kv_state, grad_state = refs[12:14]
    g = pl.program_id(0)
    count = q.shape[0]
    steps = pl.num_programs(0)
    early_kv = info[EARLY_KV] == 1
    for kind in range(4):

        @pl.when(g // (steps // 4) == kind)
        def _():
            t, u = early[kind][...], late[kind][...]
            kv_state[...] = jnp.where(early_kv, t, u).astype(BF16)
            grad_state[...] = jnp.where(early_kv, u, t).astype(BF16)

    scale = rows_scale(info[START], count)
    lower = lax.broadcasted_iota(jnp.int32, (count, count), 1) <= lax.broadcasted_iota(
        jnp.int32, (count, count), 0
    )
    for i in range(kv_state.shape[0]):
        cols = slice(i * DH, (i + 1) * DH)
        qh, kh, vh = q[:, cols], k[:, cols], v[:, cols]
        ph = (d[:, cols].astype(F32) * scale).astype(BF16)
        kv, gr = kv_state[i], grad_state[i]
        scores = jnp.where(lower, dot(qh, kh, 1, 1), 0.0).astype(BF16)
        back = jnp.where(lower, dot(ph, vh, 1, 1), 0.0).astype(BF16)
        o_ref[:, cols] = ((dot(scores, vh, 1, 0) + dot(qh, kv, 1, 0)) * scale).astype(BF16)
        dq_ref[:, cols] = (dot(back, kh, 1, 0) + dot(ph, kv, 1, 1)).astype(BF16)
        dk_ref[:, cols] = (dot(back, qh, 0, 0) + dot(vh, gr, 1, 1)).astype(BF16)
        dv_ref[:, cols] = (dot(scores, ph, 0, 0) + dot(kh, gr, 1, 0)).astype(BF16)


def finish(info, query, key_in, value, d_out, early, late):
    count, width = query.shape
    heads = width // DH
    two = 2
    steps = heads // two
    quarter = steps // 4

    def cols(g, info):
        kind = g // quarter
        core = jnp.where(kind < 2, info[CORE], 1 - info[CORE])
        row = jnp.where(kind % 2 == 0, info[ROW], 1 - info[ROW])
        return 0, (core * 2 + row) * quarter + g % quarter

    def state(kind):
        def index(g, info):
            return jnp.clip(g - kind * quarter, 0, quarter - 1), 0, 0

        return pl.BlockSpec((two, DH, DH), index)

    block = pl.BlockSpec((count, two * DH), cols)
    return pl.pallas_call(
        final_kernel,
        out_shape=[jax.ShapeDtypeStruct((count, width), BF16)] * 4,
        grid_spec=pltpu.PrefetchScalarGridSpec(
            num_scalar_prefetch=1,
            grid=(steps,),
            in_specs=[block] * 4 + [state(n) for n in range(4)] * 2,
            out_specs=[block] * 4,
            scratch_shapes=[pltpu.VMEM((two, DH, DH), BF16)] * 2,
        ),
        compiler_params=pltpu.CompilerParams(vmem_limit_bytes=24 * 2**20),
        name="finish",
    )(info, query, key_in, value, d_out, *early, *late)


def send(array, pairs):
    return lax.ppermute(array, "seq", pairs)


def plane_scan(planes, plane, first, second_of):
    def spread(pairs):
        return [(4 * a + i, 4 * b + i) for a, b in pairs for i in range(4)]

    if planes == 4:
        near = send(first, spread([(0, 1), (1, 0), (2, 3), (3, 2)]))
        inner = (plane == 1) | (plane == 2)
        early = jnp.where(inner, near, 0.0)
        middle = send(second_of() + near, spread([(1, 2), (2, 1)]))
        outer = send(middle, spread([(1, 0), (2, 3)]))
        late = middle + outer + jnp.where(inner, 0.0, near)
        return early, late
    even = plane % 2 == 0
    second = second_of()
    kv = jnp.where(even, first, second)
    qg = jnp.where(even, second, first)

    def scan(x, sign):
        def shift(x, by):
            return send(
                x, spread([(a, a + sign * by) for a in range(planes) if 0 <= a + sign * by < planes])
            )

        x, by = shift(x, 1), 1
        while by < planes:
            x, by = x + shift(x, by), 2 * by
        return x

    before, after = scan(kv, 1), scan(qg, -1)
    lower = plane < planes // 2
    return jnp.where(lower, before, after), jnp.where(lower, after, before)


def body(query, key_in, value, d_out):
    count, width = query.shape
    quarter = width // DH // 4
    size, place = lax.axis_size("seq"), lax.axis_index("seq")
    planes = size // 4
    core, row, plane = place % 2, (place // 2) % 2, place // 4
    even = plane % 2 == 0
    early_kv = plane < planes // 2
    info = jnp.stack(
        [core, row, even.astype(jnp.int32), early_kv.astype(jnp.int32), place * count]
    ).astype(jnp.int32)
    core_swap = [(i, i ^ 1) for i in range(size)]
    row_swap = [(i, i ^ 2) for i in range(size)]

    f_own, s_own, f_sib, s_sib = local_states(info, query, key_in, value, d_out)

    def chip_and_plane(own, sib):
        got = send(sib, core_swap)
        keep = own[:quarter] + got[:quarter]
        other = send(own[quarter:] + got[quarter:], row_swap)
        return got, keep, other

    f = chip_and_plane(f_own, f_sib)
    s = chip_and_plane(s_own, s_sib)
    t_val, u_val = plane_scan(planes, plane, f[1] + f[2], lambda: s[1] + s[2])

    first_is_early = even == early_kv

    def spread_out(val, is_first, is_kv):
        own = jnp.where(is_first, f_own, s_own)
        got, keep, other = (jnp.where(is_first, a, b) for a, b in zip(f, s))
        after_row = is_kv == (row == 1)
        d_keep = val + jnp.where(after_row, other, 0.0)
        d_other = send(val + jnp.where(after_row, 0.0, keep), row_swap)
        after_core = is_kv == (core == 1)
        own_states, sib_states = [], []
        for n, d in enumerate((d_keep, d_other)):
            part = slice(n * quarter, (n + 1) * quarter)
            own_states.append(d + jnp.where(after_core, got[part], 0.0))
            sib_states.append(send(d + jnp.where(after_core, 0.0, own[part]), core_swap))
        return own_states + sib_states

    early = spread_out(t_val, first_is_early, early_kv)
    late = spread_out(u_val, ~first_is_early, ~early_kv)
    return tuple(finish(info, query, key_in, value, d_out, early, late))


def solution(mesh):
    spec = P(("group", "seq"), None)
    return jax.shard_map(
        body, mesh=mesh, in_specs=(spec,) * 4, out_specs=(spec,) * 4, check_vma=False
    )
```

time: 319 us -> 65.6 us (0.21)
  waiting for transfers between devices: 208 us -> 34.3 us
  other arithmetic: 53 us -> 0.81 us
  matrix products: 25.5 us -> 0 us
  between operations: 14.2 us -> 0.86 us
  Pallas kernels: 0 us -> 13.1 us
  local copies, waits for them, and re-layouts: 16.5 us -> 5 us
  starting transfers between devices: 0.08 us -> 11.2 us
    all_gather x2 -> x0, waiting for transfers between devices: 208 us -> none  [carried_in(): everything = lax.all_gather(array, axis)]
    select_n x32 -> x2, other arithmetic: 51.1 us -> 0.14 us  [the longest x1 0.07 us: spread_out(): own = jnp.where(is_first, f_own, s_own)]
    ppermute x0 -> x13, waiting for transfers between devices: none -> 34.3 us  [send(): return lax.ppermute(array, 'seq', pairs)]
    dot_general x12 -> x0, matrix products: 25.5 us -> none  [the longest x1 3.38 us: body(): jnp.einsum('shd,hde->she', kblk, grad_state, preferred_element_type=jnp.f...]
    pallas_call x0 -> x2, Pallas kernels: none -> 13.1 us  [the longest x1 9.9 us: finish(): pl.pallas_call(final_kernel, out_shape=[jax.ShapeDtypeStruct((count, widt...]
    ppermute x0 -> x13, starting transfers between devices: none -> 11.2 us  [send(): return lax.ppermute(array, 'seq', pairs)]
    unnamed x25 -> x16, local copies, waits for them, and re-layouts: 12.8 us -> 4.91 us
  transfers between devices with their start and end apart: 2 -> 13, of which waited for: 2 -> 8; matrix products, arithmetic and copies ran while one was open for 15% -> 1% of each run, Pallas kernels for 0% -> 0%
where the time goes in v1:
time: 65.6 us; the launch traced here: 65.3 us
  waiting for transfers between devices  34.3 us (52%)
  Pallas kernels  13.1 us (20%)
  starting transfers between devices  11.2 us (17%)
  local copies, waits for them, and re-layouts  5 us (8%)
  between operations  0.86 us (1%)
  other arithmetic  0.81 us (1%)
    ppermute x13, waiting for transfers between devices, send(): return lax.ppermute(array, 'seq', pairs)  34.3 us
    ppermute x13, starting transfers between devices, send(): return lax.ppermute(array, 'seq', pairs)  11.2 us
    pallas_call x1, Pallas kernels, finish(): pl.pallas_call(final_kernel, out_shape=[jax.ShapeDtypeStruct((count, widt...  9.9 us
    unnamed x16, local copies, waits for them, and re-layouts  4.91 us
    pallas_call x1, Pallas kernels, local_states(): pl.pallas_call(states_kernel, out_shape=[jax.ShapeDtypeStruct((half, DH,...  3.19 us
  transfers between devices with their start and end apart: 13, of which 8 were waited for; matrix products, arithmetic and copies ran while one was open for 1% of the time, Pallas kernels for 0%

profile of v1, /device:TPU:0, one launch (start us, length us, event | category | flops | bytes accessed | tf_op | source)
XLA Modules:
  0.0 65.3 jit_solution(6251325806925904408)
XLA Ops:
  0.7 0.1 stack.31.info
  0.8 1.2 %copy-done = bf16[256,2048]{1,0:T(8,128)(2,1)S(1)} copy-done((bf16[256,2048]{1,0:T(8,128)(2,1)S(1)}, bf16[256,2048]{1,0:T(8,128)(2,1)}, u32[]{:S(2)}) %copy-start) | copy-done | bytes 1048600
  2.0 1.2 %copy-done.2 = bf16[256,2048]{1,0:T(8,128)(2,1)S(1)} copy-done((bf16[256,2048]{1,0:T(8,128)(2,1)S(1)}, bf16[256,2048]{1,0:T(8,128)(2,1)}, u32[]{:S(2)}) %copy-start.2) | copy-done | bytes 1048600
  3.2 1.2 %copy-done.4 = bf16[256,2048]{1,0:T(8,128)(2,1)S(1)} copy-done((bf16[256,2048]{1,0:T(8,128)(2,1)S(1)}, bf16[256,2048]{1,0:T(8,128)(2,1)}, u32[]{:S(2)}) %copy-start.4) | copy-done | bytes 1048600
  4.5 1.2 %copy-done.6 = bf16[256,2048]{1,0:T(8,128)(2,1)S(1)} copy-done((bf16[256,2048]{1,0:T(8,128)(2,1)S(1)}, bf16[256,2048]{1,0:T(8,128)(2,1)}, u32[]{:S(2)}) %copy-start.6) | copy-done | bytes 1048600
  5.7 3.2 %states.1 = (f32[8,128,128]{2,1,0:T(8,128)S(1)}, f32[8,128,128]{2,1,0:T(8,128)S(1)}, f32[8,128,128]{2,1,0:T(8,128)S(1)}, f32[8,128,128]{2,1,0:T(8,128)S(1)}) custom-call(s32[5]{0:T(128)S(1)} %stack.31.info, bf16[256,2048]{1,0:T(8,128)(2,1)S(1)} %copy-done, bf16[256,2048]{1,0:T(8,128)(2,1)S(1)} %copy-done.2, bf16[256,2048]{1,0:T(8,128)(2,1)S(1)} %copy-done.4, ...), custom_call_target="tpu_custom_call" | custom-call | tf_op jit(solution)/shard_map/states/pallas_call | solution.py:60
  8.9 0.5 collective-permute-start
  9.4 0.1 collective-permute-start.3
  9.5 1.5 %collective-permute-done = f32[8,128,128]{2,1,0:T(8,128)S(1)} collective-permute-done((f32[8,128,128]{2,1,0:T(8,128)S(1)}, f32[8,128,128]{2,1,0:T(8,128)S(1)}, u32[]{:S(2)}, u32[]{:S(2)}) %collective-permute-start) | collective-permute-done | bytes 524320 | tf_op jit(solution)/shard_map/ppermute | solution.py:143
  11.0 3.0 %collective-permute-start.1 = (f32[4,128,128]{2,1,0:T(8,128)S(1)}, f32[4,128,128]{2,1,0:T(8,128)S(1)}, u32[]{:S(2)}, u32[]{:S(2)}) collective-permute-start(f32[4,128,128]{2,1,0:T(8,128)S(1)} %slice_add_fusion.2), channel_id=1, source_target_pairs={{0,2},{1,3},{2,0},{3,1},{4,6},{5,7},{6,4},{7,5},{8,10},{9,11},{10,... | collective-permute-start | bytes 786440 | tf_op jit(solution)/shard_map/ppermute | solution.py:143
  14.0 0.7 %collective-permute-start.4 = (f32[4,128,128]{2,1,0:T(8,128)S(1)}, f32[4,128,128]{2,1,0:T(8,128)S(1)}, u32[]{:S(2)}, u32[]{:S(2)}) collective-permute-start(f32[4,128,128]{2,1,0:T(8,128)S(1)} %slice_add_fusion.1), channel_id=1, source_target_pairs={{0,2},{1,3},{2,0},{3,1},{4,6},{5,7},{6,4},{7,5},{8,10},{9,11},{10,... | collective-permute-start | bytes 786440 | tf_op jit(solution)/shard_map/ppermute | solution.py:143
  14.7 6.3 %collective-permute-done.1 = f32[4,128,128]{2,1,0:T(8,128)S(1)} collective-permute-done((f32[4,128,128]{2,1,0:T(8,128)S(1)}, f32[4,128,128]{2,1,0:T(8,128)S(1)}, u32[]{:S(2)}, u32[]{:S(2)}) %collective-permute-start.1) | collective-permute-done | bytes 262176 | tf_op jit(solution)/shard_map/ppermute | solution.py:143
  21.1 2.2 %collective-permute-start.2 = (f32[4,128,128]{2,1,0:T(8,128)S(1)}, f32[4,128,128]{2,1,0:T(8,128)S(1)}, u32[]{:S(2)}, u32[]{:S(2)}) collective-permute-start(f32[4,128,128]{2,1,0:T(8,128)S(1)} %fusion.8), channel_id=1, source_target_pairs={{0,4},{1,5},{2,6},{3,7},{4,0},{5,1},{6,2},{7,3},{8,12},{9,13},{10,... | collective-permute-start | bytes 786440 | tf_op jit(solution)/shard_map/ppermute | solution.py:143
  23.3 2.9 %collective-permute-done.4 = f32[4,128,128]{2,1,0:T(8,128)S(1)} collective-permute-done((f32[4,128,128]{2,1,0:T(8,128)S(1)}, f32[4,128,128]{2,1,0:T(8,128)S(1)}, u32[]{:S(2)}, u32[]{:S(2)}) %collective-permute-start.4) | collective-permute-done | bytes 262176 | tf_op jit(solution)/shard_map/ppermute | solution.py:143
  26.2 2.3 %collective-permute-done.2 = f32[4,128,128]{2,1,0:T(8,128)S(1)} collective-permute-done((f32[4,128,128]{2,1,0:T(8,128)S(1)}, f32[4,128,128]{2,1,0:T(8,128)S(1)}, u32[]{:S(2)}, u32[]{:S(2)}) %collective-permute-start.2) | collective-permute-done | bytes 262176 | tf_op jit(solution)/shard_map/ppermute | solution.py:143
  28.5 0.1 add_add_fusion
  28.6 0.7 %collective-permute-start.8 = (f32[4,128,128]{2,1,0:T(8,128)S(1)}, f32[4,128,128]{2,1,0:T(8,128)S(1)}, u32[]{:S(2)}, u32[]{:S(2)}) collective-permute-start(f32[4,128,128]{2,1,0:T(8,128)S(1)} %add_add_fusion), channel_id=1, source_target_pairs={{4,8},{5,9},{6,10},{7,11},{8,4},{9,5},{10,6},{11,7},{20,24},{21,25... | collective-permute-start | bytes 786440 | tf_op jit(solution)/shard_map/ppermute | solution.py:143
  29.3 1.3 %collective-permute-start.9 = (f32[4,128,128]{2,1,0:T(8,128)S(1)}, f32[4,128,128]{2,1,0:T(8,128)S(1)}, u32[]{:S(2)}, u32[]{:S(2)}) collective-permute-start(f32[4,128,128]{2,1,0:T(8,128)S(1)} %collective-permute-done.8), channel_id=1, source_target_pairs={{4,0},{5,1},{6,2},{7,3},{8,12},{9,13},{10,14},{11,15},{20,16},{21,... | collective-permute-start | bytes 786440 | tf_op jit(solution)/shard_map/ppermute | solution.py:143
  30.6 0.1 broadcast_select_fusion
  30.7 13.2 %collective-permute-done.9 = f32[4,128,128]{2,1,0:T(8,128)S(1)} collective-permute-done((f32[4,128,128]{2,1,0:T(8,128)S(1)}, f32[4,128,128]{2,1,0:T(8,128)S(1)}, u32[]{:S(2)}, u32[]{:S(2)}) %collective-permute-start.9) | collective-permute-done | bytes 262176 | tf_op jit(solution)/shard_map/ppermute | solution.py:143
  43.9 0.1 fusion.1
  44.1 0.1 select_add_fusion
  44.2 1.6 %collective-permute-start.10 = (f32[4,128,128]{2,1,0:T(8,128)S(1)}, f32[4,128,128]{2,1,0:T(8,128)S(1)}, u32[]{:S(2)}, u32[]{:S(2)}) collective-permute-start(f32[4,128,128]{2,1,0:T(8,128)S(1)} %get-tuple-element.17), channel_id=1, source_target_pairs={{0,2},{1,3},{2,0},{3,1},{4,6},{5,7},{6,4},{7,5},{8,10},{9,11},{10,... | collective-permute-start | bytes 786440 | tf_op jit(solution)/shard_map/ppermute | solution.py:143
  45.9 0.6 collective-permute-start.5
  46.4 0.5 collective-permute-start.6
  46.9 3.9 %collective-permute-done.10 = f32[4,128,128]{2,1,0:T(8,128)S(1)} collective-permute-done((f32[4,128,128]{2,1,0:T(8,128)S(1)}, f32[4,128,128]{2,1,0:T(8,128)S(1)}, u32[]{:S(2)}, u32[]{:S(2)}) %collective-permute-start.10) | collective-permute-done | bytes 262176 | tf_op jit(solution)/shard_map/ppermute | solution.py:143
  50.8 0.1 fusion.2
  51.0 2.6 %collective-permute-done.5 = f32[4,128,128]{2,1,0:T(8,128)S(1)} collective-permute-done((f32[4,128,128]{2,1,0:T(8,128)S(1)}, f32[4,128,128]{2,1,0:T(8,128)S(1)}, u32[]{:S(2)}, u32[]{:S(2)}) %collective-permute-start.5) | collective-permute-done | bytes 262176 | tf_op jit(solution)/shard_map/ppermute | solution.py:143
  53.7 0.1 fusion.6
  53.7 0.1 collective-permute-start.7
  53.9 1.5 %collective-permute-done.7.refs_3_ = f32[4,128,128]{2,1,0:T(8,128)S(1)} collective-permute-done((f32[4,128,128]{2,1,0:T(8,128)S(1)}, f32[4,128,128]{2,1,0:T(8,128)S(1)}, u32[]{:S(2)}, u32[]{:S(2)}) %collective-permute-start.7) | collective-permute-done | bytes 262176 | tf_op jit(solution)/shard_map/ppermute | solution.py:143
  55.4 9.9 %finish.1 = (bf16[256,2048]{1,0:T(8,128)(2,1)}, bf16[256,2048]{1,0:T(8,128)(2,1)}, bf16[256,2048]{1,0:T(8,128)(2,1)}, bf16[256,2048]{1,0:T(8,128)(2,1)}) custom-call(s32[5]{0:T(128)S(1)} %stack.31.info, bf16[256,2048]{1,0:T(8,128)(2,1)S(1)} %copy-done.1, bf16[256,2048]{1,0:T(8,128)(2,1)S(1)} %copy-done.3, bf16[256,2048]{1,0:T(8,128)(2,1)S(1)} %copy-done.5, ...), custom_call_target="tpu_custom_call" | custom-call | tf_op jit(solution)/shard_map/finish/pallas_call | solution.py:127
  (23 shorter events, 0.3 us)
Async XLA Ops:
  0.8 1.2 %copy-start = (bf16[256,2048]{1,0:T(8,128)(2,1)S(1)}, bf16[256,2048]{1,0:T(8,128)(2,1)}, u32[]{:S(2)}) copy-start(bf16[256,2048]{1,0:T(8,128)(2,1)} %q.1) | copy-start | bytes 3145732
  2.0 1.2 %copy-start.2 = (bf16[256,2048]{1,0:T(8,128)(2,1)S(1)}, bf16[256,2048]{1,0:T(8,128)(2,1)}, u32[]{:S(2)}) copy-start(bf16[256,2048]{1,0:T(8,128)(2,1)} %k.1) | copy-start | bytes 3145732
  3.2 1.2 %copy-start.4 = (bf16[256,2048]{1,0:T(8,128)(2,1)S(1)}, bf16[256,2048]{1,0:T(8,128)(2,1)}, u32[]{:S(2)}) copy-start(bf16[256,2048]{1,0:T(8,128)(2,1)} %v.1) | copy-start | bytes 3145732
  4.5 1.2 %copy-start.6 = (bf16[256,2048]{1,0:T(8,128)(2,1)S(1)}, bf16[256,2048]{1,0:T(8,128)(2,1)}, u32[]{:S(2)}) copy-start(bf16[256,2048]{1,0:T(8,128)(2,1)} %d.1) | copy-start | bytes 3145732
  8.9 2.0 %collective-permute-start = (f32[8,128,128]{2,1,0:T(8,128)S(1)}, f32[8,128,128]{2,1,0:T(8,128)S(1)}, u32[]{:S(2)}, u32[]{:S(2)}) collective-permute-start(f32[8,128,128]{2,1,0:T(8,128)S(1)} %get-tuple-element.9), channel_id=1, source_target_pairs={{0,1},{1,0},{2,3},{3,2},{4,5},{5,4},{6,7},{7,6},{8,9},{9,8},{10,11... | collective-permute-start | bytes 1572872 | tf_op jit(solution)/shard_map/ppermute | solution.py:143
  9.4 4.5 %collective-permute-start.3 = (f32[8,128,128]{2,1,0:T(8,128)S(1)}, f32[8,128,128]{2,1,0:T(8,128)S(1)}, u32[]{:S(2)}, u32[]{:S(2)}) collective-permute-start(f32[8,128,128]{2,1,0:T(8,128)S(1)} %get-tuple-element.11), channel_id=1, source_target_pairs={{0,1},{1,0},{2,3},{3,2},{4,5},{5,4},{6,7},{7,6},{8,9},{9,8},{10,11... | collective-permute-start | bytes 1572872 | tf_op jit(solution)/shard_map/ppermute | solution.py:143
  11.0 10.0 %collective-permute-start.1 = (f32[4,128,128]{2,1,0:T(8,128)S(1)}, f32[4,128,128]{2,1,0:T(8,128)S(1)}, u32[]{:S(2)}, u32[]{:S(2)}) collective-permute-start(f32[4,128,128]{2,1,0:T(8,128)S(1)} %slice_add_fusion.2), channel_id=1, source_target_pairs={{0,2},{1,3},{2,0},{3,1},{4,6},{5,7},{6,4},{7,5},{8,10},{9,11},{10,... | collective-permute-start | bytes 786440 | tf_op jit(solution)/shard_map/ppermute | solution.py:143
  14.0 12.2 %collective-permute-start.4 = (f32[4,128,128]{2,1,0:T(8,128)S(1)}, f32[4,128,128]{2,1,0:T(8,128)S(1)}, u32[]{:S(2)}, u32[]{:S(2)}) collective-permute-start(f32[4,128,128]{2,1,0:T(8,128)S(1)} %slice_add_fusion.1), channel_id=1, source_target_pairs={{0,2},{1,3},{2,0},{3,1},{4,6},{5,7},{6,4},{7,5},{8,10},{9,11},{10,... | collective-permute-start | bytes 786440 | tf_op jit(solution)/shard_map/ppermute | solution.py:143
  21.1 7.4 %collective-permute-start.2 = (f32[4,128,128]{2,1,0:T(8,128)S(1)}, f32[4,128,128]{2,1,0:T(8,128)S(1)}, u32[]{:S(2)}, u32[]{:S(2)}) collective-permute-start(f32[4,128,128]{2,1,0:T(8,128)S(1)} %fusion.8), channel_id=1, source_target_pairs={{0,4},{1,5},{2,6},{3,7},{4,0},{5,1},{6,2},{7,3},{8,12},{9,13},{10,... | collective-permute-start | bytes 786440 | tf_op jit(solution)/shard_map/ppermute | solution.py:143
  28.6 0.7 %collective-permute-start.8 = (f32[4,128,128]{2,1,0:T(8,128)S(1)}, f32[4,128,128]{2,1,0:T(8,128)S(1)}, u32[]{:S(2)}, u32[]{:S(2)}) collective-permute-start(f32[4,128,128]{2,1,0:T(8,128)S(1)} %add_add_fusion), channel_id=1, source_target_pairs={{4,8},{5,9},{6,10},{7,11},{8,4},{9,5},{10,6},{11,7},{20,24},{21,25... | collective-permute-start | bytes 786440 | tf_op jit(solution)/shard_map/ppermute | solution.py:143
  29.3 14.6 %collective-permute-start.9 = (f32[4,128,128]{2,1,0:T(8,128)S(1)}, f32[4,128,128]{2,1,0:T(8,128)S(1)}, u32[]{:S(2)}, u32[]{:S(2)}) collective-permute-start(f32[4,128,128]{2,1,0:T(8,128)S(1)} %collective-permute-done.8), channel_id=1, source_target_pairs={{4,0},{5,1},{6,2},{7,3},{8,12},{9,13},{10,14},{11,15},{20,16},{21,... | collective-permute-start | bytes 786440 | tf_op jit(solution)/shard_map/ppermute | solution.py:143
  44.2 6.7 %collective-permute-start.10 = (f32[4,128,128]{2,1,0:T(8,128)S(1)}, f32[4,128,128]{2,1,0:T(8,128)S(1)}, u32[]{:S(2)}, u32[]{:S(2)}) collective-permute-start(f32[4,128,128]{2,1,0:T(8,128)S(1)} %get-tuple-element.17), channel_id=1, source_target_pairs={{0,2},{1,3},{2,0},{3,1},{4,6},{5,7},{6,4},{7,5},{8,10},{9,11},{10,... | collective-permute-start | bytes 786440 | tf_op jit(solution)/shard_map/ppermute | solution.py:143
  45.9 7.8 %collective-permute-start.5 = (f32[4,128,128]{2,1,0:T(8,128)S(1)}, f32[4,128,128]{2,1,0:T(8,128)S(1)}, u32[]{:S(2)}, u32[]{:S(2)}) collective-permute-start(f32[4,128,128]{2,1,0:T(8,128)S(1)} %get-tuple-element.18), channel_id=1, source_target_pairs={{0,2},{1,3},{2,0},{3,1},{4,6},{5,7},{6,4},{7,5},{8,10},{9,11},{10,... | collective-permute-start | bytes 786440 | tf_op jit(solution)/shard_map/ppermute | solution.py:143
  46.4 7.4 %collective-permute-start.11 = (f32[4,128,128]{2,1,0:T(8,128)S(1)}, f32[4,128,128]{2,1,0:T(8,128)S(1)}, u32[]{:S(2)}, u32[]{:S(2)}) collective-permute-start(f32[4,128,128]{2,1,0:T(8,128)S(1)} %get-tuple-element.12), channel_id=1, source_target_pairs={{0,1},{1,0},{2,3},{3,2},{4,5},{5,4},{6,7},{7,6},{8,9},{9,8},{10,11... | collective-permute-start | bytes 786440 | tf_op jit(solution)/shard_map/ppermute | solution.py:143
  46.4 7.4 %collective-permute-start.6 = (f32[4,128,128]{2,1,0:T(8,128)S(1)}, f32[4,128,128]{2,1,0:T(8,128)S(1)}, u32[]{:S(2)}, u32[]{:S(2)}) collective-permute-start(f32[4,128,128]{2,1,0:T(8,128)S(1)} %get-tuple-element.23), channel_id=1, source_target_pairs={{0,1},{1,0},{2,3},{3,2},{4,5},{5,4},{6,7},{7,6},{8,9},{9,8},{10,11... | collective-permute-start | bytes 786440 | tf_op jit(solution)/shard_map/ppermute | solution.py:143
  50.8 4.5 %copy-start.5 = (bf16[256,2048]{1,0:T(8,128)(2,1)S(1)}, bf16[256,2048]{1,0:T(8,128)(2,1)}, u32[]{:S(2)}) copy-start(bf16[256,2048]{1,0:T(8,128)(2,1)} %v.1) | copy-start | bytes 3145732
  50.8 4.5 %copy-start.7 = (bf16[256,2048]{1,0:T(8,128)(2,1)S(1)}, bf16[256,2048]{1,0:T(8,128)(2,1)}, u32[]{:S(2)}) copy-start(bf16[256,2048]{1,0:T(8,128)(2,1)} %d.1) | copy-start | bytes 3145732
  50.9 2.9 %collective-permute-start.12 = (f32[4,128,128]{2,1,0:T(8,128)S(1)}, f32[4,128,128]{2,1,0:T(8,128)S(1)}, u32[]{:S(2)}, u32[]{:S(2)}) collective-permute-start(f32[4,128,128]{2,1,0:T(8,128)S(1)} %get-tuple-element.29), channel_id=1, source_target_pairs={{0,1},{1,0},{2,3},{3,2},{4,5},{5,4},{6,7},{7,6},{8,9},{9,8},{10,11... | collective-permute-start | bytes 786440 | tf_op jit(solution)/shard_map/ppermute | solution.py:143
  53.6 1.7 %copy-start.1 = (bf16[256,2048]{1,0:T(8,128)(2,1)S(1)}, bf16[256,2048]{1,0:T(8,128)(2,1)}, u32[]{:S(2)}) copy-start(bf16[256,2048]{1,0:T(8,128)(2,1)} %q.1) | copy-start | bytes 3145732
  53.7 1.7 %copy-start.3 = (bf16[256,2048]{1,0:T(8,128)(2,1)S(1)}, bf16[256,2048]{1,0:T(8,128)(2,1)}, u32[]{:S(2)}) copy-start(bf16[256,2048]{1,0:T(8,128)(2,1)} %k.1) | copy-start | bytes 3145732
  53.7 1.6 %collective-permute-start.7 = (f32[4,128,128]{2,1,0:T(8,128)S(1)}, f32[4,128,128]{2,1,0:T(8,128)S(1)}, u32[]{:S(2)}, u32[]{:S(2)}) collective-permute-start(f32[4,128,128]{2,1,0:T(8,128)S(1)} %get-tuple-element.30), channel_id=1, source_target_pairs={{0,1},{1,0},{2,3},{3,2},{4,5},{5,4},{6,7},{7,6},{8,9},{9,8},{10,11... | collective-permute-start | bytes 786440 | tf_op jit(solution)/shard_map/ppermute | solution.py:143

commit v2 on v0

v2 whole, which is shorter than its diff:
```python
import functools

import jax
import jax.numpy as jnp
from jax import lax
from jax.experimental import pallas as pl
from jax.experimental.pallas import tpu as pltpu
from jax.sharding import PartitionSpec as P

DH = 128
F32 = jnp.float32
BF16 = jnp.bfloat16
MIB = 2**20
SMALL = pl.CostEstimate(flops=1, bytes_accessed=1, transcendentals=0)

CORE, ROW, EVEN, EARLY_KV, START, INNER = range(6)

IN_SMEM = pl.BlockSpec(memory_space=pltpu.SMEM)
IN_VMEM = pl.BlockSpec(memory_space=pltpu.VMEM)
IN_HBM = pl.BlockSpec(memory_space=pltpu.HBM)


def rows_scale(start, count):
    where = start + lax.broadcasted_iota(jnp.int32, (count, DH), 0)
    return 1.0 / jnp.sqrt(DH * (where.astype(F32) + 1.0))


def dot(a, b, ca, cb):
    return lax.dot_general(a, b, (((ca,), (cb,)), ((), ())), preferred_element_type=F32)


def first_head(info, side, part, quarter):
    core = info[CORE] if side == 0 else 1 - info[CORE]
    row = info[ROW] if part == 0 else 1 - info[ROW]
    return (core * 2 + row) * quarter


def half_cols(info, side, width):
    core = info[CORE] if side == 0 else 1 - info[CORE]
    half = width // 2
    return pl.multiple_of(core * half, half)


def state_products(is_kv, side, quarter, info, q, k, v, d, out):
    count = q.shape[0]

    @pl.when(is_kv)
    def _():
        for part in range(2):
            head = first_head(info, side, part, quarter)
            for i in range(quarter):
                cols = pl.ds(pl.multiple_of((head + i) * DH, DH), DH)
                out[part * quarter + i] = dot(k[:, cols], v[:, cols], 0, 0)

    @pl.when(jnp.logical_not(is_kv))
    def _():
        scale = rows_scale(info[START], count)
        for part in range(2):
            head = first_head(info, side, part, quarter)
            for i in range(quarter):
                cols = pl.ds(pl.multiple_of((head + i) * DH, DH), DH)
                scaled = (d[:, cols].astype(F32) * scale).astype(BF16)
                out[part * quarter + i] = dot(q[:, cols], scaled, 0, 0)


def pair_copies(info, side, width, rows, sems, *pair):
    half = width // 2
    for n, (there, here) in enumerate(pair):
        for step in range(there.shape[0] // rows):
            at = pl.ds(step * rows, rows), pl.ds(half_cols(info, side, width), half)
            yield pltpu.make_async_copy(there.at[at], here.at[at], sems.at[n, step])


def first_kernel(quarter, rows, info, q, k, v, d, out, left, right, sems):
    width = q.shape[1]
    is_kv = info[EVEN] == 1

    def copies(side, a, b):
        return pair_copies(info, side, width, rows, sems.at[side], (a, left), (b, right))

    @pl.when(is_kv)
    def _():
        for side in (1, 0):
            for copy in copies(side, k, v):
                copy.start()

    @pl.when(jnp.logical_not(is_kv))
    def _():
        for side in (1, 0):
            for copy in copies(side, q, d):
                copy.start()

    for copy in copies(1, k, v):
        copy.wait()
    state_products(is_kv, 1, quarter, info, left, left, right, right, out)
    for copy in copies(0, k, v):
        copy.wait()


def first_state(info, args):
    count, width = args[0].shape
    heads = width // DH
    rows = count // 4
    return pl.pallas_call(
        functools.partial(first_kernel, heads // 4, rows),
        out_shape=[jax.ShapeDtypeStruct((heads // 2, DH, DH), F32)]
        + [jax.ShapeDtypeStruct((count, width), BF16)] * 2,
        in_specs=[IN_SMEM] + [IN_HBM] * 4,
        out_specs=[IN_VMEM] * 3,
        scratch_shapes=[pltpu.SemaphoreType.DMA((2, 2, count // rows))],
        compiler_params=pltpu.CompilerParams(vmem_limit_bytes=4 * MIB),
        cost_estimate=SMALL,
        name="first",
    )(info, *args)


def own_kernel(quarter, info, left, right, out):
    state_products(info[EVEN] == 1, 0, quarter, info, left, left, right, right, out)


def own_state(info, left, right):
    width = left.shape[1]
    heads = width // DH
    return pl.pallas_call(
        functools.partial(own_kernel, heads // 4),
        out_shape=jax.ShapeDtypeStruct((heads // 2, DH, DH), F32),
        in_specs=[IN_SMEM] + [IN_VMEM] * 2,
        out_specs=IN_VMEM,
        compiler_params=pltpu.CompilerParams(vmem_limit_bytes=4 * MIB),
        cost_estimate=SMALL,
        name="own",
    )(info, left, right)


def second_kernel(quarter, rows, n_after, info, q, k, v, d, *refs):
    sib, own, qv, kv, vv, dv, sems = refs[n_after:]
    width = q.shape[1]
    is_kv = info[EVEN] != 1

    def copies(n, side, *pair):
        return pair_copies(info, side, width, rows, sems.at[n], *pair)

    keys, queries = ((k, kv), (v, vv)), ((q, qv), (d, dv))

    def start(*pairs):
        for n, pair in enumerate(pairs):
            for copy in copies(n, 1 - n % 2, *pair):
                copy.start()

    @pl.when(is_kv)
    def _():
        start(keys, keys, queries, queries)

    @pl.when(jnp.logical_not(is_kv))
    def _():
        start(queries, queries, keys, keys)

    for n, out in ((0, sib), (1, own)):
        for copy in copies(n, 1 - n, *keys):
            copy.wait()
        state_products(is_kv, 1 - n, quarter, info, qv, kv, vv, dv, out)
    for n in (2, 3):
        for copy in copies(n, 1 - n % 2, *keys):
            copy.wait()


def second_states(info, args, after):
    count, width = args[0].shape
    heads = width // DH
    rows = count // 4
    return pl.pallas_call(
        functools.partial(second_kernel, heads // 4, rows, len(after)),
        out_shape=[jax.ShapeDtypeStruct((heads // 2, DH, DH), F32)] * 2
        + [jax.ShapeDtypeStruct((count, width), BF16)] * 4,
        in_specs=[IN_SMEM] + [IN_HBM] * 4 + [IN_VMEM] * len(after),
        out_specs=[IN_VMEM] * 6,
        scratch_shapes=[pltpu.SemaphoreType.DMA((4, 2, count // rows))],
        compiler_params=pltpu.CompilerParams(vmem_limit_bytes=4 * MIB),
        cost_estimate=SMALL,
        name="second",
    )(info, *args, *after)


def local_kernel(side, quarter, n_after, info, q, k, v, d, *refs):
    o_ref, dq_ref, dk_ref, dv_ref, zero = refs[n_after:]
    zero[...] = jnp.zeros_like(zero)
    count = q.shape[0]
    two = 2
    scale = rows_scale(info[START], count)
    lower = lax.broadcasted_iota(jnp.int32, (count, count), 1) <= lax.broadcasted_iota(
        jnp.int32, (count, count), 0
    )

    for part in range(2):
        first = first_head(info, side, part, quarter)

        def step(g, carry):
            for i in range(two):
                to = pl.ds(pl.multiple_of((part * quarter + g * two + i) * DH, DH), DH)
                cols = pl.ds(pl.multiple_of((first + g * two + i) * DH, DH), DH)
                qh, kh, vh = q[:, cols], k[:, cols], v[:, cols]
                ph = (d[:, cols].astype(F32) * scale).astype(BF16)
                scores = jnp.where(lower, dot(qh, kh, 1, 1), 0.0).astype(BF16)
                back = jnp.where(lower, dot(ph, vh, 1, 1), 0.0).astype(BF16)
                o_ref[:, to] = dot(scores, vh, 1, 0)
                dq_ref[:, to] = dot(back, kh, 1, 0)
                dk_ref[:, to] = dot(back, qh, 0, 0)
                dv_ref[:, to] = dot(scores, ph, 0, 0)
            return carry

        lax.fori_loop(0, quarter // two, step, 0)


def local_part(info, args, side, after=()):
    count, width = args[0].shape
    quarter = width // DH // 4
    *partials, zero = pl.pallas_call(
        functools.partial(local_kernel, side, quarter, len(after)),
        out_shape=[jax.ShapeDtypeStruct((count, width // 2), F32)] * 4
        + [jax.ShapeDtypeStruct((quarter, DH, DH), F32)],
        in_specs=[IN_SMEM] + [IN_VMEM] * (4 + len(after)),
        out_specs=[IN_VMEM] * 5,
        compiler_params=pltpu.CompilerParams(vmem_limit_bytes=8 * MIB),
        cost_estimate=SMALL,
        name="local",
    )(info, *args, *after)
    return partials, zero


def apply_kernel(early, kinds, sides, quarter, n_filled, n_after, info, *refs):
    q, k, v, d = refs[:4]
    refs = refs[4:]
    partials = {side: refs[4 * n : 4 * n + 4] for n, side in enumerate(sides)}
    refs = refs[4 * len(sides) :]
    state_refs, refs = refs[: len(kinds)], refs[len(kinds) + n_filled + n_after :]
    o_hbm, dq_hbm, dk_hbm, dv_hbm, zero, one, other, sems = refs
    zero[...] = jnp.zeros_like(zero)
    count = q.shape[0]
    two = 2
    is_kv = (info[EARLY_KV] == 1) if early else (info[EARLY_KV] != 1)
    steps = [(n, j) for n in range(len(kinds)) for j in range(quarter // two)]
    starts = [first_head(info, side, part, quarter) * DH for side, part in kinds]

    def columns(n, head):
        return pl.multiple_of(starts[n] + head * DH, DH)

    def copies(step, a, b):
        n, j = steps[step]
        here = pl.ds(step * two * DH, two * DH)
        there = pl.ds(pl.multiple_of(starts[n] + j * two * DH, two * DH), two * DH)
        return (
            pltpu.make_async_copy(one.at[:, here], a.at[:, there], sems.at[step, 0]),
            pltpu.make_async_copy(other.at[:, here], b.at[:, there], sems.at[step, 1]),
        )

    def each_head(products, a, b):
        for step, (n, j) in enumerate(steps):
            side, part = kinds[n]
            for i in range(two):
                head = j * two + i
                cols = pl.ds(columns(n, head), DH)
                at = (part * quarter + head) * DH
                here = slice((step * two + i) * DH, (step * two + i + 1) * DH)
                one[:, here], other[:, here] = products(
                    cols, partials[side], slice(at, at + DH), state_refs[n][head].astype(BF16)
                )
            for copy in copies(step, a, b):
                copy.start()

    @pl.when(is_kv)
    def _():
        scale = rows_scale(info[START], count)

        def products(cols, partial, at, kv):
            o_part, dq_part = partial[0][:, at], partial[1][:, at]
            ph = (d[:, cols].astype(F32) * scale).astype(BF16)
            return (
                ((o_part + dot(q[:, cols], kv, 1, 0)) * scale).astype(BF16),
                (dq_part + dot(ph, kv, 1, 1)).astype(BF16),
            )

        each_head(products, o_hbm, dq_hbm)

    @pl.when(jnp.logical_not(is_kv))
    def _():
        def products(cols, partial, at, gr):
            dk_part, dv_part = partial[2][:, at], partial[3][:, at]
            return (
                (dk_part + dot(v[:, cols], gr, 1, 1)).astype(BF16),
                (dv_part + dot(k[:, cols], gr, 1, 0)).astype(BF16),
            )

        each_head(products, dk_hbm, dv_hbm)

    for step in range(len(steps)):
        for copy in copies(step, o_hbm, dq_hbm):
            copy.wait()


def apply_states(info, args, partials, early, kinds, arrays, outs, after=()):
    count, width = args[0].shape
    quarter = width // DH // 4
    filled = () if outs is None else tuple(outs)
    sides = sorted({side for side, _ in kinds})
    partials = [x for side in sides for x in partials[side]]
    first_out = 5 + len(partials) + len(kinds)
    columns = len(kinds) * quarter * DH
    return pl.pallas_call(
        functools.partial(
            apply_kernel, early, kinds, sides, quarter, len(filled), len(after)
        ),
        out_shape=[jax.ShapeDtypeStruct((count, width), BF16)] * 4
        + [jax.ShapeDtypeStruct((quarter, DH, DH), F32)],
        in_specs=[IN_SMEM]
        + [IN_VMEM] * (4 + len(partials) + len(kinds))
        + [IN_HBM] * len(filled)
        + [IN_VMEM] * len(after),
        out_specs=[IN_HBM] * 4 + [IN_VMEM],
        scratch_shapes=[
            pltpu.VMEM((count, columns), BF16),
            pltpu.VMEM((count, columns), BF16),
            pltpu.SemaphoreType.DMA((columns // (2 * DH), 2)),
        ],
        input_output_aliases={first_out + n: n for n in range(len(filled))},
        compiler_params=pltpu.CompilerParams(vmem_limit_bytes=8 * MIB),
        cost_estimate=SMALL,
        name="apply",
    )(info, *args, *partials, *arrays, *filled, *after)


def prepare_kernel(early, n_after, info, *refs):
    near, f_own, f_got, f_keep, f_other, s_own, s_got, s_keep, s_other = refs[:9]
    across, mine, theirs, rest_mine, rest_theirs = refs[9 + n_after :]
    quarter = near.shape[0]
    is_kv = (info[EARLY_KV] == 1) if early else (info[EARLY_KV] != 1)
    is_first = (info[EVEN] == 1) == is_kv
    takes_near = (info[INNER] == 1) if early else (info[INNER] != 1)
    after_row = is_kv == (info[ROW] == 1)
    after_core = is_kv == (info[CORE] == 1)
    for i in range(quarter):
        val = jnp.where(takes_near, near[i], 0.0)
        keep = jnp.where(is_first, f_keep[i], s_keep[i])
        other = jnp.where(is_first, f_other[i], s_other[i])
        own = jnp.where(is_first, f_own[i], s_own[i])
        got = jnp.where(is_first, f_got[i], s_got[i])
        across[i] = val + jnp.where(after_row, 0.0, keep)
        here = val + jnp.where(after_row, other, 0.0)
        mine[i] = here + jnp.where(after_core, got, 0.0)
        theirs[i] = here + jnp.where(after_core, 0.0, own)
        own = jnp.where(is_first, f_own[quarter + i], s_own[quarter + i])
        got = jnp.where(is_first, f_got[quarter + i], s_got[quarter + i])
        rest_mine[i] = jnp.where(after_core, got, 0.0)
        rest_theirs[i] = jnp.where(after_core, 0.0, own)


def prepare(info, early, near, f, s, after):
    return pl.pallas_call(
        functools.partial(prepare_kernel, early, len(after)),
        out_shape=[jax.ShapeDtypeStruct(near.shape, F32)] * 5,
        in_specs=[IN_SMEM] + [IN_VMEM] * (9 + len(after)),
        out_specs=[IN_VMEM] * 5,
        compiler_params=pltpu.CompilerParams(vmem_limit_bytes=4 * MIB),
        cost_estimate=SMALL,
        name="prepare",
    )(info, near, *f, *s, *after)


def send(array, pairs):
    return lax.ppermute(array, "seq", pairs)


def plane_scan(planes, kv, qg):
    def scan(x, sign):
        def shift(x, by):
            pairs = [(a, a + sign * by) for a in range(planes) if 0 <= a + sign * by < planes]
            return send(x, spread_pairs(pairs))

        x, by = shift(x, 1), 1
        while by < planes:
            x, by = x + shift(x, by), 2 * by
        return x

    return scan(kv, 1), scan(qg, -1)


def spread_pairs(pairs):
    return [(4 * a + i, 4 * b + i) for a, b in pairs for i in range(4)]


def body(query, key_in, value, d_out):
    args = (query, key_in, value, d_out)
    count, width = query.shape
    heads = width // DH
    size, place = lax.axis_size("seq"), lax.axis_index("seq")
    planes = size // 4
    core, row, plane = place % 2, (place // 2) % 2, place // 4
    even = plane % 2 == 0
    early_kv = plane < planes // 2
    inner = (plane == 1) | (plane == 2) | (planes != 4)
    info = jnp.stack([core, row, even, early_kv, place * count, inner]).astype(jnp.int32)
    core_swap = [(i, i ^ 1) for i in range(size)]
    row_swap = [(i, i ^ 2) for i in range(size)]
    far_args = tuple(pltpu.with_memory_space_constraint(x, pltpu.HBM) for x in args)

    quarter = heads // 4

    def halves(own, got):
        return own[:quarter] + got[:quarter], own[quarter:] + got[quarter:]

    f_sib, left, right = first_state(info, far_args)
    f_got = send(f_sib, core_swap)
    f_own = own_state(info, left, right)
    f_keep, f_give = halves(f_own, f_got)
    f_other = send(f_give, row_swap)
    s_sib, s_own, *args = second_states(info, far_args, (f_give,))
    s_sib, f_other = lax.optimization_barrier((s_sib, f_other))
    s_got = send(s_sib, core_swap)
    s_keep, s_give = halves(s_own, s_got)
    s_other = send(s_give, row_swap)
    f_total = f_keep + f_other
    f = f_own, f_got, f_keep, f_other
    s = s_own, s_got, s_keep, s_other
    half_a, zero = local_part(info, args, 0, (s_give,))
    half_b, zero = local_part(info, args, 1, (zero,))
    partials = half_a, half_b
    if planes == 4:
        near = send(f_total, spread_pairs([(0, 1), (1, 0), (2, 3), (3, 2)]))
        pair = s_keep + s_other + near + zero
        far = send(pair, spread_pairs([(1, 3), (2, 0)]))
        middle = send(pair, spread_pairs([(1, 2), (2, 1)]))
        coming = far + middle
    else:
        s_total = s_keep + s_other + zero
        kv, qg = plane_scan(
            planes, jnp.where(even, f_total, s_total), jnp.where(even, s_total, f_total)
        )
        near = pair = jnp.where(early_kv, kv, qg)
        coming = jnp.where(early_kv, qg, kv)
    across, mine, theirs, rest_mine, rest_theirs = prepare(info, True, near, f, s, ())

    finish = functools.partial(apply_states, info, args, partials)
    kept_heads, other_heads = ((0, 0), (1, 0)), ((0, 1), (1, 1))
    t_other = send(across, row_swap)
    t_kept = mine, send(theirs, core_swap)
    late = prepare(info, False, near, f, s, (across,))
    *outs, zero = finish(True, kept_heads, t_kept, None, (across, late[0]))
    t_rest = t_other + rest_mine + zero, send(t_other + rest_theirs, core_swap)

    across, mine, theirs = (coming + x for x in late[:3])
    u_other = send(across, row_swap)
    u_kept = mine, send(theirs, core_swap)
    *outs, _ = finish(True, other_heads, t_rest, outs, (across,))
    *outs, zero = finish(False, kept_heads, u_kept, outs)
    u_rest = u_other + late[3] + zero, send(u_other + late[4], core_swap)
    *outs, _ = finish(False, other_heads, u_rest, outs)
    return tuple(outs)


def solution(mesh):
    spec = P(("group", "seq"), None)
    return jax.shard_map(
        body, mesh=mesh, in_specs=(spec,) * 4, out_specs=(spec,) * 4, check_vma=False
    )
```

time: 319 us -> 57.5 us (0.18)
  the two profiles are of different devices: /device:TPU:0 before, /device:TPU:19 now
where the time goes in v2:
time: 57.5 us; the launch traced here: 57.4 us
  Pallas kernels  25.3 us (44%)
  starting transfers between devices  17.6 us (31%)
  waiting for transfers between devices  13 us (23%)
  between operations  0.86 us (1%)
    ppermute x13, starting transfers between devices, send(): return lax.ppermute(array, 'seq', pairs)  17.6 us
    ppermute x13, waiting for transfers between devices, send(): return lax.ppermute(array, 'seq', pairs)  13 us
    pallas_call x4, Pallas kernels, apply_states(): pl.pallas_call(functools.partial(apply_kernel, early, kinds, sides, quart...  8.92 us
    pallas_call x2, Pallas kernels, local_part(): pl.pallas_call(functools.partial(local_kernel, side, quarter, len(after))...  8.24 us
    pallas_call x1, Pallas kernels, second_states(): pl.pallas_call(functools.partial(second_kernel, heads // 4, rows, len(aft...  3.21 us
    pallas_call x1, Pallas kernels, first_state(): pl.pallas_call(functools.partial(first_kernel, heads // 4, rows), out_sha...  2.46 us
    pallas_call x2, Pallas kernels, prepare(): pl.pallas_call(functools.partial(prepare_kernel, early, len(after)), out_...  1.49 us
  transfers between devices with their start and end apart: 13, of which 6 were waited for; matrix products, arithmetic and copies ran while one was open for 0% of the time, Pallas kernels for 34%

profile of v2, /device:TPU:19, one launch (start us, length us, event | category | flops | bytes accessed | tf_op | source)
XLA Modules:
  0.0 57.4 jit_solution(15512557578944901672)
XLA Ops:
  0.7 0.1 stack.39.info
  0.8 2.5 %first.1 = (f32[8,128,128]{2,1,0:T(8,128)S(1)}, bf16[256,2048]{1,0:T(8,128)(2,1)S(1)}, bf16[256,2048]{1,0:T(8,128)(2,1)S(1)}) custom-call(s32[6]{0:T(128)S(1)} %stack.39.info, bf16[256,2048]{1,0:T(8,128)(2,1)} %q.3, bf16[256,2048]{1,0:T(8,128)(2,1)} %k.3, bf16[256,2048]{1,0:T(8,128)(2,1)} %v.3, bf16[256,2048]{1,0:T(8,128)(2,1)} %d.3), custom_call_target="tpu_custom_call" | custom-call | flops 1 | bytes 1 | tf_op jit(solution)/shard_map/first/pallas_call | solution.py:104
  3.2 0.7 %collective-permute-start = (f32[8,128,128]{2,1,0:T(8,128)S(1)}, f32[8,128,128]{2,1,0:T(8,128)S(1)}, u32[]{:S(2)}, u32[]{:S(2)}) collective-permute-start(f32[8,128,128]{2,1,0:T(8,128)S(1)} %get-tuple-element.55), channel_id=1, source_target_pairs={{0,1},{1,0},{2,3},{3,2},{4,5},{5,4},{6,7},{7,6},{8,9},{9,8},{10,11... | collective-permute-start | bytes 1572872 | tf_op jit(solution)/shard_map/ppermute | solution.py:369
  4.0 1.0 %own.1.refs_1_ = f32[8,128,128]{2,1,0:T(8,128)S(1)} custom-call(s32[6]{0:T(128)S(1)} %stack.39.info, bf16[256,2048]{1,0:T(8,128)(2,1)S(1)} %get-tuple-element.53.left, bf16[256,2048]{1,0:T(8,128)(2,1)S(1)} %get-tuple-element.54.right), custom_call_target="tpu_custom_call" | custom-call | flops 1 | bytes 1 | tf_op jit(solution)/shard_map/own/pallas_call | solution.py:124
  5.0 0.5 collective-permute-done.refs_2_
  5.6 1.3 %collective-permute-start.1 = (f32[4,128,128]{2,1,0:T(8,128)S(1)}, f32[4,128,128]{2,1,0:T(8,128)S(1)}, u32[]{:S(2)}, u32[]{:S(2)}) collective-permute-start(f32[4,128,128]{2,1,0:T(8,128)S(1)} %slice_add_fusion.3.refs_0_), channel_id=1, source_target_pairs={{0,2},{1,3},{2,0},{3,1},{4,6},{5,7},{6,4},{7,5},{8,10},{9,11},{10,... | collective-permute-start | bytes 786440 | tf_op jit(solution)/shard_map/ppermute | solution.py:369
  6.9 3.2 %second.1 = (f32[8,128,128]{2,1,0:T(8,128)S(1)}, f32[8,128,128]{2,1,0:T(8,128)S(1)}, bf16[256,2048]{1,0:T(8,128)(2,1)S(1)}, bf16[256,2048]{1,0:T(8,128)(2,1)S(1)...) custom-call(s32[6]{0:T(128)S(1)} %stack.39.info, bf16[256,2048]{1,0:T(8,128)(2,1)} %q.3, ...), custom_call_target="tpu_custom_call" | custom-call | flops 1 | bytes 1 | tf_op jit(solution)/shard_map/second/pallas_call | solution.py:171
  10.1 3.1 %collective-permute-done.1.refs_4_ = f32[4,128,128]{2,1,0:T(8,128)S(1)} collective-permute-done((f32[4,128,128]{2,1,0:T(8,128)S(1)}, f32[4,128,128]{2,1,0:T(8,128)S(1)}, u32[]{:S(2)}, u32[]{:S(2)}) %collective-permute-start.1) | collective-permute-done | bytes 262176 | tf_op jit(solution)/shard_map/ppermute | solution.py:369
  13.1 1.2 %collective-permute-start.2 = (f32[8,128,128]{2,1,0:T(8,128)S(1)}, f32[8,128,128]{2,1,0:T(8,128)S(1)}, u32[]{:S(2)}, u32[]{:S(2)}) collective-permute-start(f32[8,128,128]{2,1,0:T(8,128)S(1)} %get-tuple-element.62), channel_id=1, source_target_pairs={{0,1},{1,0},{2,3},{3,2},{4,5},{5,4},{6,7},{7,6},{8,9},{9,8},{10,11... | collective-permute-start | bytes 1572872 | tf_op jit(solution)/shard_map/ppermute | solution.py:369
  14.4 1.4 %collective-permute-start.4 = (f32[4,128,128]{2,1,0:T(8,128)S(1)}, f32[4,128,128]{2,1,0:T(8,128)S(1)}, u32[]{:S(2)}, u32[]{:S(2)}) collective-permute-start(f32[4,128,128]{2,1,0:T(8,128)S(1)} %get-tuple-element.104), channel_id=1, source_target_pairs={{0,4},{1,5},{2,6},{3,7},{4,0},{5,1},{6,2},{7,3},{8,12},{9,13},{10,... | collective-permute-start | bytes 786440 | tf_op jit(solution)/shard_map/ppermute | solution.py:369
  15.9 1.3 %collective-permute-start.3 = (f32[4,128,128]{2,1,0:T(8,128)S(1)}, f32[4,128,128]{2,1,0:T(8,128)S(1)}, u32[]{:S(2)}, u32[]{:S(2)}) collective-permute-start(f32[4,128,128]{2,1,0:T(8,128)S(1)} %slice_add_fusion.2.refs_0_), channel_id=1, source_target_pairs={{0,2},{1,3},{2,0},{3,1},{4,6},{5,7},{6,4},{7,5},{8,10},{9,11},{10,... | collective-permute-start | bytes 786440 | tf_op jit(solution)/shard_map/ppermute | solution.py:369
  17.2 4.1 %local.2 = (f32[256,1024]{1,0:T(8,128)S(1)}, f32[256,1024]{1,0:T(8,128)S(1)}, f32[256,1024]{1,0:T(8,128)S(1)}, f32[256,1024]{1,0:T(8,128)S(1)}, f32[4,128,128]{2,1,0:T(8,128)S(1)}) custom-call(s32[6]{0:T(128)S(1)} %stack.39.info, bf16[256,2048]{1,0:T(8,128)(2,1)S(1)} %get-tuple-element.56.q.refs_0_, bf16[256,2048]{1,0:T(8,128)(2,1)S(1)} %get-tuple-element.57.k.refs_1_, ...), custom_call_target="tpu_custom_call" | custom-call | flops 1 | bytes 1 | tf_op jit(solution)/shard_map/local/pallas_call | solution.py:217
  21.3 4.1 %local.3 = (f32[256,1024]{1,0:T(8,128)S(1)}, f32[256,1024]{1,0:T(8,128)S(1)}, f32[256,1024]{1,0:T(8,128)S(1)}, f32[256,1024]{1,0:T(8,128)S(1)}, f32[4,128,128]{2,1,0:T(8,128)S(1)}) custom-call(s32[6]{0:T(128)S(1)} %stack.39.info, bf16[256,2048]{1,0:T(8,128)(2,1)S(1)} %get-tuple-element.56.q.refs_0_, bf16[256,2048]{1,0:T(8,128)(2,1)S(1)} %get-tuple-element.57.k.refs_1_, ...), custom_call_target="tpu_custom_call" | custom-call | flops 1 | bytes 1 | tf_op jit(solution)/shard_map/local/pallas_call | solution.py:217
  25.5 0.1 add_add_fusion.2
  25.6 0.7 %prepare.2 = (f32[4,128,128]{2,1,0:T(8,128)S(1)}, f32[4,128,128]{2,1,0:T(8,128)S(1)}, f32[4,128,128]{2,1,0:T(8,128)S(1)}, f32[4,128,128]{2,1,0:T(8,128)S(1)}, f32[4,128,128]{2,1,0:T(8,128)S(1)}) custom-call(s32[6]{0:T(128)S(1)} %stack.39.info, f32[4,128,128]{2,1,0:T(8,128)S(1)} %collective-permute-done.4.refs_0_, f32[8,128,128]{2,1,0:T(8,128)S(1)} %own.1.refs_1_, ...), custom_call_target="tpu_custom_call" | custom-call | flops 1 | bytes 1 | tf_op jit(solution)/shard_map/prepare/pallas_call | solution.py:357
  26.4 0.7 %collective-permute-start.10 = (f32[4,128,128]{2,1,0:T(8,128)S(1)}, f32[4,128,128]{2,1,0:T(8,128)S(1)}, u32[]{:S(2)}, u32[]{:S(2)}) collective-permute-start(f32[4,128,128]{2,1,0:T(8,128)S(1)} %get-tuple-element.81), channel_id=1, source_target_pairs={{0,1},{1,0},{2,3},{3,2},{4,5},{5,4},{6,7},{7,6},{8,9},{9,8},{10,11... | collective-permute-start | bytes 786440 | tf_op jit(solution)/shard_map/ppermute | solution.py:369
  27.1 0.2 collective-permute-start.9
  27.3 2.0 %collective-permute-start.5 = (f32[4,128,128]{2,1,0:T(8,128)S(1)}, f32[4,128,128]{2,1,0:T(8,128)S(1)}, u32[]{:S(2)}, u32[]{:S(2)}) collective-permute-start(f32[4,128,128]{2,1,0:T(8,128)S(1)} %get-tuple-element.102), channel_id=1, source_target_pairs={{4,12},{5,13},{6,14},{7,15},{8,0},{9,1},{10,2},{11,3},{20,28},{21,... | collective-permute-start | bytes 786440 | tf_op jit(solution)/shard_map/ppermute | solution.py:369
  29.3 4.4 %collective-permute-start.6 = (f32[4,128,128]{2,1,0:T(8,128)S(1)}, f32[4,128,128]{2,1,0:T(8,128)S(1)}, u32[]{:S(2)}, u32[]{:S(2)}) collective-permute-start(f32[4,128,128]{2,1,0:T(8,128)S(1)} %get-tuple-element.102), channel_id=1, source_target_pairs={{4,8},{5,9},{6,10},{7,11},{8,4},{9,5},{10,6},{11,7},{20,24},{21,25... | collective-permute-start | bytes 786440 | tf_op jit(solution)/shard_map/ppermute | solution.py:369
  33.7 0.7 %prepare.3 = (f32[4,128,128]{2,1,0:T(8,128)S(1)}, f32[4,128,128]{2,1,0:T(8,128)S(1)}, f32[4,128,128]{2,1,0:T(8,128)S(1)}, f32[4,128,128]{2,1,0:T(8,128)S(1)}, f32[4,128,128]{2,1,0:T(8,128)S(1)}) custom-call(s32[6]{0:T(128)S(1)} %stack.39.info, f32[4,128,128]{2,1,0:T(8,128)S(1)} %collective-permute-done.4.refs_0_, f32[8,128,128]{2,1,0:T(8,128)S(1)} %own.1.refs_1_, ...), custom_call_target="tpu_custom_call" | custom-call | flops 1 | bytes 1 | tf_op jit(solution)/shard_map/prepare/pallas_call | solution.py:357
  34.4 1.8 %apply.4 = (bf16[256,2048]{1,0:T(8,128)(2,1)}, bf16[256,2048]{1,0:T(8,128)(2,1)}, bf16[256,2048]{1,0:T(8,128)(2,1)}, bf16[256,2048]{1,0:T(8,128)(2,1)}, f32[4,128,128]{2,1,0:T(8,128)S(1)}) custom-call(s32[6]{0:T(128)S(1)} %stack.39.info, bf16[256,2048]{1,0:T(8,128)(2,1)S(1)} %get-tuple-element.56.q.refs_0_, ...), custom_call_target="tpu_custom_call" | custom-call | flops 1 | bytes 1 | tf_op jit(solution)/shard_map/apply/pallas_call | solution.py:308
  36.3 1.0 %collective-permute-start.11 = (f32[4,128,128]{2,1,0:T(8,128)S(1)}, f32[4,128,128]{2,1,0:T(8,128)S(1)}, u32[]{:S(2)}, u32[]{:S(2)}) collective-permute-start(f32[4,128,128]{2,1,0:T(8,128)S(1)} %get-tuple-element.111), channel_id=1, source_target_pairs={{0,1},{1,0},{2,3},{3,2},{4,5},{5,4},{6,7},{7,6},{8,9},{9,8},{10,11... | collective-permute-start | bytes 786440 | tf_op jit(solution)/shard_map/ppermute | solution.py:369
  37.3 6.1 %collective-permute-done.6 = f32[4,128,128]{2,1,0:T(8,128)S(1)} collective-permute-done((f32[4,128,128]{2,1,0:T(8,128)S(1)}, f32[4,128,128]{2,1,0:T(8,128)S(1)}, u32[]{:S(2)}, u32[]{:S(2)}) %collective-permute-start.6) | collective-permute-done | bytes 262176 | tf_op jit(solution)/shard_map/ppermute | solution.py:369
  43.4 0.1 add_add_fusion.5
  43.5 1.2 %collective-permute-start.8 = (f32[4,128,128]{2,1,0:T(8,128)S(1)}, f32[4,128,128]{2,1,0:T(8,128)S(1)}, u32[]{:S(2)}, u32[]{:S(2)}) collective-permute-start(f32[4,128,128]{2,1,0:T(8,128)S(1)} %get-tuple-element.108), channel_id=1, source_target_pairs={{0,1},{1,0},{2,3},{3,2},{4,5},{5,4},{6,7},{7,6},{8,9},{9,8},{10,11... | collective-permute-start | bytes 786440 | tf_op jit(solution)/shard_map/ppermute | solution.py:369
  44.7 1.3 %collective-permute-start.7 = (f32[4,128,128]{2,1,0:T(8,128)S(1)}, f32[4,128,128]{2,1,0:T(8,128)S(1)}, u32[]{:S(2)}, u32[]{:S(2)}) collective-permute-start(f32[4,128,128]{2,1,0:T(8,128)S(1)} %get-tuple-element.106.refs_18_), channel_id=1, source_target_pairs={{0,2},{1,3},{2,0},{3,1},{4,6},{5,7},{6,4},{7,5},{8,10},{9,11},{10,... | collective-permute-start | bytes 786440 | tf_op jit(solution)/shard_map/ppermute | solution.py:369
  46.0 2.6 %apply.5 = (bf16[256,2048]{1,0:T(8,128)(2,1)}, bf16[256,2048]{1,0:T(8,128)(2,1)}, bf16[256,2048]{1,0:T(8,128)(2,1)}, bf16[256,2048]{1,0:T(8,128)(2,1)}, f32[4,128,128]{2,1,0:T(8,128)}) custom-call(s32[6]{0:T(128)S(1)} %stack.39.info, ...), custom_call_target="tpu_custom_call", output_to_operand_aliasing={{0}: (15, {}), {1}: (16, {}), {2}: (17, {}), {3}: (18, {})} | custom-call | flops 1 | bytes 1 | tf_op jit(solution)/shard_map/apply/pallas_call | solution.py:308
  48.6 1.9 %apply.6 = (bf16[256,2048]{1,0:T(8,128)(2,1)}, bf16[256,2048]{1,0:T(8,128)(2,1)}, bf16[256,2048]{1,0:T(8,128)(2,1)}, bf16[256,2048]{1,0:T(8,128)(2,1)}, f32[4,128,128]{2,1,0:T(8,128)S(1)}) custom-call(s32[6]{0:T(128)S(1)} %stack.39.info, ...), custom_call_target="tpu_custom_call", output_to_operand_aliasing={{0}: (15, {}), {1}: (16, {}), {2}: (17, {}), {3}: (18, {})} | custom-call | flops 1 | bytes 1 | tf_op jit(solution)/shard_map/apply/pallas_call | solution.py:308
  50.5 2.1 %collective-permute-done.7 = f32[4,128,128]{2,1,0:T(8,128)S(1)} collective-permute-done((f32[4,128,128]{2,1,0:T(8,128)S(1)}, f32[4,128,128]{2,1,0:T(8,128)S(1)}, u32[]{:S(2)}, u32[]{:S(2)}) %collective-permute-start.7) | collective-permute-done | bytes 262176 | tf_op jit(solution)/shard_map/ppermute | solution.py:369
  52.7 0.9 %collective-permute-start.12 = (f32[4,128,128]{2,1,0:T(8,128)S(1)}, f32[4,128,128]{2,1,0:T(8,128)S(1)}, u32[]{:S(2)}, u32[]{:S(2)}) collective-permute-start(f32[4,128,128]{2,1,0:T(8,128)S(1)} %get-tuple-element.109), channel_id=1, source_target_pairs={{0,1},{1,0},{2,3},{3,2},{4,5},{5,4},{6,7},{7,6},{8,9},{9,8},{10,11... | collective-permute-start | bytes 786440 | tf_op jit(solution)/shard_map/ppermute | solution.py:369
  53.6 1.2 %collective-permute-done.12.refs_13_ = f32[4,128,128]{2,1,0:T(8,128)S(1)} collective-permute-done((f32[4,128,128]{2,1,0:T(8,128)S(1)}, f32[4,128,128]{2,1,0:T(8,128)S(1)}, u32[]{:S(2)}, u32[]{:S(2)}) %collective-permute-start.12) | collective-permute-done | bytes 262176 | tf_op jit(solution)/shard_map/ppermute | solution.py:369
  54.8 2.6 %apply.7 = (bf16[256,2048]{1,0:T(8,128)(2,1)}, bf16[256,2048]{1,0:T(8,128)(2,1)}, bf16[256,2048]{1,0:T(8,128)(2,1)}, bf16[256,2048]{1,0:T(8,128)(2,1)}, f32[4,128,128]{2,1,0:T(8,128)}) custom-call(s32[6]{0:T(128)S(1)} %stack.39.info, ...), custom_call_target="tpu_custom_call", output_to_operand_aliasing={{0}: (15, {}), {1}: (16, {}), {2}: (17, {}), {3}: (18, {})} | custom-call | flops 1 | bytes 1 | tf_op jit(solution)/shard_map/apply/pallas_call | solution.py:308
  (13 shorter events, 0.3 us)
Async XLA Ops:
  3.2 2.3 %collective-permute-start = (f32[8,128,128]{2,1,0:T(8,128)S(1)}, f32[8,128,128]{2,1,0:T(8,128)S(1)}, u32[]{:S(2)}, u32[]{:S(2)}) collective-permute-start(f32[8,128,128]{2,1,0:T(8,128)S(1)} %get-tuple-element.55), channel_id=1, source_target_pairs={{0,1},{1,0},{2,3},{3,2},{4,5},{5,4},{6,7},{7,6},{8,9},{9,8},{10,11... | collective-permute-start | bytes 1572872 | tf_op jit(solution)/shard_map/ppermute | solution.py:369
  5.6 7.6 %collective-permute-start.1 = (f32[4,128,128]{2,1,0:T(8,128)S(1)}, f32[4,128,128]{2,1,0:T(8,128)S(1)}, u32[]{:S(2)}, u32[]{:S(2)}) collective-permute-start(f32[4,128,128]{2,1,0:T(8,128)S(1)} %slice_add_fusion.3.refs_0_), channel_id=1, source_target_pairs={{0,2},{1,3},{2,0},{3,1},{4,6},{5,7},{6,4},{7,5},{8,10},{9,11},{10,... | collective-permute-start | bytes 786440 | tf_op jit(solution)/shard_map/ppermute | solution.py:369
  13.1 2.7 %collective-permute-start.2 = (f32[8,128,128]{2,1,0:T(8,128)S(1)}, f32[8,128,128]{2,1,0:T(8,128)S(1)}, u32[]{:S(2)}, u32[]{:S(2)}) collective-permute-start(f32[8,128,128]{2,1,0:T(8,128)S(1)} %get-tuple-element.62), channel_id=1, source_target_pairs={{0,1},{1,0},{2,3},{3,2},{4,5},{5,4},{6,7},{7,6},{8,9},{9,8},{10,11... | collective-permute-start | bytes 1572872 | tf_op jit(solution)/shard_map/ppermute | solution.py:369
  14.4 11.1 %collective-permute-start.4 = (f32[4,128,128]{2,1,0:T(8,128)S(1)}, f32[4,128,128]{2,1,0:T(8,128)S(1)}, u32[]{:S(2)}, u32[]{:S(2)}) collective-permute-start(f32[4,128,128]{2,1,0:T(8,128)S(1)} %get-tuple-element.104), channel_id=1, source_target_pairs={{0,4},{1,5},{2,6},{3,7},{4,0},{5,1},{6,2},{7,3},{8,12},{9,13},{10,... | collective-permute-start | bytes 786440 | tf_op jit(solution)/shard_map/ppermute | solution.py:369
  15.9 9.6 %collective-permute-start.3 = (f32[4,128,128]{2,1,0:T(8,128)S(1)}, f32[4,128,128]{2,1,0:T(8,128)S(1)}, u32[]{:S(2)}, u32[]{:S(2)}) collective-permute-start(f32[4,128,128]{2,1,0:T(8,128)S(1)} %slice_add_fusion.2.refs_0_), channel_id=1, source_target_pairs={{0,2},{1,3},{2,0},{3,1},{4,6},{5,7},{6,4},{7,5},{8,10},{9,11},{10,... | collective-permute-start | bytes 786440 | tf_op jit(solution)/shard_map/ppermute | solution.py:369
  26.4 8.0 %collective-permute-start.10 = (f32[4,128,128]{2,1,0:T(8,128)S(1)}, f32[4,128,128]{2,1,0:T(8,128)S(1)}, u32[]{:S(2)}, u32[]{:S(2)}) collective-permute-start(f32[4,128,128]{2,1,0:T(8,128)S(1)} %get-tuple-element.81), channel_id=1, source_target_pairs={{0,1},{1,0},{2,3},{3,2},{4,5},{5,4},{6,7},{7,6},{8,9},{9,8},{10,11... | collective-permute-start | bytes 786440 | tf_op jit(solution)/shard_map/ppermute | solution.py:369
  27.1 9.2 %collective-permute-start.9 = (f32[4,128,128]{2,1,0:T(8,128)S(1)}, f32[4,128,128]{2,1,0:T(8,128)S(1)}, u32[]{:S(2)}, u32[]{:S(2)}) collective-permute-start(f32[4,128,128]{2,1,0:T(8,128)S(1)} %get-tuple-element.74.refs_9_.refs_14_), channel_id=1, source_target_pairs={{0,2},{1,3},{2,0},{3,1},{4,6},{5,7},{6,4},{7,5},{8,10},{9,11},{10,... | collective-permute-start | bytes 786440 | tf_op jit(solution)/shard_map/ppermute | solution.py:369
  27.3 10.0 %collective-permute-start.5 = (f32[4,128,128]{2,1,0:T(8,128)S(1)}, f32[4,128,128]{2,1,0:T(8,128)S(1)}, u32[]{:S(2)}, u32[]{:S(2)}) collective-permute-start(f32[4,128,128]{2,1,0:T(8,128)S(1)} %get-tuple-element.102), channel_id=1, source_target_pairs={{4,12},{5,13},{6,14},{7,15},{8,0},{9,1},{10,2},{11,3},{20,28},{21,... | collective-permute-start | bytes 786440 | tf_op jit(solution)/shard_map/ppermute | solution.py:369
  29.3 14.2 %collective-permute-start.6 = (f32[4,128,128]{2,1,0:T(8,128)S(1)}, f32[4,128,128]{2,1,0:T(8,128)S(1)}, u32[]{:S(2)}, u32[]{:S(2)}) collective-permute-start(f32[4,128,128]{2,1,0:T(8,128)S(1)} %get-tuple-element.102), channel_id=1, source_target_pairs={{4,8},{5,9},{6,10},{7,11},{8,4},{9,5},{10,6},{11,7},{20,24},{21,25... | collective-permute-start | bytes 786440 | tf_op jit(solution)/shard_map/ppermute | solution.py:369
  36.3 9.7 %collective-permute-start.11 = (f32[4,128,128]{2,1,0:T(8,128)S(1)}, f32[4,128,128]{2,1,0:T(8,128)S(1)}, u32[]{:S(2)}, u32[]{:S(2)}) collective-permute-start(f32[4,128,128]{2,1,0:T(8,128)S(1)} %get-tuple-element.111), channel_id=1, source_target_pairs={{0,1},{1,0},{2,3},{3,2},{4,5},{5,4},{6,7},{7,6},{8,9},{9,8},{10,11... | collective-permute-start | bytes 786440 | tf_op jit(solution)/shard_map/ppermute | solution.py:369
  43.5 5.1 %collective-permute-start.8 = (f32[4,128,128]{2,1,0:T(8,128)S(1)}, f32[4,128,128]{2,1,0:T(8,128)S(1)}, u32[]{:S(2)}, u32[]{:S(2)}) collective-permute-start(f32[4,128,128]{2,1,0:T(8,128)S(1)} %get-tuple-element.108), channel_id=1, source_target_pairs={{0,1},{1,0},{2,3},{3,2},{4,5},{5,4},{6,7},{7,6},{8,9},{9,8},{10,11... | collective-permute-start | bytes 786440 | tf_op jit(solution)/shard_map/ppermute | solution.py:369
  44.7 7.9 %collective-permute-start.7 = (f32[4,128,128]{2,1,0:T(8,128)S(1)}, f32[4,128,128]{2,1,0:T(8,128)S(1)}, u32[]{:S(2)}, u32[]{:S(2)}) collective-permute-start(f32[4,128,128]{2,1,0:T(8,128)S(1)} %get-tuple-element.106.refs_18_), channel_id=1, source_target_pairs={{0,2},{1,3},{2,0},{3,1},{4,6},{5,7},{6,4},{7,5},{8,10},{9,11},{10,... | collective-permute-start | bytes 786440 | tf_op jit(solution)/shard_map/ppermute | solution.py:369
  52.7 2.1 %collective-permute-start.12 = (f32[4,128,128]{2,1,0:T(8,128)S(1)}, f32[4,128,128]{2,1,0:T(8,128)S(1)}, u32[]{:S(2)}, u32[]{:S(2)}) collective-permute-start(f32[4,128,128]{2,1,0:T(8,128)S(1)} %get-tuple-element.109), channel_id=1, source_target_pairs={{0,1},{1,0},{2,3},{3,2},{4,5},{5,4},{6,7},{7,6},{8,9},{9,8},{10,11... | collective-permute-start | bytes 786440 | tf_op jit(solution)/shard_map/ppermute | solution.py:369

commit v3 on v2

--- a/solution.py
+++ b/solution.py
@@ -181,9 +181,9 @@
     )(info, *args, *after)
 
 
-def local_kernel(side, quarter, n_after, info, q, k, v, d, *refs):
+def local_kernel(side, quarter, mark, n_after, info, q, k, v, d, *refs):
     o_ref, dq_ref, dk_ref, dv_ref, zero = refs[n_after:]
-    zero[...] = jnp.zeros_like(zero)
+    zero[...] = jnp.full(zero.shape, jnp.where(info[INNER] == 1, mark, 0.0), F32)
     count = q.shape[0]
     two = 2
     scale = rows_scale(info[START], count)
@@ -211,11 +211,11 @@
         lax.fori_loop(0, quarter // two, step, 0)
 
 
-def local_part(info, args, side, after=()):
+def local_part(info, args, side, mark, after=()):
     count, width = args[0].shape
     quarter = width // DH // 4
     *partials, zero = pl.pallas_call(
-        functools.partial(local_kernel, side, quarter, len(after)),
+        functools.partial(local_kernel, side, quarter, mark, len(after)),
         out_shape=[jax.ShapeDtypeStruct((count, width // 2), F32)] * 4
         + [jax.ShapeDtypeStruct((quarter, DH, DH), F32)],
         in_specs=[IN_SMEM] + [IN_VMEM] * (4 + len(after)),
@@ -413,24 +413,24 @@
     f_keep, f_give = halves(f_own, f_got)
     f_other = send(f_give, row_swap)
     s_sib, s_own, *args = second_states(info, far_args, (f_give,))
-    s_sib, f_other = lax.optimization_barrier((s_sib, f_other))
+    half_a, zero = local_part(info, args, 0, 0.0, (s_own,))
+    s_sib, f_other, zero = lax.optimization_barrier((s_sib, f_other, zero))
     s_got = send(s_sib, core_swap)
     s_keep, s_give = halves(s_own, s_got)
     s_other = send(s_give, row_swap)
-    f_total = f_keep + f_other
+    f_total = f_keep + f_other + zero
     f = f_own, f_got, f_keep, f_other
     s = s_own, s_got, s_keep, s_other
-    half_a, zero = local_part(info, args, 0, (s_give,))
-    half_b, zero = local_part(info, args, 1, (zero,))
+    half_b, inside = local_part(info, args, 1, 1.0, (s_give,))
     partials = half_a, half_b
     if planes == 4:
         near = send(f_total, spread_pairs([(0, 1), (1, 0), (2, 3), (3, 2)]))
-        pair = s_keep + s_other + near + zero
-        far = send(pair, spread_pairs([(1, 3), (2, 0)]))
-        middle = send(pair, spread_pairs([(1, 2), (2, 1)]))
-        coming = far + middle
+        pair = jnp.where(inside > 0.0, s_keep + s_other + near, 0.0)
+        middle = send(pair, spread_pairs([(1, 2), (2, 1)]) + core_swap[:4] + core_swap[-4:])
+        outer = send(middle, spread_pairs([(0, 1), (1, 0), (2, 3), (3, 2)]))
+        coming = middle + outer
     else:
-        s_total = s_keep + s_other + zero
+        s_total = s_keep + s_other
         kv, qg = plane_scan(
             planes, jnp.where(even, f_total, s_total), jnp.where(even, s_total, f_total)
         )

time: 57.5 us -> 53.4 us (0.929)
  the two profiles are of different devices: /device:TPU:19 before, /device:TPU:0 now
where the time goes in v3:
time: 53.4 us; the launch traced here: 53.2 us
  Pallas kernels  25.3 us (47%)
  starting transfers between devices  15.1 us (28%)
  waiting for transfers between devices  11.5 us (22%)
  between operations  0.88 us (2%)
    ppermute x13, starting transfers between devices, send(): return lax.ppermute(array, 'seq', pairs)  15.1 us
    ppermute x13, waiting for transfers between devices, send(): return lax.ppermute(array, 'seq', pairs)  11.5 us
    pallas_call x4, Pallas kernels, apply_states(): pl.pallas_call(functools.partial(apply_kernel, early, kinds, sides, quart...  8.91 us
    pallas_call x2, Pallas kernels, local_part(): pl.pallas_call(functools.partial(local_kernel, side, quarter, mark, len(a...  8.24 us
    pallas_call x1, Pallas kernels, second_states(): pl.pallas_call(functools.partial(second_kernel, heads // 4, rows, len(aft...  3.21 us
    pallas_call x1, Pallas kernels, first_state(): pl.pallas_call(functools.partial(first_kernel, heads // 4, rows), out_sha...  2.46 us
    pallas_call x2, Pallas kernels, prepare(): pl.pallas_call(functools.partial(prepare_kernel, early, len(after)), out_...  1.44 us
  transfers between devices with their start and end apart: 13, of which 7 were waited for; matrix products, arithmetic and copies ran while one was open for 0% of the time, Pallas kernels for 38%

profile of v3, /device:TPU:0, one launch (start us, length us, event | category | flops | bytes accessed | tf_op | source)
XLA Modules:
  0.0 53.2 jit_solution(17582825910219888781)
XLA Ops:
  0.7 0.1 stack.39.info
  0.8 2.5 %first.1 = (f32[8,128,128]{2,1,0:T(8,128)S(1)}, bf16[256,2048]{1,0:T(8,128)(2,1)S(1)}, bf16[256,2048]{1,0:T(8,128)(2,1)S(1)}) custom-call(s32[6]{0:T(128)S(1)} %stack.39.info, bf16[256,2048]{1,0:T(8,128)(2,1)} %q.3, bf16[256,2048]{1,0:T(8,128)(2,1)} %k.3, bf16[256,2048]{1,0:T(8,128)(2,1)} %v.3, bf16[256,2048]{1,0:T(8,128)(2,1)} %d.3), custom_call_target="tpu_custom_call" | custom-call | flops 1 | bytes 1 | tf_op jit(solution)/shard_map/first/pallas_call | solution.py:104
  3.2 0.5 collective-permute-start
  3.8 1.0 %own.1.refs_1_ = f32[8,128,128]{2,1,0:T(8,128)S(1)} custom-call(s32[6]{0:T(128)S(1)} %stack.39.info, bf16[256,2048]{1,0:T(8,128)(2,1)S(1)} %get-tuple-element.54.left, bf16[256,2048]{1,0:T(8,128)(2,1)S(1)} %get-tuple-element.55.right), custom_call_target="tpu_custom_call" | custom-call | flops 1 | bytes 1 | tf_op jit(solution)/shard_map/own/pallas_call | solution.py:124
  4.8 0.5 collective-permute-done.refs_2_
  5.3 3.0 %collective-permute-start.1 = (f32[4,128,128]{2,1,0:T(8,128)S(1)}, f32[4,128,128]{2,1,0:T(8,128)S(1)}, u32[]{:S(2)}, u32[]{:S(2)}) collective-permute-start(f32[4,128,128]{2,1,0:T(8,128)S(1)} %slice_add_fusion.3.refs_0_), channel_id=1, source_target_pairs={{0,2},{1,3},{2,0},{3,1},{4,6},{5,7},{6,4},{7,5},{8,10},{9,11},{10,... | collective-permute-start | bytes 786440 | tf_op jit(solution)/shard_map/ppermute | solution.py:369
  8.3 3.2 %second.1 = (f32[8,128,128]{2,1,0:T(8,128)S(1)}, f32[8,128,128]{2,1,0:T(8,128)S(1)}, bf16[256,2048]{1,0:T(8,128)(2,1)S(1)}, bf16[256,2048]{1,0:T(8,128)(2,1)S(1)...) custom-call(s32[6]{0:T(128)S(1)} %stack.39.info, bf16[256,2048]{1,0:T(8,128)(2,1)} %q.3, ...), custom_call_target="tpu_custom_call" | custom-call | flops 1 | bytes 1 | tf_op jit(solution)/shard_map/second/pallas_call | solution.py:171
  11.5 4.1 %local.2 = (f32[256,1024]{1,0:T(8,128)S(1)}, f32[256,1024]{1,0:T(8,128)S(1)}, f32[256,1024]{1,0:T(8,128)S(1)}, f32[256,1024]{1,0:T(8,128)S(1)}, f32[4,128,128]{2,1,0:T(8,128)S(1)}) custom-call(s32[6]{0:T(128)S(1)} %stack.39.info, bf16[256,2048]{1,0:T(8,128)(2,1)S(1)} %get-tuple-element.57.q.refs_0_, bf16[256,2048]{1,0:T(8,128)(2,1)S(1)} %get-tuple-element.58.k.refs_1_, ...), custom_call_target="tpu_custom_call" | custom-call | flops 1 | bytes 1 | tf_op jit(solution)/shard_map/local/pallas_call | solution.py:217
  15.6 0.1 collective-permute-start.2
  15.7 0.1 add_add_fusion.2
  15.8 1.6 %collective-permute-start.4 = (f32[4,128,128]{2,1,0:T(8,128)S(1)}, f32[4,128,128]{2,1,0:T(8,128)S(1)}, u32[]{:S(2)}, u32[]{:S(2)}) collective-permute-start(f32[4,128,128]{2,1,0:T(8,128)S(1)} %get-tuple-element.106), channel_id=1, source_target_pairs={{0,4},{1,5},{2,6},{3,7},{4,0},{5,1},{6,2},{7,3},{8,12},{9,13},{10,... | collective-permute-start | bytes 786440 | tf_op jit(solution)/shard_map/ppermute | solution.py:369
  17.4 0.2 collective-permute-done.2.refs_6_
  17.7 1.0 %collective-permute-start.3 = (f32[4,128,128]{2,1,0:T(8,128)S(1)}, f32[4,128,128]{2,1,0:T(8,128)S(1)}, u32[]{:S(2)}, u32[]{:S(2)}) collective-permute-start(f32[4,128,128]{2,1,0:T(8,128)S(1)} %slice_add_fusion.2.refs_0_), channel_id=1, source_target_pairs={{0,2},{1,3},{2,0},{3,1},{4,6},{5,7},{6,4},{7,5},{8,10},{9,11},{10,... | collective-permute-start | bytes 786440 | tf_op jit(solution)/shard_map/ppermute | solution.py:369
  18.6 4.1 %local.3 = (f32[256,1024]{1,0:T(8,128)S(1)}, f32[256,1024]{1,0:T(8,128)S(1)}, f32[256,1024]{1,0:T(8,128)S(1)}, f32[256,1024]{1,0:T(8,128)S(1)}, f32[4,128,128]{2,1,0:T(8,128)S(1)}) custom-call(s32[6]{0:T(128)S(1)} %stack.39.info, bf16[256,2048]{1,0:T(8,128)(2,1)S(1)} %get-tuple-element.57.q.refs_0_, bf16[256,2048]{1,0:T(8,128)(2,1)S(1)} %get-tuple-element.58.k.refs_1_, ...), custom_call_target="tpu_custom_call" | custom-call | flops 1 | bytes 1 | tf_op jit(solution)/shard_map/local/pallas_call | solution.py:217
  22.8 1.8 %collective-permute-done.4.refs_0_ = f32[4,128,128]{2,1,0:T(8,128)S(1)} collective-permute-done((f32[4,128,128]{2,1,0:T(8,128)S(1)}, f32[4,128,128]{2,1,0:T(8,128)S(1)}, u32[]{:S(2)}, u32[]{:S(2)}) %collective-permute-start.4) | collective-permute-done | bytes 262176 | tf_op jit(solution)/shard_map/ppermute | solution.py:369
  24.6 1.5 %collective-permute-done.3.refs_8_ = f32[4,128,128]{2,1,0:T(8,128)S(1)} collective-permute-done((f32[4,128,128]{2,1,0:T(8,128)S(1)}, f32[4,128,128]{2,1,0:T(8,128)S(1)}, u32[]{:S(2)}, u32[]{:S(2)}) %collective-permute-start.3) | collective-permute-done | bytes 262176 | tf_op jit(solution)/shard_map/ppermute | solution.py:369
  26.1 0.1 add_select_fusion
  26.2 0.1 collective-permute-start.5
  26.2 0.7 %prepare.2 = (f32[4,128,128]{2,1,0:T(8,128)S(1)}, f32[4,128,128]{2,1,0:T(8,128)S(1)}, f32[4,128,128]{2,1,0:T(8,128)S(1)}, f32[4,128,128]{2,1,0:T(8,128)S(1)}, f32[4,128,128]{2,1,0:T(8,128)S(1)}) custom-call(s32[6]{0:T(128)S(1)} %stack.39.info, f32[4,128,128]{2,1,0:T(8,128)S(1)} %collective-permute-done.4.refs_0_, f32[8,128,128]{2,1,0:T(8,128)S(1)} %own.1.refs_1_, ...), custom_call_target="tpu_custom_call" | custom-call | flops 1 | bytes 1 | tf_op jit(solution)/shard_map/prepare/pallas_call | solution.py:357
  27.0 0.6 %collective-permute-start.10 = (f32[4,128,128]{2,1,0:T(8,128)S(1)}, f32[4,128,128]{2,1,0:T(8,128)S(1)}, u32[]{:S(2)}, u32[]{:S(2)}) collective-permute-start(f32[4,128,128]{2,1,0:T(8,128)S(1)} %get-tuple-element.83), channel_id=1, source_target_pairs={{0,1},{1,0},{2,3},{3,2},{4,5},{5,4},{6,7},{7,6},{8,9},{9,8},{10,11... | collective-permute-start | bytes 786440 | tf_op jit(solution)/shard_map/ppermute | solution.py:369
  27.5 0.9 %collective-permute-start.9 = (f32[4,128,128]{2,1,0:T(8,128)S(1)}, f32[4,128,128]{2,1,0:T(8,128)S(1)}, u32[]{:S(2)}, u32[]{:S(2)}) collective-permute-start(f32[4,128,128]{2,1,0:T(8,128)S(1)} %get-tuple-element.76.refs_9_.refs_14_), channel_id=1, source_target_pairs={{0,2},{1,3},{2,0},{3,1},{4,6},{5,7},{6,4},{7,5},{8,10},{9,11},{10,... | collective-permute-start | bytes 786440 | tf_op jit(solution)/shard_map/ppermute | solution.py:369
  28.5 0.7 %prepare.3 = (f32[4,128,128]{2,1,0:T(8,128)S(1)}, f32[4,128,128]{2,1,0:T(8,128)S(1)}, f32[4,128,128]{2,1,0:T(8,128)S(1)}, f32[4,128,128]{2,1,0:T(8,128)S(1)}, f32[4,128,128]{2,1,0:T(8,128)S(1)}) custom-call(s32[6]{0:T(128)S(1)} %stack.39.info, f32[4,128,128]{2,1,0:T(8,128)S(1)} %collective-permute-done.4.refs_0_, f32[8,128,128]{2,1,0:T(8,128)S(1)} %own.1.refs_1_, ...), custom_call_target="tpu_custom_call" | custom-call | flops 1 | bytes 1 | tf_op jit(solution)/shard_map/prepare/pallas_call | solution.py:357
  29.2 6.1 %collective-permute-start.6 = (f32[4,128,128]{2,1,0:T(8,128)S(1)}, f32[4,128,128]{2,1,0:T(8,128)S(1)}, u32[]{:S(2)}, u32[]{:S(2)}) collective-permute-start(f32[4,128,128]{2,1,0:T(8,128)S(1)} %collective-permute-done.5), channel_id=1, source_target_pairs={{0,4},{1,5},{2,6},{3,7},{4,0},{5,1},{6,2},{7,3},{8,12},{9,13},{10,... | collective-permute-start | bytes 786440 | tf_op jit(solution)/shard_map/ppermute | solution.py:369
  35.3 1.9 %apply.4 = (bf16[256,2048]{1,0:T(8,128)(2,1)}, bf16[256,2048]{1,0:T(8,128)(2,1)}, bf16[256,2048]{1,0:T(8,128)(2,1)}, bf16[256,2048]{1,0:T(8,128)(2,1)}, f32[4,128,128]{2,1,0:T(8,128)S(1)}) custom-call(s32[6]{0:T(128)S(1)} %stack.39.info, bf16[256,2048]{1,0:T(8,128)(2,1)S(1)} %get-tuple-element.57.q.refs_0_, ...), custom_call_target="tpu_custom_call" | custom-call | flops 1 | bytes 1 | tf_op jit(solution)/shard_map/apply/pallas_call | solution.py:308
  37.3 2.8 %collective-permute-done.6 = f32[4,128,128]{2,1,0:T(8,128)S(1)} collective-permute-done((f32[4,128,128]{2,1,0:T(8,128)S(1)}, f32[4,128,128]{2,1,0:T(8,128)S(1)}, u32[]{:S(2)}, u32[]{:S(2)}) %collective-permute-start.6) | collective-permute-done | bytes 262176 | tf_op jit(solution)/shard_map/ppermute | solution.py:369
  40.1 0.1 add_add_fusion.5
  40.3 1.1 %collective-permute-start.7 = (f32[4,128,128]{2,1,0:T(8,128)S(1)}, f32[4,128,128]{2,1,0:T(8,128)S(1)}, u32[]{:S(2)}, u32[]{:S(2)}) collective-permute-start(f32[4,128,128]{2,1,0:T(8,128)S(1)} %get-tuple-element.108.refs_18_), channel_id=1, source_target_pairs={{0,2},{1,3},{2,0},{3,1},{4,6},{5,7},{6,4},{7,5},{8,10},{9,11},{10,... | collective-permute-start | bytes 786440 | tf_op jit(solution)/shard_map/ppermute | solution.py:369
  41.4 2.6 %apply.5 = (bf16[256,2048]{1,0:T(8,128)(2,1)}, bf16[256,2048]{1,0:T(8,128)(2,1)}, bf16[256,2048]{1,0:T(8,128)(2,1)}, bf16[256,2048]{1,0:T(8,128)(2,1)}, f32[4,128,128]{2,1,0:T(8,128)}) custom-call(s32[6]{0:T(128)S(1)} %stack.39.info, ...), custom_call_target="tpu_custom_call", output_to_operand_aliasing={{0}: (15, {}), {1}: (16, {}), {2}: (17, {}), {3}: (18, {})} | custom-call | flops 1 | bytes 1 | tf_op jit(solution)/shard_map/apply/pallas_call | solution.py:308
  44.0 1.8 %apply.6 = (bf16[256,2048]{1,0:T(8,128)(2,1)}, bf16[256,2048]{1,0:T(8,128)(2,1)}, bf16[256,2048]{1,0:T(8,128)(2,1)}, bf16[256,2048]{1,0:T(8,128)(2,1)}, f32[4,128,128]{2,1,0:T(8,128)S(1)}) custom-call(s32[6]{0:T(128)S(1)} %stack.39.info, ...), custom_call_target="tpu_custom_call", output_to_operand_aliasing={{0}: (15, {}), {1}: (16, {}), {2}: (17, {}), {3}: (18, {})} | custom-call | flops 1 | bytes 1 | tf_op jit(solution)/shard_map/apply/pallas_call | solution.py:308
  45.9 3.1 %collective-permute-done.7 = f32[4,128,128]{2,1,0:T(8,128)S(1)} collective-permute-done((f32[4,128,128]{2,1,0:T(8,128)S(1)}, f32[4,128,128]{2,1,0:T(8,128)S(1)}, u32[]{:S(2)}, u32[]{:S(2)}) %collective-permute-start.7) | collective-permute-done | bytes 262176 | tf_op jit(solution)/shard_map/ppermute | solution.py:369
  49.2 1.5 %collective-permute-done.12.refs_13_ = f32[4,128,128]{2,1,0:T(8,128)S(1)} collective-permute-done((f32[4,128,128]{2,1,0:T(8,128)S(1)}, f32[4,128,128]{2,1,0:T(8,128)S(1)}, u32[]{:S(2)}, u32[]{:S(2)}) %collective-permute-start.12) | collective-permute-done | bytes 262176 | tf_op jit(solution)/shard_map/ppermute | solution.py:369
  50.7 2.6 %apply.7 = (bf16[256,2048]{1,0:T(8,128)(2,1)}, bf16[256,2048]{1,0:T(8,128)(2,1)}, bf16[256,2048]{1,0:T(8,128)(2,1)}, bf16[256,2048]{1,0:T(8,128)(2,1)}, f32[4,128,128]{2,1,0:T(8,128)}) custom-call(s32[6]{0:T(128)S(1)} %stack.39.info, ...), custom_call_target="tpu_custom_call", output_to_operand_aliasing={{0}: (15, {}), {1}: (16, {}), {2}: (17, {}), {3}: (18, {})} | custom-call | flops 1 | bytes 1 | tf_op jit(solution)/shard_map/apply/pallas_call | solution.py:308
  (13 shorter events, 0.4 us)
Async XLA Ops:
  3.2 2.1 %collective-permute-start = (f32[8,128,128]{2,1,0:T(8,128)S(1)}, f32[8,128,128]{2,1,0:T(8,128)S(1)}, u32[]{:S(2)}, u32[]{:S(2)}) collective-permute-start(f32[8,128,128]{2,1,0:T(8,128)S(1)} %get-tuple-element.56), channel_id=1, source_target_pairs={{0,1},{1,0},{2,3},{3,2},{4,5},{5,4},{6,7},{7,6},{8,9},{9,8},{10,11... | collective-permute-start | bytes 1572872 | tf_op jit(solution)/shard_map/ppermute | solution.py:369
  5.3 10.3 %collective-permute-start.1 = (f32[4,128,128]{2,1,0:T(8,128)S(1)}, f32[4,128,128]{2,1,0:T(8,128)S(1)}, u32[]{:S(2)}, u32[]{:S(2)}) collective-permute-start(f32[4,128,128]{2,1,0:T(8,128)S(1)} %slice_add_fusion.3.refs_0_), channel_id=1, source_target_pairs={{0,2},{1,3},{2,0},{3,1},{4,6},{5,7},{6,4},{7,5},{8,10},{9,11},{10,... | collective-permute-start | bytes 786440 | tf_op jit(solution)/shard_map/ppermute | solution.py:369
  15.6 2.0 %collective-permute-start.2 = (f32[8,128,128]{2,1,0:T(8,128)S(1)}, f32[8,128,128]{2,1,0:T(8,128)S(1)}, u32[]{:S(2)}, u32[]{:S(2)}) collective-permute-start(f32[8,128,128]{2,1,0:T(8,128)S(1)} %get-tuple-element.68), channel_id=1, source_target_pairs={{0,1},{1,0},{2,3},{3,2},{4,5},{5,4},{6,7},{7,6},{8,9},{9,8},{10,11... | collective-permute-start | bytes 1572872 | tf_op jit(solution)/shard_map/ppermute | solution.py:369
  15.8 8.8 %collective-permute-start.4 = (f32[4,128,128]{2,1,0:T(8,128)S(1)}, f32[4,128,128]{2,1,0:T(8,128)S(1)}, u32[]{:S(2)}, u32[]{:S(2)}) collective-permute-start(f32[4,128,128]{2,1,0:T(8,128)S(1)} %get-tuple-element.106), channel_id=1, source_target_pairs={{0,4},{1,5},{2,6},{3,7},{4,0},{5,1},{6,2},{7,3},{8,12},{9,13},{10,... | collective-permute-start | bytes 786440 | tf_op jit(solution)/shard_map/ppermute | solution.py:369
  17.7 8.4 %collective-permute-start.3 = (f32[4,128,128]{2,1,0:T(8,128)S(1)}, f32[4,128,128]{2,1,0:T(8,128)S(1)}, u32[]{:S(2)}, u32[]{:S(2)}) collective-permute-start(f32[4,128,128]{2,1,0:T(8,128)S(1)} %slice_add_fusion.2.refs_0_), channel_id=1, source_target_pairs={{0,2},{1,3},{2,0},{3,1},{4,6},{5,7},{6,4},{7,5},{8,10},{9,11},{10,... | collective-permute-start | bytes 786440 | tf_op jit(solution)/shard_map/ppermute | solution.py:369
  26.2 3.0 %collective-permute-start.5 = (f32[4,128,128]{2,1,0:T(8,128)S(1)}, f32[4,128,128]{2,1,0:T(8,128)S(1)}, u32[]{:S(2)}, u32[]{:S(2)}) collective-permute-start(f32[4,128,128]{2,1,0:T(8,128)S(1)} %get-tuple-element.104), channel_id=1, source_target_pairs={{4,8},{5,9},{6,10},{7,11},{8,4},{9,5},{10,6},{11,7},{0,1},{1,0},{2... | collective-permute-start | bytes 786440 | tf_op jit(solution)/shard_map/ppermute | solution.py:369
  27.0 8.3 %collective-permute-start.10 = (f32[4,128,128]{2,1,0:T(8,128)S(1)}, f32[4,128,128]{2,1,0:T(8,128)S(1)}, u32[]{:S(2)}, u32[]{:S(2)}) collective-permute-start(f32[4,128,128]{2,1,0:T(8,128)S(1)} %get-tuple-element.83), channel_id=1, source_target_pairs={{0,1},{1,0},{2,3},{3,2},{4,5},{5,4},{6,7},{7,6},{8,9},{9,8},{10,11... | collective-permute-start | bytes 786440 | tf_op jit(solution)/shard_map/ppermute | solution.py:369
  27.5 9.7 %collective-permute-start.9 = (f32[4,128,128]{2,1,0:T(8,128)S(1)}, f32[4,128,128]{2,1,0:T(8,128)S(1)}, u32[]{:S(2)}, u32[]{:S(2)}) collective-permute-start(f32[4,128,128]{2,1,0:T(8,128)S(1)} %get-tuple-element.76.refs_9_.refs_14_), channel_id=1, source_target_pairs={{0,2},{1,3},{2,0},{3,1},{4,6},{5,7},{6,4},{7,5},{8,10},{9,11},{10,... | collective-permute-start | bytes 786440 | tf_op jit(solution)/shard_map/ppermute | solution.py:369
  29.2 10.9 %collective-permute-start.6 = (f32[4,128,128]{2,1,0:T(8,128)S(1)}, f32[4,128,128]{2,1,0:T(8,128)S(1)}, u32[]{:S(2)}, u32[]{:S(2)}) collective-permute-start(f32[4,128,128]{2,1,0:T(8,128)S(1)} %collective-permute-done.5), channel_id=1, source_target_pairs={{0,4},{1,5},{2,6},{3,7},{4,0},{5,1},{6,2},{7,3},{8,12},{9,13},{10,... | collective-permute-start | bytes 786440 | tf_op jit(solution)/shard_map/ppermute | solution.py:369
  37.3 4.1 %collective-permute-start.11 = (f32[4,128,128]{2,1,0:T(8,128)S(1)}, f32[4,128,128]{2,1,0:T(8,128)S(1)}, u32[]{:S(2)}, u32[]{:S(2)}) collective-permute-start(f32[4,128,128]{2,1,0:T(8,128)S(1)} %get-tuple-element.113), channel_id=1, source_target_pairs={{0,1},{1,0},{2,3},{3,2},{4,5},{5,4},{6,7},{7,6},{8,9},{9,8},{10,11... | collective-permute-start | bytes 786440 | tf_op jit(solution)/shard_map/ppermute | solution.py:369
  40.2 3.8 %collective-permute-start.8 = (f32[4,128,128]{2,1,0:T(8,128)S(1)}, f32[4,128,128]{2,1,0:T(8,128)S(1)}, u32[]{:S(2)}, u32[]{:S(2)}) collective-permute-start(f32[4,128,128]{2,1,0:T(8,128)S(1)} %get-tuple-element.110), channel_id=1, source_target_pairs={{0,1},{1,0},{2,3},{3,2},{4,5},{5,4},{6,7},{7,6},{8,9},{9,8},{10,11... | collective-permute-start | bytes 786440 | tf_op jit(solution)/shard_map/ppermute | solution.py:369
  40.3 8.7 %collective-permute-start.7 = (f32[4,128,128]{2,1,0:T(8,128)S(1)}, f32[4,128,128]{2,1,0:T(8,128)S(1)}, u32[]{:S(2)}, u32[]{:S(2)}) collective-permute-start(f32[4,128,128]{2,1,0:T(8,128)S(1)} %get-tuple-element.108.refs_18_), channel_id=1, source_target_pairs={{0,2},{1,3},{2,0},{3,1},{4,6},{5,7},{6,4},{7,5},{8,10},{9,11},{10,... | collective-permute-start | bytes 786440 | tf_op jit(solution)/shard_map/ppermute | solution.py:369
  49.1 1.6 %collective-permute-start.12 = (f32[4,128,128]{2,1,0:T(8,128)S(1)}, f32[4,128,128]{2,1,0:T(8,128)S(1)}, u32[]{:S(2)}, u32[]{:S(2)}) collective-permute-start(f32[4,128,128]{2,1,0:T(8,128)S(1)} %get-tuple-element.111), channel_id=1, source_target_pairs={{0,1},{1,0},{2,3},{3,2},{4,5},{5,4},{6,7},{7,6},{8,9},{9,8},{10,11... | collective-permute-start | bytes 786440 | tf_op jit(solution)/shard_map/ppermute | solution.py:369

commit v4 on v3

--- a/solution.py
+++ b/solution.py
@@ -181,9 +181,9 @@
     )(info, *args, *after)
 
 
-def local_kernel(side, quarter, mark, n_after, info, q, k, v, d, *refs):
-    o_ref, dq_ref, dk_ref, dv_ref, zero = refs[n_after:]
-    zero[...] = jnp.full(zero.shape, jnp.where(info[INNER] == 1, mark, 0.0), F32)
+def local_kernel(kinds, quarter, mark, n_after, info, q, k, v, d, *refs):
+    *parts, flag = refs[n_after:]
+    flag[...] = jnp.full(flag.shape, jnp.where(info[INNER] == 1, mark, 0.0), F32)
     count = q.shape[0]
     two = 2
     scale = rows_scale(info[START], count)
@@ -191,12 +191,13 @@
         jnp.int32, (count, count), 0
     )
 
-    for part in range(2):
+    for n, (side, part) in enumerate(kinds):
         first = first_head(info, side, part, quarter)
+        o_ref, dq_ref, dk_ref, dv_ref = parts[4 * n : 4 * n + 4]
 
         def step(g, carry):
             for i in range(two):
-                to = pl.ds(pl.multiple_of((part * quarter + g * two + i) * DH, DH), DH)
+                to = pl.ds(pl.multiple_of((g * two + i) * DH, DH), DH)
                 cols = pl.ds(pl.multiple_of((first + g * two + i) * DH, DH), DH)
                 qh, kh, vh = q[:, cols], k[:, cols], v[:, cols]
                 ph = (d[:, cols].astype(F32) * scale).astype(BF16)
@@ -211,27 +212,27 @@
         lax.fori_loop(0, quarter // two, step, 0)
 
 
-def local_part(info, args, side, mark, after=()):
+def local_part(info, args, kinds, mark, after=()):
     count, width = args[0].shape
     quarter = width // DH // 4
-    *partials, zero = pl.pallas_call(
-        functools.partial(local_kernel, side, quarter, mark, len(after)),
-        out_shape=[jax.ShapeDtypeStruct((count, width // 2), F32)] * 4
+    *parts, flag = pl.pallas_call(
+        functools.partial(local_kernel, kinds, quarter, mark, len(after)),
+        out_shape=[jax.ShapeDtypeStruct((count, width // 4), F32)] * (4 * len(kinds))
         + [jax.ShapeDtypeStruct((quarter, DH, DH), F32)],
         in_specs=[IN_SMEM] + [IN_VMEM] * (4 + len(after)),
-        out_specs=[IN_VMEM] * 5,
+        out_specs=[IN_VMEM] * (4 * len(kinds) + 1),
         compiler_params=pltpu.CompilerParams(vmem_limit_bytes=8 * MIB),
         cost_estimate=SMALL,
         name="local",
     )(info, *args, *after)
-    return partials, zero
-
-
-def apply_kernel(early, kinds, sides, quarter, n_filled, n_after, info, *refs):
+    return {kind: parts[4 * n : 4 * n + 4] for n, kind in enumerate(kinds)}, flag
+
+
+def apply_kernel(early, kinds, quarter, n_filled, n_after, info, *refs):
     q, k, v, d = refs[:4]
     refs = refs[4:]
-    partials = {side: refs[4 * n : 4 * n + 4] for n, side in enumerate(sides)}
-    refs = refs[4 * len(sides) :]
+    partials = [refs[4 * n : 4 * n + 4] for n in range(len(kinds))]
+    refs = refs[4 * len(kinds) :]
     state_refs, refs = refs[: len(kinds)], refs[len(kinds) + n_filled + n_after :]
     o_hbm, dq_hbm, dk_hbm, dv_hbm, zero, one, other, sems = refs
     zero[...] = jnp.zeros_like(zero)
@@ -255,14 +256,13 @@
 
     def each_head(products, a, b):
         for step, (n, j) in enumerate(steps):
-            side, part = kinds[n]
             for i in range(two):
                 head = j * two + i
                 cols = pl.ds(columns(n, head), DH)
-                at = (part * quarter + head) * DH
+                at = head * DH
                 here = slice((step * two + i) * DH, (step * two + i + 1) * DH)
                 one[:, here], other[:, here] = products(
-                    cols, partials[side], slice(at, at + DH), state_refs[n][head].astype(BF16)
+                    cols, partials[n], slice(at, at + DH), state_refs[n][head].astype(BF16)
                 )
             for copy in copies(step, a, b):
                 copy.start()
@@ -301,13 +301,12 @@
     count, width = args[0].shape
     quarter = width // DH // 4
     filled = () if outs is None else tuple(outs)
-    sides = sorted({side for side, _ in kinds})
-    partials = [x for side in sides for x in partials[side]]
+    partials = [x for kind in kinds for x in partials[kind]]
     first_out = 5 + len(partials) + len(kinds)
     columns = len(kinds) * quarter * DH
     return pl.pallas_call(
         functools.partial(
-            apply_kernel, early, kinds, sides, quarter, len(filled), len(after)
+            apply_kernel, early, kinds, quarter, len(filled), len(after)
         ),
         out_shape=[jax.ShapeDtypeStruct((count, width), BF16)] * 4
         + [jax.ShapeDtypeStruct((quarter, DH, DH), F32)],
@@ -407,22 +406,22 @@
     def halves(own, got):
         return own[:quarter] + got[:quarter], own[quarter:] + got[quarter:]
 
+    kinds = (0, 0), (0, 1), (1, 0), (1, 1)
     f_sib, left, right = first_state(info, far_args)
     f_got = send(f_sib, core_swap)
     f_own = own_state(info, left, right)
     f_keep, f_give = halves(f_own, f_got)
     f_other = send(f_give, row_swap)
     s_sib, s_own, *args = second_states(info, far_args, (f_give,))
-    half_a, zero = local_part(info, args, 0, 0.0, (s_own,))
-    s_sib, f_other, zero = lax.optimization_barrier((s_sib, f_other, zero))
+    part_a, zero = local_part(info, args, kinds[:1], 0.0, (s_own,))
     s_got = send(s_sib, core_swap)
     s_keep, s_give = halves(s_own, s_got)
     s_other = send(s_give, row_swap)
     f_total = f_keep + f_other + zero
     f = f_own, f_got, f_keep, f_other
     s = s_own, s_got, s_keep, s_other
-    half_b, inside = local_part(info, args, 1, 1.0, (s_give,))
-    partials = half_a, half_b
+    part_b, inside = local_part(info, args, kinds[1:], 1.0, (s_give,))
+    partials = part_a | part_b
     if planes == 4:
         near = send(f_total, spread_pairs([(0, 1), (1, 0), (2, 3), (3, 2)]))
         pair = jnp.where(inside > 0.0, s_keep + s_other + near, 0.0)
@@ -439,7 +438,7 @@
     across, mine, theirs, rest_mine, rest_theirs = prepare(info, True, near, f, s, ())
 
     finish = functools.partial(apply_states, info, args, partials)
-    kept_heads, other_heads = ((0, 0), (1, 0)), ((0, 1), (1, 1))
+    kept_heads, other_heads = kinds[0::2], kinds[1::2]
     t_other = send(across, row_swap)
     t_kept = mine, send(theirs, core_swap)
     late = prepare(info, False, near, f, s, (across,))

time: 53.4 us -> 50.7 us (0.949)
  waiting for transfers between devices: 11.5 us -> 9.07 us
    ppermute x13, waiting for transfers between devices: 11.5 us -> 9.07 us  [send(): return lax.ppermute(array, 'seq', pairs)]
  transfers between devices with their start and end apart: 13 -> 13, of which waited for: 7 -> 5; matrix products, arithmetic and copies ran while one was open for 0% -> 0% of each run, Pallas kernels for 38% -> 40%
where the time goes in v4:
time: 50.7 us; the launch traced here: 50.6 us
  Pallas kernels  25.3 us (50%)
  starting transfers between devices  14.8 us (29%)
  waiting for transfers between devices  9.07 us (18%)
  between operations  0.88 us (2%)
    ppermute x13, starting transfers between devices, send(): return lax.ppermute(array, 'seq', pairs)  14.8 us
    ppermute x13, waiting for transfers between devices, send(): return lax.ppermute(array, 'seq', pairs)  9.07 us
    pallas_call x4, Pallas kernels, apply_states(): pl.pallas_call(functools.partial(apply_kernel, early, kinds, quarter, len...  8.93 us
    pallas_call x2, Pallas kernels, local_part(): pl.pallas_call(functools.partial(local_kernel, kinds, quarter, mark, len(...  8.24 us
    pallas_call x1, Pallas kernels, second_states(): pl.pallas_call(functools.partial(second_kernel, heads // 4, rows, len(aft...  3.21 us
    pallas_call x1, Pallas kernels, first_state(): pl.pallas_call(functools.partial(first_kernel, heads // 4, rows), out_sha...  2.46 us
    pallas_call x2, Pallas kernels, prepare(): pl.pallas_call(functools.partial(prepare_kernel, early, len(after)), out_...  1.44 us
    pallas_call x1, Pallas kernels, own_state(): pl.pallas_call(functools.partial(own_kernel, heads // 4), out_shape=jax.S...  1.02 us
  transfers between devices with their start and end apart: 13, of which 5 were waited for; matrix products, arithmetic and copies ran while one was open for 0% of the time, Pallas kernels for 40%

profile of v4, /device:TPU:0, one launch (start us, length us, event | category | flops | bytes accessed | tf_op | source)
XLA Modules:
  0.0 50.6 jit_solution(7559981016803445622)
XLA Ops:
  0.7 0.1 stack.39.info
  0.8 2.5 %first.1 = (f32[8,128,128]{2,1,0:T(8,128)S(1)}, bf16[256,2048]{1,0:T(8,128)(2,1)S(1)}, bf16[256,2048]{1,0:T(8,128)(2,1)S(1)}) custom-call(s32[6]{0:T(128)S(1)} %stack.39.info, bf16[256,2048]{1,0:T(8,128)(2,1)} %q.3, bf16[256,2048]{1,0:T(8,128)(2,1)} %k.3, bf16[256,2048]{1,0:T(8,128)(2,1)} %v.3, bf16[256,2048]{1,0:T(8,128)(2,1)} %d.3), custom_call_target="tpu_custom_call" | custom-call | flops 1 | bytes 1 | tf_op jit(solution)/shard_map/first/pallas_call | solution.py:104
  3.2 0.5 %collective-permute-start = (f32[8,128,128]{2,1,0:T(8,128)S(1)}, f32[8,128,128]{2,1,0:T(8,128)S(1)}, u32[]{:S(2)}, u32[]{:S(2)}) collective-permute-start(f32[8,128,128]{2,1,0:T(8,128)S(1)} %get-tuple-element.61), channel_id=1, source_target_pairs={{0,1},{1,0},{2,3},{3,2},{4,5},{5,4},{6,7},{7,6},{8,9},{9,8},{10,11... | collective-permute-start | bytes 1572872 | tf_op jit(solution)/shard_map/ppermute | solution.py:368
  3.8 1.0 %own.1.refs_1_ = f32[8,128,128]{2,1,0:T(8,128)S(1)} custom-call(s32[6]{0:T(128)S(1)} %stack.39.info, bf16[256,2048]{1,0:T(8,128)(2,1)S(1)} %get-tuple-element.59.left, bf16[256,2048]{1,0:T(8,128)(2,1)S(1)} %get-tuple-element.60.right), custom_call_target="tpu_custom_call" | custom-call | flops 1 | bytes 1 | tf_op jit(solution)/shard_map/own/pallas_call | solution.py:124
  4.8 0.5 %collective-permute-done.refs_2_ = f32[8,128,128]{2,1,0:T(8,128)S(1)} collective-permute-done((f32[8,128,128]{2,1,0:T(8,128)S(1)}, f32[8,128,128]{2,1,0:T(8,128)S(1)}, u32[]{:S(2)}, u32[]{:S(2)}) %collective-permute-start) | collective-permute-done | bytes 524320 | tf_op jit(solution)/shard_map/ppermute | solution.py:368
  5.3 3.0 %collective-permute-start.3 = (f32[4,128,128]{2,1,0:T(8,128)S(1)}, f32[4,128,128]{2,1,0:T(8,128)S(1)}, u32[]{:S(2)}, u32[]{:S(2)}) collective-permute-start(f32[4,128,128]{2,1,0:T(8,128)S(1)} %slice_add_fusion.3.refs_0_), channel_id=1, source_target_pairs={{0,2},{1,3},{2,0},{3,1},{4,6},{5,7},{6,4},{7,5},{8,10},{9,11},{10,... | collective-permute-start | bytes 786440 | tf_op jit(solution)/shard_map/ppermute | solution.py:368
  8.3 3.2 %second.1 = (f32[8,128,128]{2,1,0:T(8,128)S(1)}, f32[8,128,128]{2,1,0:T(8,128)S(1)}, bf16[256,2048]{1,0:T(8,128)(2,1)S(1)}, bf16[256,2048]{1,0:T(8,128)(2,1)S(1)...) custom-call(s32[6]{0:T(128)S(1)} %stack.39.info, bf16[256,2048]{1,0:T(8,128)(2,1)} %q.3, ...), custom_call_target="tpu_custom_call" | custom-call | flops 1 | bytes 1 | tf_op jit(solution)/shard_map/second/pallas_call | solution.py:171
  11.5 0.1 collective-permute-start.1
  11.6 2.4 %local.3 = (f32[256,512]{1,0:T(8,128)S(1)}, f32[256,512]{1,0:T(8,128)S(1)}, f32[256,512]{1,0:T(8,128)S(1)}, f32[256,512]{1,0:T(8,128)S(1)}, f32[4,128,128]{2,1,0:T(8,128)S(1)}) custom-call(s32[6]{0:T(128)S(1)} %stack.39.info, bf16[256,2048]{1,0:T(8,128)(2,1)S(1)} %get-tuple-element.62.q.refs_0_, bf16[256,2048]{1,0:T(8,128)(2,1)S(1)} %get-tuple-element.63.k.refs_1_, ...), custom_call_target="tpu_custom_call" | custom-call | flops 1 | bytes 1 | tf_op jit(solution)/shard_map/local/pallas_call | solution.py:218
  14.0 0.9 %collective-permute-done.3.refs_4_ = f32[4,128,128]{2,1,0:T(8,128)S(1)} collective-permute-done((f32[4,128,128]{2,1,0:T(8,128)S(1)}, f32[4,128,128]{2,1,0:T(8,128)S(1)}, u32[]{:S(2)}, u32[]{:S(2)}) %collective-permute-start.3) | collective-permute-done | bytes 262176 | tf_op jit(solution)/shard_map/ppermute | solution.py:368
  15.0 1.9 %collective-permute-start.4 = (f32[4,128,128]{2,1,0:T(8,128)S(1)}, f32[4,128,128]{2,1,0:T(8,128)S(1)}, u32[]{:S(2)}, u32[]{:S(2)}) collective-permute-start(f32[4,128,128]{2,1,0:T(8,128)S(1)} %get-tuple-element.116), channel_id=1, source_target_pairs={{0,4},{1,5},{2,6},{3,7},{4,0},{5,1},{6,2},{7,3},{8,12},{9,13},{10,... | collective-permute-start | bytes 786440 | tf_op jit(solution)/shard_map/ppermute | solution.py:368
  16.9 1.6 %collective-permute-start.2 = (f32[4,128,128]{2,1,0:T(8,128)S(1)}, f32[4,128,128]{2,1,0:T(8,128)S(1)}, u32[]{:S(2)}, u32[]{:S(2)}) collective-permute-start(f32[4,128,128]{2,1,0:T(8,128)S(1)} %slice_add_fusion.2.refs_0_), channel_id=1, source_target_pairs={{0,2},{1,3},{2,0},{3,1},{4,6},{5,7},{6,4},{7,5},{8,10},{9,11},{10,... | collective-permute-start | bytes 786440 | tf_op jit(solution)/shard_map/ppermute | solution.py:368
  18.5 5.8 %local.2 = (f32[256,512]{1,0:T(8,128)S(1)}, f32[256,512]{1,0:T(8,128)S(1)}, f32[256,512]{1,0:T(8,128)S(1)}, f32[256,512]{1,0:T(8,128)S(1)}, f32[256,512]{1,0:T(8...) custom-call(s32[6]{0:T(128)S(1)} %stack.39.info, ...), custom_call_target="tpu_custom_call" | custom-call | flops 1 | bytes 1 | tf_op jit(solution)/shard_map/local/pallas_call | solution.py:218
  24.4 0.1 add_select_fusion
  24.5 0.1 collective-permute-start.5
  24.5 0.7 %prepare.2 = (f32[4,128,128]{2,1,0:T(8,128)S(1)}, f32[4,128,128]{2,1,0:T(8,128)S(1)}, f32[4,128,128]{2,1,0:T(8,128)S(1)}, f32[4,128,128]{2,1,0:T(8,128)S(1)}, f32[4,128,128]{2,1,0:T(8,128)S(1)}) custom-call(s32[6]{0:T(128)S(1)} %stack.39.info, f32[4,128,128]{2,1,0:T(8,128)S(1)} %collective-permute-done.4.refs_0_, f32[8,128,128]{2,1,0:T(8,128)S(1)} %own.1.refs_1_, ...), custom_call_target="tpu_custom_call" | custom-call | flops 1 | bytes 1 | tf_op jit(solution)/shard_map/prepare/pallas_call | solution.py:356
  25.3 0.6 %collective-permute-start.10 = (f32[4,128,128]{2,1,0:T(8,128)S(1)}, f32[4,128,128]{2,1,0:T(8,128)S(1)}, u32[]{:S(2)}, u32[]{:S(2)}) collective-permute-start(f32[4,128,128]{2,1,0:T(8,128)S(1)} %get-tuple-element.93), channel_id=1, source_target_pairs={{0,1},{1,0},{2,3},{3,2},{4,5},{5,4},{6,7},{7,6},{8,9},{9,8},{10,11... | collective-permute-start | bytes 786440 | tf_op jit(solution)/shard_map/ppermute | solution.py:368
  25.8 1.4 %collective-permute-start.9 = (f32[4,128,128]{2,1,0:T(8,128)S(1)}, f32[4,128,128]{2,1,0:T(8,128)S(1)}, u32[]{:S(2)}, u32[]{:S(2)}) collective-permute-start(f32[4,128,128]{2,1,0:T(8,128)S(1)} %get-tuple-element.78.refs_9_.refs_14_), channel_id=1, source_target_pairs={{0,2},{1,3},{2,0},{3,1},{4,6},{5,7},{6,4},{7,5},{8,10},{9,11},{10,... | collective-permute-start | bytes 786440 | tf_op jit(solution)/shard_map/ppermute | solution.py:368
  27.2 0.7 %prepare.3 = (f32[4,128,128]{2,1,0:T(8,128)S(1)}, f32[4,128,128]{2,1,0:T(8,128)S(1)}, f32[4,128,128]{2,1,0:T(8,128)S(1)}, f32[4,128,128]{2,1,0:T(8,128)S(1)}, f32[4,128,128]{2,1,0:T(8,128)S(1)}) custom-call(s32[6]{0:T(128)S(1)} %stack.39.info, f32[4,128,128]{2,1,0:T(8,128)S(1)} %collective-permute-done.4.refs_0_, f32[8,128,128]{2,1,0:T(8,128)S(1)} %own.1.refs_1_, ...), custom_call_target="tpu_custom_call" | custom-call | flops 1 | bytes 1 | tf_op jit(solution)/shard_map/prepare/pallas_call | solution.py:356
  27.9 5.0 %collective-permute-start.6 = (f32[4,128,128]{2,1,0:T(8,128)S(1)}, f32[4,128,128]{2,1,0:T(8,128)S(1)}, u32[]{:S(2)}, u32[]{:S(2)}) collective-permute-start(f32[4,128,128]{2,1,0:T(8,128)S(1)} %collective-permute-done.5), channel_id=1, source_target_pairs={{0,4},{1,5},{2,6},{3,7},{4,0},{5,1},{6,2},{7,3},{8,12},{9,13},{10,... | collective-permute-start | bytes 786440 | tf_op jit(solution)/shard_map/ppermute | solution.py:368
  32.9 1.9 %apply.4 = (bf16[256,2048]{1,0:T(8,128)(2,1)}, bf16[256,2048]{1,0:T(8,128)(2,1)}, bf16[256,2048]{1,0:T(8,128)(2,1)}, bf16[256,2048]{1,0:T(8,128)(2,1)}, f32[4,128,128]{2,1,0:T(8,128)S(1)}) custom-call(s32[6]{0:T(128)S(1)} %stack.39.info, bf16[256,2048]{1,0:T(8,128)(2,1)S(1)} %get-tuple-element.62.q.refs_0_, ...), custom_call_target="tpu_custom_call" | custom-call | flops 1 | bytes 1 | tf_op jit(solution)/shard_map/apply/pallas_call | solution.py:307
  34.9 0.1 collective-permute-start.11
  35.0 2.5 %collective-permute-done.6 = f32[4,128,128]{2,1,0:T(8,128)S(1)} collective-permute-done((f32[4,128,128]{2,1,0:T(8,128)S(1)}, f32[4,128,128]{2,1,0:T(8,128)S(1)}, u32[]{:S(2)}, u32[]{:S(2)}) %collective-permute-start.6) | collective-permute-done | bytes 262176 | tf_op jit(solution)/shard_map/ppermute | solution.py:368
  37.5 0.1 add_add_fusion.5
  37.5 0.1 collective-permute-start.8
  37.6 0.6 %collective-permute-start.7 = (f32[4,128,128]{2,1,0:T(8,128)S(1)}, f32[4,128,128]{2,1,0:T(8,128)S(1)}, u32[]{:S(2)}, u32[]{:S(2)}) collective-permute-start(f32[4,128,128]{2,1,0:T(8,128)S(1)} %get-tuple-element.118.refs_18_), channel_id=1, source_target_pairs={{0,2},{1,3},{2,0},{3,1},{4,6},{5,7},{6,4},{7,5},{8,10},{9,11},{10,... | collective-permute-start | bytes 786440 | tf_op jit(solution)/shard_map/ppermute | solution.py:368
  38.2 2.6 %apply.5 = (bf16[256,2048]{1,0:T(8,128)(2,1)}, bf16[256,2048]{1,0:T(8,128)(2,1)}, bf16[256,2048]{1,0:T(8,128)(2,1)}, bf16[256,2048]{1,0:T(8,128)(2,1)}, f32[4,128,128]{2,1,0:T(8,128)}) custom-call(s32[6]{0:T(128)S(1)} %stack.39.info, ...), custom_call_target="tpu_custom_call", output_to_operand_aliasing={{0}: (15, {}), {1}: (16, {}), {2}: (17, {}), {3}: (18, {})} | custom-call | flops 1 | bytes 1 | tf_op jit(solution)/shard_map/apply/pallas_call | solution.py:307
  40.9 1.9 %apply.6 = (bf16[256,2048]{1,0:T(8,128)(2,1)}, bf16[256,2048]{1,0:T(8,128)(2,1)}, bf16[256,2048]{1,0:T(8,128)(2,1)}, bf16[256,2048]{1,0:T(8,128)(2,1)}, f32[4,128,128]{2,1,0:T(8,128)S(1)}) custom-call(s32[6]{0:T(128)S(1)} %stack.39.info, ...), custom_call_target="tpu_custom_call", output_to_operand_aliasing={{0}: (15, {}), {1}: (16, {}), {2}: (17, {}), {3}: (18, {})} | custom-call | flops 1 | bytes 1 | tf_op jit(solution)/shard_map/apply/pallas_call | solution.py:307
  42.7 3.6 %collective-permute-done.7 = f32[4,128,128]{2,1,0:T(8,128)S(1)} collective-permute-done((f32[4,128,128]{2,1,0:T(8,128)S(1)}, f32[4,128,128]{2,1,0:T(8,128)S(1)}, u32[]{:S(2)}, u32[]{:S(2)}) %collective-permute-start.7) | collective-permute-done | bytes 262176 | tf_op jit(solution)/shard_map/ppermute | solution.py:368
  46.4 0.1 collective-permute-start.12
  46.5 1.5 %collective-permute-done.12.refs_13_ = f32[4,128,128]{2,1,0:T(8,128)S(1)} collective-permute-done((f32[4,128,128]{2,1,0:T(8,128)S(1)}, f32[4,128,128]{2,1,0:T(8,128)S(1)}, u32[]{:S(2)}, u32[]{:S(2)}) %collective-permute-start.12) | collective-permute-done | bytes 262176 | tf_op jit(solution)/shard_map/ppermute | solution.py:368
  48.0 2.6 %apply.7 = (bf16[256,2048]{1,0:T(8,128)(2,1)}, bf16[256,2048]{1,0:T(8,128)(2,1)}, bf16[256,2048]{1,0:T(8,128)(2,1)}, bf16[256,2048]{1,0:T(8,128)(2,1)}, f32[4,128,128]{2,1,0:T(8,128)}) custom-call(s32[6]{0:T(128)S(1)} %stack.39.info, ...), custom_call_target="tpu_custom_call", output_to_operand_aliasing={{0}: (15, {}), {1}: (16, {}), {2}: (17, {}), {3}: (18, {})} | custom-call | flops 1 | bytes 1 | tf_op jit(solution)/shard_map/apply/pallas_call | solution.py:307
  (13 shorter events, 0.3 us)
Async XLA Ops:
  3.2 2.1 %collective-permute-start = (f32[8,128,128]{2,1,0:T(8,128)S(1)}, f32[8,128,128]{2,1,0:T(8,128)S(1)}, u32[]{:S(2)}, u32[]{:S(2)}) collective-permute-start(f32[8,128,128]{2,1,0:T(8,128)S(1)} %get-tuple-element.61), channel_id=1, source_target_pairs={{0,1},{1,0},{2,3},{3,2},{4,5},{5,4},{6,7},{7,6},{8,9},{9,8},{10,11... | collective-permute-start | bytes 1572872 | tf_op jit(solution)/shard_map/ppermute | solution.py:368
  5.3 9.6 %collective-permute-start.3 = (f32[4,128,128]{2,1,0:T(8,128)S(1)}, f32[4,128,128]{2,1,0:T(8,128)S(1)}, u32[]{:S(2)}, u32[]{:S(2)}) collective-permute-start(f32[4,128,128]{2,1,0:T(8,128)S(1)} %slice_add_fusion.3.refs_0_), channel_id=1, source_target_pairs={{0,2},{1,3},{2,0},{3,1},{4,6},{5,7},{6,4},{7,5},{8,10},{9,11},{10,... | collective-permute-start | bytes 786440 | tf_op jit(solution)/shard_map/ppermute | solution.py:368
  11.5 5.4 %collective-permute-start.1 = (f32[8,128,128]{2,1,0:T(8,128)S(1)}, f32[8,128,128]{2,1,0:T(8,128)S(1)}, u32[]{:S(2)}, u32[]{:S(2)}) collective-permute-start(f32[8,128,128]{2,1,0:T(8,128)S(1)} %get-tuple-element.67), channel_id=1, source_target_pairs={{0,1},{1,0},{2,3},{3,2},{4,5},{5,4},{6,7},{7,6},{8,9},{9,8},{10,11... | collective-permute-start | bytes 1572872 | tf_op jit(solution)/shard_map/ppermute | solution.py:368
  15.0 9.4 %collective-permute-start.4 = (f32[4,128,128]{2,1,0:T(8,128)S(1)}, f32[4,128,128]{2,1,0:T(8,128)S(1)}, u32[]{:S(2)}, u32[]{:S(2)}) collective-permute-start(f32[4,128,128]{2,1,0:T(8,128)S(1)} %get-tuple-element.116), channel_id=1, source_target_pairs={{0,4},{1,5},{2,6},{3,7},{4,0},{5,1},{6,2},{7,3},{8,12},{9,13},{10,... | collective-permute-start | bytes 786440 | tf_op jit(solution)/shard_map/ppermute | solution.py:368
  16.9 7.5 %collective-permute-start.2 = (f32[4,128,128]{2,1,0:T(8,128)S(1)}, f32[4,128,128]{2,1,0:T(8,128)S(1)}, u32[]{:S(2)}, u32[]{:S(2)}) collective-permute-start(f32[4,128,128]{2,1,0:T(8,128)S(1)} %slice_add_fusion.2.refs_0_), channel_id=1, source_target_pairs={{0,2},{1,3},{2,0},{3,1},{4,6},{5,7},{6,4},{7,5},{8,10},{9,11},{10,... | collective-permute-start | bytes 786440 | tf_op jit(solution)/shard_map/ppermute | solution.py:368
  24.5 3.5 %collective-permute-start.5 = (f32[4,128,128]{2,1,0:T(8,128)S(1)}, f32[4,128,128]{2,1,0:T(8,128)S(1)}, u32[]{:S(2)}, u32[]{:S(2)}) collective-permute-start(f32[4,128,128]{2,1,0:T(8,128)S(1)} %get-tuple-element.114), channel_id=1, source_target_pairs={{4,8},{5,9},{6,10},{7,11},{8,4},{9,5},{10,6},{11,7},{0,1},{1,0},{2... | collective-permute-start | bytes 786440 | tf_op jit(solution)/shard_map/ppermute | solution.py:368
  25.3 7.6 %collective-permute-start.10 = (f32[4,128,128]{2,1,0:T(8,128)S(1)}, f32[4,128,128]{2,1,0:T(8,128)S(1)}, u32[]{:S(2)}, u32[]{:S(2)}) collective-permute-start(f32[4,128,128]{2,1,0:T(8,128)S(1)} %get-tuple-element.93), channel_id=1, source_target_pairs={{0,1},{1,0},{2,3},{3,2},{4,5},{5,4},{6,7},{7,6},{8,9},{9,8},{10,11... | collective-permute-start | bytes 786440 | tf_op jit(solution)/shard_map/ppermute | solution.py:368
  25.8 9.0 %collective-permute-start.9 = (f32[4,128,128]{2,1,0:T(8,128)S(1)}, f32[4,128,128]{2,1,0:T(8,128)S(1)}, u32[]{:S(2)}, u32[]{:S(2)}) collective-permute-start(f32[4,128,128]{2,1,0:T(8,128)S(1)} %get-tuple-element.78.refs_9_.refs_14_), channel_id=1, source_target_pairs={{0,2},{1,3},{2,0},{3,1},{4,6},{5,7},{6,4},{7,5},{8,10},{9,11},{10,... | collective-permute-start | bytes 786440 | tf_op jit(solution)/shard_map/ppermute | solution.py:368
  27.9 9.5 %collective-permute-start.6 = (f32[4,128,128]{2,1,0:T(8,128)S(1)}, f32[4,128,128]{2,1,0:T(8,128)S(1)}, u32[]{:S(2)}, u32[]{:S(2)}) collective-permute-start(f32[4,128,128]{2,1,0:T(8,128)S(1)} %collective-permute-done.5), channel_id=1, source_target_pairs={{0,4},{1,5},{2,6},{3,7},{4,0},{5,1},{6,2},{7,3},{8,12},{9,13},{10,... | collective-permute-start | bytes 786440 | tf_op jit(solution)/shard_map/ppermute | solution.py:368
  34.9 3.4 %collective-permute-start.11 = (f32[4,128,128]{2,1,0:T(8,128)S(1)}, f32[4,128,128]{2,1,0:T(8,128)S(1)}, u32[]{:S(2)}, u32[]{:S(2)}) collective-permute-start(f32[4,128,128]{2,1,0:T(8,128)S(1)} %get-tuple-element.123), channel_id=1, source_target_pairs={{0,1},{1,0},{2,3},{3,2},{4,5},{5,4},{6,7},{7,6},{8,9},{9,8},{10,11... | collective-permute-start | bytes 786440 | tf_op jit(solution)/shard_map/ppermute | solution.py:368
  37.5 3.3 %collective-permute-start.8 = (f32[4,128,128]{2,1,0:T(8,128)S(1)}, f32[4,128,128]{2,1,0:T(8,128)S(1)}, u32[]{:S(2)}, u32[]{:S(2)}) collective-permute-start(f32[4,128,128]{2,1,0:T(8,128)S(1)} %get-tuple-element.120), channel_id=1, source_target_pairs={{0,1},{1,0},{2,3},{3,2},{4,5},{5,4},{6,7},{7,6},{8,9},{9,8},{10,11... | collective-permute-start | bytes 786440 | tf_op jit(solution)/shard_map/ppermute | solution.py:368
  37.6 8.7 %collective-permute-start.7 = (f32[4,128,128]{2,1,0:T(8,128)S(1)}, f32[4,128,128]{2,1,0:T(8,128)S(1)}, u32[]{:S(2)}, u32[]{:S(2)}) collective-permute-start(f32[4,128,128]{2,1,0:T(8,128)S(1)} %get-tuple-element.118.refs_18_), channel_id=1, source_target_pairs={{0,2},{1,3},{2,0},{3,1},{4,6},{5,7},{6,4},{7,5},{8,10},{9,11},{10,... | collective-permute-start | bytes 786440 | tf_op jit(solution)/shard_map/ppermute | solution.py:368
  46.4 1.6 %collective-permute-start.12 = (f32[4,128,128]{2,1,0:T(8,128)S(1)}, f32[4,128,128]{2,1,0:T(8,128)S(1)}, u32[]{:S(2)}, u32[]{:S(2)}) collective-permute-start(f32[4,128,128]{2,1,0:T(8,128)S(1)} %get-tuple-element.121), channel_id=1, source_target_pairs={{0,1},{1,0},{2,3},{3,2},{4,5},{5,4},{6,7},{7,6},{8,9},{9,8},{10,11... | collective-permute-start | bytes 786440 | tf_op jit(solution)/shard_map/ppermute | solution.py:368

commit v5 on v4

--- a/solution.py
+++ b/solution.py
@@ -228,12 +228,14 @@
     return {kind: parts[4 * n : 4 * n + 4] for n, kind in enumerate(kinds)}, flag
 
 
-def apply_kernel(early, kinds, quarter, n_filled, n_after, info, *refs):
+def apply_kernel(early, kinds, pieces, quarter, n_filled, n_after, info, *refs):
     q, k, v, d = refs[:4]
     refs = refs[4:]
     partials = [refs[4 * n : 4 * n + 4] for n in range(len(kinds))]
     refs = refs[4 * len(kinds) :]
-    state_refs, refs = refs[: len(kinds)], refs[len(kinds) + n_filled + n_after :]
+    n_states = len(kinds) * pieces
+    state_refs, refs = refs[:n_states], refs[n_states + n_filled + n_after :]
+    each = quarter // pieces
     o_hbm, dq_hbm, dk_hbm, dv_hbm, zero, one, other, sems = refs
     zero[...] = jnp.zeros_like(zero)
     count = q.shape[0]
@@ -262,7 +264,7 @@
                 at = head * DH
                 here = slice((step * two + i) * DH, (step * two + i + 1) * DH)
                 one[:, here], other[:, here] = products(
-                    cols, partials[n], slice(at, at + DH), state_refs[n][head].astype(BF16)
+                    cols, partials[n], slice(at, at + DH), state_refs[n * pieces + head // each][head % each].astype(BF16)
                 )
             for copy in copies(step, a, b):
                 copy.start()
@@ -302,16 +304,16 @@
     quarter = width // DH // 4
     filled = () if outs is None else tuple(outs)
     partials = [x for kind in kinds for x in partials[kind]]
-    first_out = 5 + len(partials) + len(kinds)
+    first_out = 5 + len(partials) + len(arrays)
     columns = len(kinds) * quarter * DH
     return pl.pallas_call(
         functools.partial(
-            apply_kernel, early, kinds, quarter, len(filled), len(after)
+            apply_kernel, early, kinds, len(arrays) // len(kinds), quarter, len(filled), len(after)
         ),
         out_shape=[jax.ShapeDtypeStruct((count, width), BF16)] * 4
         + [jax.ShapeDtypeStruct((quarter, DH, DH), F32)],
         in_specs=[IN_SMEM]
-        + [IN_VMEM] * (4 + len(partials) + len(kinds))
+        + [IN_VMEM] * (4 + len(partials) + len(arrays))
         + [IN_HBM] * len(filled)
         + [IN_VMEM] * len(after),
         out_specs=[IN_HBM] * 4 + [IN_VMEM],
@@ -402,6 +404,7 @@
     far_args = tuple(pltpu.with_memory_space_constraint(x, pltpu.HBM) for x in args)
 
     quarter = heads // 4
+    cuts = slice(0, quarter // 2), slice(quarter // 2, quarter)
 
     def halves(own, got):
         return own[:quarter] + got[:quarter], own[quarter:] + got[quarter:]
@@ -416,8 +419,9 @@
     part_a, zero = local_part(info, args, kinds[:1], 0.0, (s_own,))
     s_got = send(s_sib, core_swap)
     s_keep, s_give = halves(s_own, s_got)
+    f_total = f_keep + f_other + zero
+    s_give, f_total = lax.optimization_barrier((s_give, f_total))
     s_other = send(s_give, row_swap)
-    f_total = f_keep + f_other + zero
     f = f_own, f_got, f_keep, f_other
     s = s_own, s_got, s_keep, s_other
     part_b, inside = local_part(info, args, kinds[1:], 1.0, (s_give,))
@@ -445,9 +449,10 @@
     *outs, zero = finish(True, kept_heads, t_kept, None, (across, late[0]))
     t_rest = t_other + rest_mine + zero, send(t_other + rest_theirs, core_swap)
 
-    across, mine, theirs = (coming + x for x in late[:3])
+    across = coming + late[0]
     u_other = send(across, row_swap)
-    u_kept = mine, send(theirs, core_swap)
+    u_kept = [coming[cut] + late[1][cut] for cut in cuts]
+    u_kept += [send(coming[cut] + late[2][cut], core_swap) for cut in cuts]
     *outs, _ = finish(True, other_heads, t_rest, outs, (across,))
     *outs, zero = finish(False, kept_heads, u_kept, outs)
     u_rest = u_other + late[3] + zero, send(u_other + late[4], core_swap)

time: 50.7 us -> 48.3 us (0.953)
  waiting for transfers between devices: 9.07 us -> 6.17 us
    ppermute x13 -> x14, waiting for transfers between devices: 9.07 us -> 6.17 us  [send(): return lax.ppermute(array, 'seq', pairs)]
    ppermute x13 -> x14, starting transfers between devices: 14.8 us -> 15.3 us  [send(): return lax.ppermute(array, 'seq', pairs)]
  transfers between devices with their start and end apart: 13 -> 14, of which waited for: 5 -> 5; matrix products, arithmetic and copies ran while one was open for 0% -> 1% of each run, Pallas kernels for 40% -> 42%
where the time goes in v5:
time: 48.3 us; the launch traced here: 48.2 us
  Pallas kernels  25.3 us (52%)
  starting transfers between devices  15.3 us (32%)
  waiting for transfers between devices  6.17 us (13%)
  between operations  0.9 us (2%)
    ppermute x14, starting transfers between devices, send(): return lax.ppermute(array, 'seq', pairs)  15.3 us
    pallas_call x4, Pallas kernels, apply_states(): pl.pallas_call(functools.partial(apply_kernel, early, kinds, len(arrays)...  8.92 us
    pallas_call x2, Pallas kernels, local_part(): pl.pallas_call(functools.partial(local_kernel, kinds, quarter, mark, len(...  8.23 us
    ppermute x14, waiting for transfers between devices, send(): return lax.ppermute(array, 'seq', pairs)  6.17 us
    pallas_call x1, Pallas kernels, second_states(): pl.pallas_call(functools.partial(second_kernel, heads // 4, rows, len(aft...  3.21 us
    pallas_call x1, Pallas kernels, first_state(): pl.pallas_call(functools.partial(first_kernel, heads // 4, rows), out_sha...  2.46 us
    pallas_call x2, Pallas kernels, prepare(): pl.pallas_call(functools.partial(prepare_kernel, early, len(after)), out_...  1.44 us
    pallas_call x1, Pallas kernels, own_state(): pl.pallas_call(functools.partial(own_kernel, heads // 4), out_shape=jax.S...  1.02 us
  transfers between devices with their start and end apart: 14, of which 5 were waited for; matrix products, arithmetic and copies ran while one was open for 1% of the time, Pallas kernels for 42%

profile of v5, /device:TPU:0, one launch (start us, length us, event | category | flops | bytes accessed | tf_op | source)
XLA Modules:
  0.0 48.2 jit_solution(7912262691746200268)
XLA Ops:
  0.7 0.1 stack.39.info
  0.8 2.5 %first.1 = (f32[8,128,128]{2,1,0:T(8,128)S(1)}, bf16[256,2048]{1,0:T(8,128)(2,1)S(1)}, bf16[256,2048]{1,0:T(8,128)(2,1)S(1)}) custom-call(s32[6]{0:T(128)S(1)} %stack.39.info, bf16[256,2048]{1,0:T(8,128)(2,1)} %q.3, bf16[256,2048]{1,0:T(8,128)(2,1)} %k.3, bf16[256,2048]{1,0:T(8,128)(2,1)} %v.3, bf16[256,2048]{1,0:T(8,128)(2,1)} %d.3), custom_call_target="tpu_custom_call" | custom-call | flops 1 | bytes 1 | tf_op jit(solution)/shard_map/first/pallas_call | solution.py:104
  3.2 0.5 %collective-permute-start = (f32[8,128,128]{2,1,0:T(8,128)S(1)}, f32[8,128,128]{2,1,0:T(8,128)S(1)}, u32[]{:S(2)}, u32[]{:S(2)}) collective-permute-start(f32[8,128,128]{2,1,0:T(8,128)S(1)} %get-tuple-element.63), channel_id=1, source_target_pairs={{0,1},{1,0},{2,3},{3,2},{4,5},{5,4},{6,7},{7,6},{8,9},{9,8},{10,11... | collective-permute-start | bytes 1572872 | tf_op jit(solution)/shard_map/ppermute | solution.py:370
  3.8 1.0 %own.1.refs_1_ = f32[8,128,128]{2,1,0:T(8,128)S(1)} custom-call(s32[6]{0:T(128)S(1)} %stack.39.info, bf16[256,2048]{1,0:T(8,128)(2,1)S(1)} %get-tuple-element.61.left, bf16[256,2048]{1,0:T(8,128)(2,1)S(1)} %get-tuple-element.62.right), custom_call_target="tpu_custom_call" | custom-call | flops 1 | bytes 1 | tf_op jit(solution)/shard_map/own/pallas_call | solution.py:124
  4.8 0.5 %collective-permute-done.refs_2_ = f32[8,128,128]{2,1,0:T(8,128)S(1)} collective-permute-done((f32[8,128,128]{2,1,0:T(8,128)S(1)}, f32[8,128,128]{2,1,0:T(8,128)S(1)}, u32[]{:S(2)}, u32[]{:S(2)}) %collective-permute-start) | collective-permute-done | bytes 524320 | tf_op jit(solution)/shard_map/ppermute | solution.py:370
  5.3 3.0 %collective-permute-start.2 = (f32[4,128,128]{2,1,0:T(8,128)S(1)}, f32[4,128,128]{2,1,0:T(8,128)S(1)}, u32[]{:S(2)}, u32[]{:S(2)}) collective-permute-start(f32[4,128,128]{2,1,0:T(8,128)S(1)} %slice_add_fusion.3.refs_0_), channel_id=1, source_target_pairs={{0,2},{1,3},{2,0},{3,1},{4,6},{5,7},{6,4},{7,5},{8,10},{9,11},{10,... | collective-permute-start | bytes 786440 | tf_op jit(solution)/shard_map/ppermute | solution.py:370
  8.3 3.2 %second.1 = (f32[8,128,128]{2,1,0:T(8,128)S(1)}, f32[8,128,128]{2,1,0:T(8,128)S(1)}, bf16[256,2048]{1,0:T(8,128)(2,1)S(1)}, bf16[256,2048]{1,0:T(8,128)(2,1)S(1)...) custom-call(s32[6]{0:T(128)S(1)} %stack.39.info, bf16[256,2048]{1,0:T(8,128)(2,1)} %q.3, ...), custom_call_target="tpu_custom_call" | custom-call | flops 1 | bytes 1 | tf_op jit(solution)/shard_map/second/pallas_call | solution.py:171
  11.5 0.1 collective-permute-start.1
  11.6 2.4 %local.2 = (f32[256,512]{1,0:T(8,128)S(1)}, f32[256,512]{1,0:T(8,128)S(1)}, f32[256,512]{1,0:T(8,128)S(1)}, f32[256,512]{1,0:T(8,128)S(1)}, f32[4,128,128]{2,1,0:T(8,128)S(1)}) custom-call(s32[6]{0:T(128)S(1)} %stack.39.info, bf16[256,2048]{1,0:T(8,128)(2,1)S(1)} %get-tuple-element.64.q.refs_0_, bf16[256,2048]{1,0:T(8,128)(2,1)S(1)} %get-tuple-element.65.k.refs_1_, ...), custom_call_target="tpu_custom_call" | custom-call | flops 1 | bytes 1 | tf_op jit(solution)/shard_map/local/pallas_call | solution.py:218
  14.0 0.9 %collective-permute-done.2.refs_4_ = f32[4,128,128]{2,1,0:T(8,128)S(1)} collective-permute-done((f32[4,128,128]{2,1,0:T(8,128)S(1)}, f32[4,128,128]{2,1,0:T(8,128)S(1)}, u32[]{:S(2)}, u32[]{:S(2)}) %collective-permute-start.2) | collective-permute-done | bytes 262176 | tf_op jit(solution)/shard_map/ppermute | solution.py:370
  15.0 1.9 %collective-permute-start.4 = (f32[4,128,128]{2,1,0:T(8,128)S(1)}, f32[4,128,128]{2,1,0:T(8,128)S(1)}, u32[]{:S(2)}, u32[]{:S(2)}) collective-permute-start(f32[4,128,128]{2,1,0:T(8,128)S(1)} %get-tuple-element.81), channel_id=1, source_target_pairs={{0,4},{1,5},{2,6},{3,7},{4,0},{5,1},{6,2},{7,3},{8,12},{9,13},{10,... | collective-permute-start | bytes 786440 | tf_op jit(solution)/shard_map/ppermute | solution.py:370
  16.9 1.5 %collective-permute-start.3 = (f32[4,128,128]{2,1,0:T(8,128)S(1)}, f32[4,128,128]{2,1,0:T(8,128)S(1)}, u32[]{:S(2)}, u32[]{:S(2)}) collective-permute-start(f32[4,128,128]{2,1,0:T(8,128)S(1)} %slice_add_fusion.2.refs_0_), channel_id=1, source_target_pairs={{0,2},{1,3},{2,0},{3,1},{4,6},{5,7},{6,4},{7,5},{8,10},{9,11},{10,... | collective-permute-start | bytes 786440 | tf_op jit(solution)/shard_map/ppermute | solution.py:370
  18.4 5.8 %local.3 = (f32[256,512]{1,0:T(8,128)S(1)}, f32[256,512]{1,0:T(8,128)S(1)}, f32[256,512]{1,0:T(8,128)S(1)}, f32[256,512]{1,0:T(8,128)S(1)}, f32[256,512]{1,0:T(8...) custom-call(s32[6]{0:T(128)S(1)} %stack.39.info, ...), custom_call_target="tpu_custom_call" | custom-call | flops 1 | bytes 1 | tf_op jit(solution)/shard_map/local/pallas_call | solution.py:218
  24.3 0.1 add_select_fusion
  24.4 0.1 collective-permute-start.5
  24.5 0.7 %prepare.2 = (f32[4,128,128]{2,1,0:T(8,128)S(1)}, f32[4,128,128]{2,1,0:T(8,128)S(1)}, f32[4,128,128]{2,1,0:T(8,128)S(1)}, f32[4,128,128]{2,1,0:T(8,128)S(1)}, f32[4,128,128]{2,1,0:T(8,128)S(1)}) custom-call(s32[6]{0:T(128)S(1)} %stack.39.info, f32[4,128,128]{2,1,0:T(8,128)S(1)} %collective-permute-done.4.refs_0_, f32[8,128,128]{2,1,0:T(8,128)S(1)} %own.1.refs_1_, ...), custom_call_target="tpu_custom_call" | custom-call | flops 1 | bytes 1 | tf_op jit(solution)/shard_map/prepare/pallas_call | solution.py:358
  25.2 0.6 %collective-permute-start.11 = (f32[4,128,128]{2,1,0:T(8,128)S(1)}, f32[4,128,128]{2,1,0:T(8,128)S(1)}, u32[]{:S(2)}, u32[]{:S(2)}) collective-permute-start(f32[4,128,128]{2,1,0:T(8,128)S(1)} %get-tuple-element.97), channel_id=1, source_target_pairs={{0,1},{1,0},{2,3},{3,2},{4,5},{5,4},{6,7},{7,6},{8,9},{9,8},{10,11... | collective-permute-start | bytes 786440 | tf_op jit(solution)/shard_map/ppermute | solution.py:370
  25.8 1.4 %collective-permute-start.10 = (f32[4,128,128]{2,1,0:T(8,128)S(1)}, f32[4,128,128]{2,1,0:T(8,128)S(1)}, u32[]{:S(2)}, u32[]{:S(2)}) collective-permute-start(f32[4,128,128]{2,1,0:T(8,128)S(1)} %get-tuple-element.82.refs_9_.refs_14_), channel_id=1, source_target_pairs={{0,2},{1,3},{2,0},{3,1},{4,6},{5,7},{6,4},{7,5},{8,10},{9,11},{10,... | collective-permute-start | bytes 786440 | tf_op jit(solution)/shard_map/ppermute | solution.py:370
  27.1 0.7 %prepare.3 = (f32[4,128,128]{2,1,0:T(8,128)S(1)}, f32[4,128,128]{2,1,0:T(8,128)S(1)}, f32[4,128,128]{2,1,0:T(8,128)S(1)}, f32[4,128,128]{2,1,0:T(8,128)S(1)}, f32[4,128,128]{2,1,0:T(8,128)S(1)}) custom-call(s32[6]{0:T(128)S(1)} %stack.39.info, f32[4,128,128]{2,1,0:T(8,128)S(1)} %collective-permute-done.4.refs_0_, f32[8,128,128]{2,1,0:T(8,128)S(1)} %own.1.refs_1_, ...), custom_call_target="tpu_custom_call" | custom-call | flops 1 | bytes 1 | tf_op jit(solution)/shard_map/prepare/pallas_call | solution.py:358
  27.9 5.0 %collective-permute-start.6 = (f32[4,128,128]{2,1,0:T(8,128)S(1)}, f32[4,128,128]{2,1,0:T(8,128)S(1)}, u32[]{:S(2)}, u32[]{:S(2)}) collective-permute-start(f32[4,128,128]{2,1,0:T(8,128)S(1)} %collective-permute-done.5), channel_id=1, source_target_pairs={{0,4},{1,5},{2,6},{3,7},{4,0},{5,1},{6,2},{7,3},{8,12},{9,13},{10,... | collective-permute-start | bytes 786440 | tf_op jit(solution)/shard_map/ppermute | solution.py:370
  32.8 1.9 %apply.4 = (bf16[256,2048]{1,0:T(8,128)(2,1)}, bf16[256,2048]{1,0:T(8,128)(2,1)}, bf16[256,2048]{1,0:T(8,128)(2,1)}, bf16[256,2048]{1,0:T(8,128)(2,1)}, f32[4,128,128]{2,1,0:T(8,128)S(1)}) custom-call(s32[6]{0:T(128)S(1)} %stack.39.info, bf16[256,2048]{1,0:T(8,128)(2,1)S(1)} %get-tuple-element.64.q.refs_0_, ...), custom_call_target="tpu_custom_call" | custom-call | flops 1 | bytes 1 | tf_op jit(solution)/shard_map/apply/pallas_call | solution.py:309
  34.8 0.1 fusion.2
  34.8 0.1 collective-permute-start.12
  34.9 2.5 %collective-permute-done.6 = f32[4,128,128]{2,1,0:T(8,128)S(1)} collective-permute-done((f32[4,128,128]{2,1,0:T(8,128)S(1)}, f32[4,128,128]{2,1,0:T(8,128)S(1)}, u32[]{:S(2)}, u32[]{:S(2)}) %collective-permute-start.6) | collective-permute-done | bytes 262176 | tf_op jit(solution)/shard_map/ppermute | solution.py:370
  37.5 0.6 %collective-permute-start.7 = (f32[4,128,128]{2,1,0:T(8,128)S(1)}, f32[4,128,128]{2,1,0:T(8,128)S(1)}, u32[]{:S(2)}, u32[]{:S(2)}) collective-permute-start(f32[4,128,128]{2,1,0:T(8,128)S(1)} %get-tuple-element.118.refs_18_), channel_id=1, source_target_pairs={{0,2},{1,3},{2,0},{3,1},{4,6},{5,7},{6,4},{7,5},{8,10},{9,11},{10,... | collective-permute-start | bytes 786440 | tf_op jit(solution)/shard_map/ppermute | solution.py:370
  38.1 0.1 collective-permute-start.9
  38.2 0.5 %collective-permute-start.8 = (f32[2,128,128]{2,1,0:T(8,128)S(1)}, f32[2,128,128]{2,1,0:T(8,128)S(1)}, u32[]{:S(2)}, u32[]{:S(2)}) collective-permute-start(f32[2,128,128]{2,1,0:T(8,128)S(1)} %get-tuple-element.125), channel_id=1, source_target_pairs={{0,1},{1,0},{2,3},{3,2},{4,5},{5,4},{6,7},{7,6},{8,9},{9,8},{10,11... | collective-permute-start | bytes 393224 | tf_op jit(solution)/shard_map/ppermute | solution.py:370
  38.7 2.6 %apply.5 = (bf16[256,2048]{1,0:T(8,128)(2,1)}, bf16[256,2048]{1,0:T(8,128)(2,1)}, bf16[256,2048]{1,0:T(8,128)(2,1)}, bf16[256,2048]{1,0:T(8,128)(2,1)}, f32[4,128,128]{2,1,0:T(8,128)}) custom-call(s32[6]{0:T(128)S(1)} %stack.39.info, ...), custom_call_target="tpu_custom_call", output_to_operand_aliasing={{0}: (15, {}), {1}: (16, {}), {2}: (17, {}), {3}: (18, {})} | custom-call | flops 1 | bytes 1 | tf_op jit(solution)/shard_map/apply/pallas_call | solution.py:309
  41.4 1.8 %apply.6 = (bf16[256,2048]{1,0:T(8,128)(2,1)}, bf16[256,2048]{1,0:T(8,128)(2,1)}, bf16[256,2048]{1,0:T(8,128)(2,1)}, bf16[256,2048]{1,0:T(8,128)(2,1)}, f32[4,128,128]{2,1,0:T(8,128)S(1)}) custom-call(s32[6]{0:T(128)S(1)} %stack.39.info, ...), custom_call_target="tpu_custom_call", output_to_operand_aliasing={{0}: (17, {}), {1}: (18, {}), {2}: (19, {}), {3}: (20, {})} | custom-call | flops 1 | bytes 1 | tf_op jit(solution)/shard_map/apply/pallas_call | solution.py:309
  43.2 0.7 %collective-permute-done.7 = f32[4,128,128]{2,1,0:T(8,128)S(1)} collective-permute-done((f32[4,128,128]{2,1,0:T(8,128)S(1)}, f32[4,128,128]{2,1,0:T(8,128)S(1)}, u32[]{:S(2)}, u32[]{:S(2)}) %collective-permute-start.7) | collective-permute-done | bytes 262176 | tf_op jit(solution)/shard_map/ppermute | solution.py:370
  44.1 1.5 %collective-permute-done.13.refs_13_ = f32[4,128,128]{2,1,0:T(8,128)S(1)} collective-permute-done((f32[4,128,128]{2,1,0:T(8,128)S(1)}, f32[4,128,128]{2,1,0:T(8,128)S(1)}, u32[]{:S(2)}, u32[]{:S(2)}) %collective-permute-start.13) | collective-permute-done | bytes 262176 | tf_op jit(solution)/shard_map/ppermute | solution.py:370
  45.6 2.6 %apply.7 = (bf16[256,2048]{1,0:T(8,128)(2,1)}, bf16[256,2048]{1,0:T(8,128)(2,1)}, bf16[256,2048]{1,0:T(8,128)(2,1)}, bf16[256,2048]{1,0:T(8,128)(2,1)}, f32[4,128,128]{2,1,0:T(8,128)}) custom-call(s32[6]{0:T(128)S(1)} %stack.39.info, ...), custom_call_target="tpu_custom_call", output_to_operand_aliasing={{0}: (15, {}), {1}: (16, {}), {2}: (17, {}), {3}: (18, {})} | custom-call | flops 1 | bytes 1 | tf_op jit(solution)/shard_map/apply/pallas_call | solution.py:309
  (16 shorter events, 0.4 us)
Async XLA Ops:
  3.2 2.1 %collective-permute-start = (f32[8,128,128]{2,1,0:T(8,128)S(1)}, f32[8,128,128]{2,1,0:T(8,128)S(1)}, u32[]{:S(2)}, u32[]{:S(2)}) collective-permute-start(f32[8,128,128]{2,1,0:T(8,128)S(1)} %get-tuple-element.63), channel_id=1, source_target_pairs={{0,1},{1,0},{2,3},{3,2},{4,5},{5,4},{6,7},{7,6},{8,9},{9,8},{10,11... | collective-permute-start | bytes 1572872 | tf_op jit(solution)/shard_map/ppermute | solution.py:370
  5.3 9.6 %collective-permute-start.2 = (f32[4,128,128]{2,1,0:T(8,128)S(1)}, f32[4,128,128]{2,1,0:T(8,128)S(1)}, u32[]{:S(2)}, u32[]{:S(2)}) collective-permute-start(f32[4,128,128]{2,1,0:T(8,128)S(1)} %slice_add_fusion.3.refs_0_), channel_id=1, source_target_pairs={{0,2},{1,3},{2,0},{3,1},{4,6},{5,7},{6,4},{7,5},{8,10},{9,11},{10,... | collective-permute-start | bytes 786440 | tf_op jit(solution)/shard_map/ppermute | solution.py:370
  11.5 3.5 %collective-permute-start.1 = (f32[8,128,128]{2,1,0:T(8,128)S(1)}, f32[8,128,128]{2,1,0:T(8,128)S(1)}, u32[]{:S(2)}, u32[]{:S(2)}) collective-permute-start(f32[8,128,128]{2,1,0:T(8,128)S(1)} %get-tuple-element.69), channel_id=1, source_target_pairs={{0,1},{1,0},{2,3},{3,2},{4,5},{5,4},{6,7},{7,6},{8,9},{9,8},{10,11... | collective-permute-start | bytes 1572872 | tf_op jit(solution)/shard_map/ppermute | solution.py:370
  15.0 9.3 %collective-permute-start.4 = (f32[4,128,128]{2,1,0:T(8,128)S(1)}, f32[4,128,128]{2,1,0:T(8,128)S(1)}, u32[]{:S(2)}, u32[]{:S(2)}) collective-permute-start(f32[4,128,128]{2,1,0:T(8,128)S(1)} %get-tuple-element.81), channel_id=1, source_target_pairs={{0,4},{1,5},{2,6},{3,7},{4,0},{5,1},{6,2},{7,3},{8,12},{9,13},{10,... | collective-permute-start | bytes 786440 | tf_op jit(solution)/shard_map/ppermute | solution.py:370
  16.9 7.4 %collective-permute-start.3 = (f32[4,128,128]{2,1,0:T(8,128)S(1)}, f32[4,128,128]{2,1,0:T(8,128)S(1)}, u32[]{:S(2)}, u32[]{:S(2)}) collective-permute-start(f32[4,128,128]{2,1,0:T(8,128)S(1)} %slice_add_fusion.2.refs_0_), channel_id=1, source_target_pairs={{0,2},{1,3},{2,0},{3,1},{4,6},{5,7},{6,4},{7,5},{8,10},{9,11},{10,... | collective-permute-start | bytes 786440 | tf_op jit(solution)/shard_map/ppermute | solution.py:370
  24.4 3.5 %collective-permute-start.5 = (f32[4,128,128]{2,1,0:T(8,128)S(1)}, f32[4,128,128]{2,1,0:T(8,128)S(1)}, u32[]{:S(2)}, u32[]{:S(2)}) collective-permute-start(f32[4,128,128]{2,1,0:T(8,128)S(1)} %get-tuple-element.120), channel_id=1, source_target_pairs={{4,8},{5,9},{6,10},{7,11},{8,4},{9,5},{10,6},{11,7},{0,1},{1,0},{2... | collective-permute-start | bytes 786440 | tf_op jit(solution)/shard_map/ppermute | solution.py:370
  25.2 7.6 %collective-permute-start.11 = (f32[4,128,128]{2,1,0:T(8,128)S(1)}, f32[4,128,128]{2,1,0:T(8,128)S(1)}, u32[]{:S(2)}, u32[]{:S(2)}) collective-permute-start(f32[4,128,128]{2,1,0:T(8,128)S(1)} %get-tuple-element.97), channel_id=1, source_target_pairs={{0,1},{1,0},{2,3},{3,2},{4,5},{5,4},{6,7},{7,6},{8,9},{9,8},{10,11... | collective-permute-start | bytes 786440 | tf_op jit(solution)/shard_map/ppermute | solution.py:370
  25.8 9.0 %collective-permute-start.10 = (f32[4,128,128]{2,1,0:T(8,128)S(1)}, f32[4,128,128]{2,1,0:T(8,128)S(1)}, u32[]{:S(2)}, u32[]{:S(2)}) collective-permute-start(f32[4,128,128]{2,1,0:T(8,128)S(1)} %get-tuple-element.82.refs_9_.refs_14_), channel_id=1, source_target_pairs={{0,2},{1,3},{2,0},{3,1},{4,6},{5,7},{6,4},{7,5},{8,10},{9,11},{10,... | collective-permute-start | bytes 786440 | tf_op jit(solution)/shard_map/ppermute | solution.py:370
  27.9 9.6 %collective-permute-start.6 = (f32[4,128,128]{2,1,0:T(8,128)S(1)}, f32[4,128,128]{2,1,0:T(8,128)S(1)}, u32[]{:S(2)}, u32[]{:S(2)}) collective-permute-start(f32[4,128,128]{2,1,0:T(8,128)S(1)} %collective-permute-done.5), channel_id=1, source_target_pairs={{0,4},{1,5},{2,6},{3,7},{4,0},{5,1},{6,2},{7,3},{8,12},{9,13},{10,... | collective-permute-start | bytes 786440 | tf_op jit(solution)/shard_map/ppermute | solution.py:370
  34.8 3.9 %collective-permute-start.12 = (f32[4,128,128]{2,1,0:T(8,128)S(1)}, f32[4,128,128]{2,1,0:T(8,128)S(1)}, u32[]{:S(2)}, u32[]{:S(2)}) collective-permute-start(f32[4,128,128]{2,1,0:T(8,128)S(1)} %get-tuple-element.130), channel_id=1, source_target_pairs={{0,1},{1,0},{2,3},{3,2},{4,5},{5,4},{6,7},{7,6},{8,9},{9,8},{10,11... | collective-permute-start | bytes 786440 | tf_op jit(solution)/shard_map/ppermute | solution.py:370
  37.5 6.4 %collective-permute-start.7 = (f32[4,128,128]{2,1,0:T(8,128)S(1)}, f32[4,128,128]{2,1,0:T(8,128)S(1)}, u32[]{:S(2)}, u32[]{:S(2)}) collective-permute-start(f32[4,128,128]{2,1,0:T(8,128)S(1)} %get-tuple-element.118.refs_18_), channel_id=1, source_target_pairs={{0,2},{1,3},{2,0},{3,1},{4,6},{5,7},{6,4},{7,5},{8,10},{9,11},{10,... | collective-permute-start | bytes 786440 | tf_op jit(solution)/shard_map/ppermute | solution.py:370
  38.1 3.2 %collective-permute-start.9 = (f32[2,128,128]{2,1,0:T(8,128)S(1)}, f32[2,128,128]{2,1,0:T(8,128)S(1)}, u32[]{:S(2)}, u32[]{:S(2)}) collective-permute-start(f32[2,128,128]{2,1,0:T(8,128)S(1)} %get-tuple-element.124), channel_id=1, source_target_pairs={{0,1},{1,0},{2,3},{3,2},{4,5},{5,4},{6,7},{7,6},{8,9},{9,8},{10,11... | collective-permute-start | bytes 393224 | tf_op jit(solution)/shard_map/ppermute | solution.py:370
  38.2 3.1 %collective-permute-start.8 = (f32[2,128,128]{2,1,0:T(8,128)S(1)}, f32[2,128,128]{2,1,0:T(8,128)S(1)}, u32[]{:S(2)}, u32[]{:S(2)}) collective-permute-start(f32[2,128,128]{2,1,0:T(8,128)S(1)} %get-tuple-element.125), channel_id=1, source_target_pairs={{0,1},{1,0},{2,3},{3,2},{4,5},{5,4},{6,7},{7,6},{8,9},{9,8},{10,11... | collective-permute-start | bytes 393224 | tf_op jit(solution)/shard_map/ppermute | solution.py:370
  44.0 1.6 %collective-permute-start.13 = (f32[4,128,128]{2,1,0:T(8,128)S(1)}, f32[4,128,128]{2,1,0:T(8,128)S(1)}, u32[]{:S(2)}, u32[]{:S(2)}) collective-permute-start(f32[4,128,128]{2,1,0:T(8,128)S(1)} %get-tuple-element.128), channel_id=1, source_target_pairs={{0,1},{1,0},{2,3},{3,2},{4,5},{5,4},{6,7},{7,6},{8,9},{9,8},{10,11... | collective-permute-start | bytes 786440 | tf_op jit(solution)/shard_map/ppermute | solution.py:370

commit v6 on v5

--- a/solution.py
+++ b/solution.py
@@ -43,6 +43,11 @@
 
 def state_products(is_kv, side, quarter, info, q, k, v, d, out):
     count = q.shape[0]
+    pieces = out if isinstance(out, tuple) else (out,)
+    each = pieces[0].shape[0]
+
+    def at(n):
+        return pieces[n // each].at[n % each]
 
     @pl.when(is_kv)
     def _():
@@ -50,7 +55,7 @@
             head = first_head(info, side, part, quarter)
             for i in range(quarter):
                 cols = pl.ds(pl.multiple_of((head + i) * DH, DH), DH)
-                out[part * quarter + i] = dot(k[:, cols], v[:, cols], 0, 0)
+                at(part * quarter + i)[...] = dot(k[:, cols], v[:, cols], 0, 0)
 
     @pl.when(jnp.logical_not(is_kv))
     def _():
@@ -60,7 +65,7 @@
             for i in range(quarter):
                 cols = pl.ds(pl.multiple_of((head + i) * DH, DH), DH)
                 scaled = (d[:, cols].astype(F32) * scale).astype(BF16)
-                out[part * quarter + i] = dot(q[:, cols], scaled, 0, 0)
+                at(part * quarter + i)[...] = dot(q[:, cols], scaled, 0, 0)
 
 
 def pair_copies(info, side, width, rows, sems, *pair):
@@ -71,7 +76,7 @@
             yield pltpu.make_async_copy(there.at[at], here.at[at], sems.at[n, step])
 
 
-def first_kernel(quarter, rows, info, q, k, v, d, out, left, right, sems):
+def first_kernel(quarter, rows, info, q, k, v, d, keep, give, left, right, sems):
     width = q.shape[1]
     is_kv = info[EVEN] == 1
 
@@ -92,7 +97,7 @@
 
     for copy in copies(1, k, v):
         copy.wait()
-    state_products(is_kv, 1, quarter, info, left, left, right, right, out)
+    state_products(is_kv, 1, quarter, info, left, left, right, right, (keep, give))
     for copy in copies(0, k, v):
         copy.wait()
 
@@ -103,10 +108,10 @@
     rows = count // 4
     return pl.pallas_call(
         functools.partial(first_kernel, heads // 4, rows),
-        out_shape=[jax.ShapeDtypeStruct((heads // 2, DH, DH), F32)]
+        out_shape=[jax.ShapeDtypeStruct((heads // 4, DH, DH), F32)] * 2
         + [jax.ShapeDtypeStruct((count, width), BF16)] * 2,
         in_specs=[IN_SMEM] + [IN_HBM] * 4,
-        out_specs=[IN_VMEM] * 3,
+        out_specs=[IN_VMEM] * 4,
         scratch_shapes=[pltpu.SemaphoreType.DMA((2, 2, count // rows))],
         compiler_params=pltpu.CompilerParams(vmem_limit_bytes=4 * MIB),
         cost_estimate=SMALL,
@@ -239,7 +244,7 @@
     o_hbm, dq_hbm, dk_hbm, dv_hbm, zero, one, other, sems = refs
     zero[...] = jnp.zeros_like(zero)
     count = q.shape[0]
-    two = 2
+    two = 4
     is_kv = (info[EARLY_KV] == 1) if early else (info[EARLY_KV] != 1)
     steps = [(n, j) for n in range(len(kinds)) for j in range(quarter // two)]
     starts = [first_head(info, side, part, quarter) * DH for side, part in kinds]
@@ -320,7 +325,7 @@
         scratch_shapes=[
             pltpu.VMEM((count, columns), BF16),
             pltpu.VMEM((count, columns), BF16),
-            pltpu.SemaphoreType.DMA((columns // (2 * DH), 2)),
+            pltpu.SemaphoreType.DMA((columns // (4 * DH), 2)),
         ],
         input_output_aliases={first_out + n: n for n in range(len(filled))},
         compiler_params=pltpu.CompilerParams(vmem_limit_bytes=8 * MIB),
@@ -330,8 +335,8 @@
 
 
 def prepare_kernel(early, n_after, info, *refs):
-    near, f_own, f_got, f_keep, f_other, s_own, s_got, s_keep, s_other = refs[:9]
-    across, mine, theirs, rest_mine, rest_theirs = refs[9 + n_after :]
+    near, f_own, f_got, f_got_give, f_keep, f_other, s_own, s_got, s_keep, s_other = refs[:10]
+    across, mine, theirs, rest_mine, rest_theirs = refs[10 + n_after :]
     quarter = near.shape[0]
     is_kv = (info[EARLY_KV] == 1) if early else (info[EARLY_KV] != 1)
     is_first = (info[EVEN] == 1) == is_kv
@@ -349,7 +354,7 @@
         mine[i] = here + jnp.where(after_core, got, 0.0)
         theirs[i] = here + jnp.where(after_core, 0.0, own)
         own = jnp.where(is_first, f_own[quarter + i], s_own[quarter + i])
-        got = jnp.where(is_first, f_got[quarter + i], s_got[quarter + i])
+        got = jnp.where(is_first, f_got_give[i], s_got[quarter + i])
         rest_mine[i] = jnp.where(after_core, got, 0.0)
         rest_theirs[i] = jnp.where(after_core, 0.0, own)
 
@@ -358,7 +363,7 @@
     return pl.pallas_call(
         functools.partial(prepare_kernel, early, len(after)),
         out_shape=[jax.ShapeDtypeStruct(near.shape, F32)] * 5,
-        in_specs=[IN_SMEM] + [IN_VMEM] * (9 + len(after)),
+        in_specs=[IN_SMEM] + [IN_VMEM] * (10 + len(after)),
         out_specs=[IN_VMEM] * 5,
         compiler_params=pltpu.CompilerParams(vmem_limit_bytes=4 * MIB),
         cost_estimate=SMALL,
@@ -410,10 +415,12 @@
         return own[:quarter] + got[:quarter], own[quarter:] + got[quarter:]
 
     kinds = (0, 0), (0, 1), (1, 0), (1, 1)
-    f_sib, left, right = first_state(info, far_args)
-    f_got = send(f_sib, core_swap)
+    sib_keep, sib_give, left, right = first_state(info, far_args)
+    got_give = send(sib_give, core_swap)
+    got_keep = send(sib_keep, core_swap)
     f_own = own_state(info, left, right)
-    f_keep, f_give = halves(f_own, f_got)
+    f_give = f_own[quarter:] + got_give
+    f_keep = f_own[:quarter] + got_keep
     f_other = send(f_give, row_swap)
     s_sib, s_own, *args = second_states(info, far_args, (f_give,))
     part_a, zero = local_part(info, args, kinds[:1], 0.0, (s_own,))
@@ -422,7 +429,7 @@
     f_total = f_keep + f_other + zero
     s_give, f_total = lax.optimization_barrier((s_give, f_total))
     s_other = send(s_give, row_swap)
-    f = f_own, f_got, f_keep, f_other
+    f = f_own, got_keep, got_give, f_keep, f_other
     s = s_own, s_got, s_keep, s_other
     part_b, inside = local_part(info, args, kinds[1:], 1.0, (s_give,))
     partials = part_a | part_b

time: 48.3 us -> 47.8 us (0.990)
  waiting for transfers between devices: 6.17 us -> 5.32 us
    ppermute x14 -> x15, waiting for transfers between devices: 6.17 us -> 5.32 us  [send(): return lax.ppermute(array, 'seq', pairs)]
    ppermute x14 -> x15, starting transfers between devices: 15.3 us -> 15.4 us  [send(): return lax.ppermute(array, 'seq', pairs)]
  transfers between devices with their start and end apart: 14 -> 15, of which waited for: 5 -> 5; matrix products, arithmetic and copies ran while one was open for 1% -> 1% of each run, Pallas kernels for 42% -> 43%
where the time goes in v6:
time: 47.8 us; the launch traced here: 47.7 us
  Pallas kernels  25.5 us (53%)
  starting transfers between devices  15.4 us (32%)
  waiting for transfers between devices  5.32 us (11%)
  between operations  0.91 us (2%)
    ppermute x15, starting transfers between devices, send(): return lax.ppermute(array, 'seq', pairs)  15.4 us
    pallas_call x4, Pallas kernels, apply_states(): pl.pallas_call(functools.partial(apply_kernel, early, kinds, len(arrays)...  9.12 us
    pallas_call x2, Pallas kernels, local_part(): pl.pallas_call(functools.partial(local_kernel, kinds, quarter, mark, len(...  8.24 us
    ppermute x15, waiting for transfers between devices, send(): return lax.ppermute(array, 'seq', pairs)  5.32 us
    pallas_call x1, Pallas kernels, second_states(): pl.pallas_call(functools.partial(second_kernel, heads // 4, rows, len(aft...  3.22 us
    pallas_call x1, Pallas kernels, first_state(): pl.pallas_call(functools.partial(first_kernel, heads // 4, rows), out_sha...  2.46 us
    pallas_call x2, Pallas kernels, prepare(): pl.pallas_call(functools.partial(prepare_kernel, early, len(after)), out_...  1.44 us
    pallas_call x1, Pallas kernels, own_state(): pl.pallas_call(functools.partial(own_kernel, heads // 4), out_shape=jax.S...  1.02 us
  transfers between devices with their start and end apart: 15, of which 5 were waited for; matrix products, arithmetic and copies ran while one was open for 1% of the time, Pallas kernels for 43%

profile of v6, /device:TPU:0, one launch (start us, length us, event | category | flops | bytes accessed | tf_op | source)
XLA Modules:
  0.0 47.7 jit_solution(6587934225216735457)
XLA Ops:
  0.7 0.1 stack.39.info
  0.8 2.5 %first.1 = (f32[4,128,128]{2,1,0:T(8,128)S(1)}, f32[4,128,128]{2,1,0:T(8,128)S(1)}, bf16[256,2048]{1,0:T(8,128)(2,1)S(1)}, bf16[256,2048]{1,0:T(8,128)(2,1)S(1)}) custom-call(s32[6]{0:T(128)S(1)} %stack.39.info, bf16[256,2048]{1,0:T(8,128)(2,1)} %q.3, bf16[256,2048]{1,0:T(8,128)(2,1)} %k.3, bf16[256,2048]{1,0:T(8,128)(2,1)} %v.3, bf16[256,2048]{1,0:T(8,128)(2,1)} %d.3), custom_call_target="tpu_custom_call" | custom-call | flops 1 | bytes 1 | tf_op jit(solution)/shard_map/first/pallas_call | solution.py:109
  3.2 0.5 %collective-permute-start = (f32[4,128,128]{2,1,0:T(8,128)S(1)}, f32[4,128,128]{2,1,0:T(8,128)S(1)}, u32[]{:S(2)}, u32[]{:S(2)}) collective-permute-start(f32[4,128,128]{2,1,0:T(8,128)S(1)} %get-tuple-element.64), channel_id=1, source_target_pairs={{0,1},{1,0},{2,3},{3,2},{4,5},{5,4},{6,7},{7,6},{8,9},{9,8},{10,11... | collective-permute-start | bytes 786440 | tf_op jit(solution)/shard_map/ppermute | solution.py:375
  3.8 0.1 collective-permute-start.2
  3.8 1.0 %own.1.refs_1_ = f32[8,128,128]{2,1,0:T(8,128)S(1)} custom-call(s32[6]{0:T(128)S(1)} %stack.39.info, bf16[256,2048]{1,0:T(8,128)(2,1)S(1)} %get-tuple-element.62.left, bf16[256,2048]{1,0:T(8,128)(2,1)S(1)} %get-tuple-element.63.right), custom_call_target="tpu_custom_call" | custom-call | flops 1 | bytes 1 | tf_op jit(solution)/shard_map/own/pallas_call | solution.py:129
  5.0 3.0 %collective-permute-start.3 = (f32[4,128,128]{2,1,0:T(8,128)S(1)}, f32[4,128,128]{2,1,0:T(8,128)S(1)}, u32[]{:S(2)}, u32[]{:S(2)}) collective-permute-start(f32[4,128,128]{2,1,0:T(8,128)S(1)} %slice_add_fusion.3.refs_0_), channel_id=1, source_target_pairs={{0,2},{1,3},{2,0},{3,1},{4,6},{5,7},{6,4},{7,5},{8,10},{9,11},{10,... | collective-permute-start | bytes 786440 | tf_op jit(solution)/shard_map/ppermute | solution.py:375
  7.9 3.2 %second.1 = (f32[8,128,128]{2,1,0:T(8,128)S(1)}, f32[8,128,128]{2,1,0:T(8,128)S(1)}, bf16[256,2048]{1,0:T(8,128)(2,1)S(1)}, bf16[256,2048]{1,0:T(8,128)(2,1)S(1)...) custom-call(s32[6]{0:T(128)S(1)} %stack.39.info, bf16[256,2048]{1,0:T(8,128)(2,1)} %q.3, ...), custom_call_target="tpu_custom_call" | custom-call | flops 1 | bytes 1 | tf_op jit(solution)/shard_map/second/pallas_call | solution.py:176
  11.2 0.1 collective-permute-start.1
  11.2 2.4 %local.2 = (f32[256,512]{1,0:T(8,128)S(1)}, f32[256,512]{1,0:T(8,128)S(1)}, f32[256,512]{1,0:T(8,128)S(1)}, f32[256,512]{1,0:T(8,128)S(1)}, f32[4,128,128]{2,1,0:T(8,128)S(1)}) custom-call(s32[6]{0:T(128)S(1)} %stack.39.info, bf16[256,2048]{1,0:T(8,128)(2,1)S(1)} %get-tuple-element.65.q.refs_0_, bf16[256,2048]{1,0:T(8,128)(2,1)S(1)} %get-tuple-element.66.k.refs_1_, ...), custom_call_target="tpu_custom_call" | custom-call | flops 1 | bytes 1 | tf_op jit(solution)/shard_map/local/pallas_call | solution.py:223
  13.6 0.9 %collective-permute-done.3.refs_5_ = f32[4,128,128]{2,1,0:T(8,128)S(1)} collective-permute-done((f32[4,128,128]{2,1,0:T(8,128)S(1)}, f32[4,128,128]{2,1,0:T(8,128)S(1)}, u32[]{:S(2)}, u32[]{:S(2)}) %collective-permute-start.3) | collective-permute-done | bytes 262176 | tf_op jit(solution)/shard_map/ppermute | solution.py:375
  14.6 1.9 %collective-permute-start.5 = (f32[4,128,128]{2,1,0:T(8,128)S(1)}, f32[4,128,128]{2,1,0:T(8,128)S(1)}, u32[]{:S(2)}, u32[]{:S(2)}) collective-permute-start(f32[4,128,128]{2,1,0:T(8,128)S(1)} %get-tuple-element.83), channel_id=1, source_target_pairs={{0,4},{1,5},{2,6},{3,7},{4,0},{5,1},{6,2},{7,3},{8,12},{9,13},{10,... | collective-permute-start | bytes 786440 | tf_op jit(solution)/shard_map/ppermute | solution.py:375
  16.6 1.5 %collective-permute-start.4 = (f32[4,128,128]{2,1,0:T(8,128)S(1)}, f32[4,128,128]{2,1,0:T(8,128)S(1)}, u32[]{:S(2)}, u32[]{:S(2)}) collective-permute-start(f32[4,128,128]{2,1,0:T(8,128)S(1)} %slice_add_fusion.2.refs_0_), channel_id=1, source_target_pairs={{0,2},{1,3},{2,0},{3,1},{4,6},{5,7},{6,4},{7,5},{8,10},{9,11},{10,... | collective-permute-start | bytes 786440 | tf_op jit(solution)/shard_map/ppermute | solution.py:375
  18.1 5.8 %local.3 = (f32[256,512]{1,0:T(8,128)S(1)}, f32[256,512]{1,0:T(8,128)S(1)}, f32[256,512]{1,0:T(8,128)S(1)}, f32[256,512]{1,0:T(8,128)S(1)}, f32[256,512]{1,0:T(8...) custom-call(s32[6]{0:T(128)S(1)} %stack.39.info, ...), custom_call_target="tpu_custom_call" | custom-call | flops 1 | bytes 1 | tf_op jit(solution)/shard_map/local/pallas_call | solution.py:223
  24.0 0.1 add_select_fusion
  24.0 0.1 collective-permute-start.6
  24.1 0.7 %prepare.2 = (f32[4,128,128]{2,1,0:T(8,128)S(1)}, f32[4,128,128]{2,1,0:T(8,128)S(1)}, f32[4,128,128]{2,1,0:T(8,128)S(1)}, f32[4,128,128]{2,1,0:T(8,128)S(1)}, f32[4,128,128]{2,1,0:T(8,128)S(1)}) custom-call(s32[6]{0:T(128)S(1)} %stack.39.info, f32[4,128,128]{2,1,0:T(8,128)S(1)} %collective-permute-done.5.refs_0_, f32[8,128,128]{2,1,0:T(8,128)S(1)} %own.1.refs_1_, ...), custom_call_target="tpu_custom_call" | custom-call | flops 1 | bytes 1 | tf_op jit(solution)/shard_map/prepare/pallas_call | solution.py:363
  24.8 0.6 %collective-permute-start.12 = (f32[4,128,128]{2,1,0:T(8,128)S(1)}, f32[4,128,128]{2,1,0:T(8,128)S(1)}, u32[]{:S(2)}, u32[]{:S(2)}) collective-permute-start(f32[4,128,128]{2,1,0:T(8,128)S(1)} %get-tuple-element.99), channel_id=1, source_target_pairs={{0,1},{1,0},{2,3},{3,2},{4,5},{5,4},{6,7},{7,6},{8,9},{9,8},{10,11... | collective-permute-start | bytes 786440 | tf_op jit(solution)/shard_map/ppermute | solution.py:375
  25.4 1.3 %collective-permute-start.11 = (f32[4,128,128]{2,1,0:T(8,128)S(1)}, f32[4,128,128]{2,1,0:T(8,128)S(1)}, u32[]{:S(2)}, u32[]{:S(2)}) collective-permute-start(f32[4,128,128]{2,1,0:T(8,128)S(1)} %get-tuple-element.84.refs_10_.refs_14_), channel_id=1, source_target_pairs={{0,2},{1,3},{2,0},{3,1},{4,6},{5,7},{6,4},{7,5},{8,10},{9,11},{10,... | collective-permute-start | bytes 786440 | tf_op jit(solution)/shard_map/ppermute | solution.py:375
  26.7 0.7 %prepare.3 = (f32[4,128,128]{2,1,0:T(8,128)S(1)}, f32[4,128,128]{2,1,0:T(8,128)S(1)}, f32[4,128,128]{2,1,0:T(8,128)S(1)}, f32[4,128,128]{2,1,0:T(8,128)S(1)}, f32[4,128,128]{2,1,0:T(8,128)S(1)}) custom-call(s32[6]{0:T(128)S(1)} %stack.39.info, f32[4,128,128]{2,1,0:T(8,128)S(1)} %collective-permute-done.5.refs_0_, f32[8,128,128]{2,1,0:T(8,128)S(1)} %own.1.refs_1_, ...), custom_call_target="tpu_custom_call" | custom-call | flops 1 | bytes 1 | tf_op jit(solution)/shard_map/prepare/pallas_call | solution.py:363
  27.4 5.0 %collective-permute-start.7 = (f32[4,128,128]{2,1,0:T(8,128)S(1)}, f32[4,128,128]{2,1,0:T(8,128)S(1)}, u32[]{:S(2)}, u32[]{:S(2)}) collective-permute-start(f32[4,128,128]{2,1,0:T(8,128)S(1)} %collective-permute-done.6), channel_id=1, source_target_pairs={{0,4},{1,5},{2,6},{3,7},{4,0},{5,1},{6,2},{7,3},{8,12},{9,13},{10,... | collective-permute-start | bytes 786440 | tf_op jit(solution)/shard_map/ppermute | solution.py:375
  32.4 1.9 %apply.4 = (bf16[256,2048]{1,0:T(8,128)(2,1)}, bf16[256,2048]{1,0:T(8,128)(2,1)}, bf16[256,2048]{1,0:T(8,128)(2,1)}, bf16[256,2048]{1,0:T(8,128)(2,1)}, f32[4,128,128]{2,1,0:T(8,128)S(1)}) custom-call(s32[6]{0:T(128)S(1)} %stack.39.info, bf16[256,2048]{1,0:T(8,128)(2,1)S(1)} %get-tuple-element.65.q.refs_0_, ...), custom_call_target="tpu_custom_call" | custom-call | flops 1 | bytes 1 | tf_op jit(solution)/shard_map/apply/pallas_call | solution.py:314
  34.4 0.1 fusion.2
  34.4 0.1 collective-permute-start.13
  34.5 2.4 %collective-permute-done.7 = f32[4,128,128]{2,1,0:T(8,128)S(1)} collective-permute-done((f32[4,128,128]{2,1,0:T(8,128)S(1)}, f32[4,128,128]{2,1,0:T(8,128)S(1)}, u32[]{:S(2)}, u32[]{:S(2)}) %collective-permute-start.7) | collective-permute-done | bytes 262176 | tf_op jit(solution)/shard_map/ppermute | solution.py:375
  37.0 0.8 %collective-permute-start.8 = (f32[4,128,128]{2,1,0:T(8,128)S(1)}, f32[4,128,128]{2,1,0:T(8,128)S(1)}, u32[]{:S(2)}, u32[]{:S(2)}) collective-permute-start(f32[4,128,128]{2,1,0:T(8,128)S(1)} %get-tuple-element.120.refs_18_), channel_id=1, source_target_pairs={{0,2},{1,3},{2,0},{3,1},{4,6},{5,7},{6,4},{7,5},{8,10},{9,11},{10,... | collective-permute-start | bytes 786440 | tf_op jit(solution)/shard_map/ppermute | solution.py:375
  37.8 0.1 collective-permute-start.10
  37.8 0.5 %collective-permute-start.9 = (f32[2,128,128]{2,1,0:T(8,128)S(1)}, f32[2,128,128]{2,1,0:T(8,128)S(1)}, u32[]{:S(2)}, u32[]{:S(2)}) collective-permute-start(f32[2,128,128]{2,1,0:T(8,128)S(1)} %get-tuple-element.127), channel_id=1, source_target_pairs={{0,1},{1,0},{2,3},{3,2},{4,5},{5,4},{6,7},{7,6},{8,9},{9,8},{10,11... | collective-permute-start | bytes 393224 | tf_op jit(solution)/shard_map/ppermute | solution.py:375
  38.4 2.7 %apply.5 = (bf16[256,2048]{1,0:T(8,128)(2,1)}, bf16[256,2048]{1,0:T(8,128)(2,1)}, bf16[256,2048]{1,0:T(8,128)(2,1)}, bf16[256,2048]{1,0:T(8,128)(2,1)}, f32[4,128,128]{2,1,0:T(8,128)}) custom-call(s32[6]{0:T(128)S(1)} %stack.39.info, ...), custom_call_target="tpu_custom_call", output_to_operand_aliasing={{0}: (15, {}), {1}: (16, {}), {2}: (17, {}), {3}: (18, {})} | custom-call | flops 1 | bytes 1 | tf_op jit(solution)/shard_map/apply/pallas_call | solution.py:314
  41.0 1.9 %apply.6 = (bf16[256,2048]{1,0:T(8,128)(2,1)}, bf16[256,2048]{1,0:T(8,128)(2,1)}, bf16[256,2048]{1,0:T(8,128)(2,1)}, bf16[256,2048]{1,0:T(8,128)(2,1)}, f32[4,128,128]{2,1,0:T(8,128)S(1)}) custom-call(s32[6]{0:T(128)S(1)} %stack.39.info, ...), custom_call_target="tpu_custom_call", output_to_operand_aliasing={{0}: (17, {}), {1}: (18, {}), {2}: (19, {}), {3}: (20, {})} | custom-call | flops 1 | bytes 1 | tf_op jit(solution)/shard_map/apply/pallas_call | solution.py:314
  42.9 0.5 collective-permute-done.8
  43.5 1.5 %collective-permute-done.14.refs_13_ = f32[4,128,128]{2,1,0:T(8,128)S(1)} collective-permute-done((f32[4,128,128]{2,1,0:T(8,128)S(1)}, f32[4,128,128]{2,1,0:T(8,128)S(1)}, u32[]{:S(2)}, u32[]{:S(2)}) %collective-permute-start.14) | collective-permute-done | bytes 262176 | tf_op jit(solution)/shard_map/ppermute | solution.py:375
  45.1 2.6 %apply.7 = (bf16[256,2048]{1,0:T(8,128)(2,1)}, bf16[256,2048]{1,0:T(8,128)(2,1)}, bf16[256,2048]{1,0:T(8,128)(2,1)}, bf16[256,2048]{1,0:T(8,128)(2,1)}, f32[4,128,128]{2,1,0:T(8,128)}) custom-call(s32[6]{0:T(128)S(1)} %stack.39.info, ...), custom_call_target="tpu_custom_call", output_to_operand_aliasing={{0}: (15, {}), {1}: (16, {}), {2}: (17, {}), {3}: (18, {})} | custom-call | flops 1 | bytes 1 | tf_op jit(solution)/shard_map/apply/pallas_call | solution.py:314
  (18 shorter events, 0.4 us)
Async XLA Ops:
  3.2 1.7 %collective-permute-start = (f32[4,128,128]{2,1,0:T(8,128)S(1)}, f32[4,128,128]{2,1,0:T(8,128)S(1)}, u32[]{:S(2)}, u32[]{:S(2)}) collective-permute-start(f32[4,128,128]{2,1,0:T(8,128)S(1)} %get-tuple-element.64), channel_id=1, source_target_pairs={{0,1},{1,0},{2,3},{3,2},{4,5},{5,4},{6,7},{7,6},{8,9},{9,8},{10,11... | collective-permute-start | bytes 786440 | tf_op jit(solution)/shard_map/ppermute | solution.py:375
  3.8 9.9 %collective-permute-start.2 = (f32[4,128,128]{2,1,0:T(8,128)S(1)}, f32[4,128,128]{2,1,0:T(8,128)S(1)}, u32[]{:S(2)}, u32[]{:S(2)}) collective-permute-start(f32[4,128,128]{2,1,0:T(8,128)S(1)} %get-tuple-element.71), channel_id=1, source_target_pairs={{0,1},{1,0},{2,3},{3,2},{4,5},{5,4},{6,7},{7,6},{8,9},{9,8},{10,11... | collective-permute-start | bytes 786440 | tf_op jit(solution)/shard_map/ppermute | solution.py:375
  5.0 9.6 %collective-permute-start.3 = (f32[4,128,128]{2,1,0:T(8,128)S(1)}, f32[4,128,128]{2,1,0:T(8,128)S(1)}, u32[]{:S(2)}, u32[]{:S(2)}) collective-permute-start(f32[4,128,128]{2,1,0:T(8,128)S(1)} %slice_add_fusion.3.refs_0_), channel_id=1, source_target_pairs={{0,2},{1,3},{2,0},{3,1},{4,6},{5,7},{6,4},{7,5},{8,10},{9,11},{10,... | collective-permute-start | bytes 786440 | tf_op jit(solution)/shard_map/ppermute | solution.py:375
  11.2 3.4 %collective-permute-start.1 = (f32[8,128,128]{2,1,0:T(8,128)S(1)}, f32[8,128,128]{2,1,0:T(8,128)S(1)}, u32[]{:S(2)}, u32[]{:S(2)}) collective-permute-start(f32[8,128,128]{2,1,0:T(8,128)S(1)} %get-tuple-element.70), channel_id=1, source_target_pairs={{0,1},{1,0},{2,3},{3,2},{4,5},{5,4},{6,7},{7,6},{8,9},{9,8},{10,11... | collective-permute-start | bytes 1572872 | tf_op jit(solution)/shard_map/ppermute | solution.py:375
  14.6 9.3 %collective-permute-start.5 = (f32[4,128,128]{2,1,0:T(8,128)S(1)}, f32[4,128,128]{2,1,0:T(8,128)S(1)}, u32[]{:S(2)}, u32[]{:S(2)}) collective-permute-start(f32[4,128,128]{2,1,0:T(8,128)S(1)} %get-tuple-element.83), channel_id=1, source_target_pairs={{0,4},{1,5},{2,6},{3,7},{4,0},{5,1},{6,2},{7,3},{8,12},{9,13},{10,... | collective-permute-start | bytes 786440 | tf_op jit(solution)/shard_map/ppermute | solution.py:375
  16.6 7.4 %collective-permute-start.4 = (f32[4,128,128]{2,1,0:T(8,128)S(1)}, f32[4,128,128]{2,1,0:T(8,128)S(1)}, u32[]{:S(2)}, u32[]{:S(2)}) collective-permute-start(f32[4,128,128]{2,1,0:T(8,128)S(1)} %slice_add_fusion.2.refs_0_), channel_id=1, source_target_pairs={{0,2},{1,3},{2,0},{3,1},{4,6},{5,7},{6,4},{7,5},{8,10},{9,11},{10,... | collective-permute-start | bytes 786440 | tf_op jit(solution)/shard_map/ppermute | solution.py:375
  24.0 3.4 %collective-permute-start.6 = (f32[4,128,128]{2,1,0:T(8,128)S(1)}, f32[4,128,128]{2,1,0:T(8,128)S(1)}, u32[]{:S(2)}, u32[]{:S(2)}) collective-permute-start(f32[4,128,128]{2,1,0:T(8,128)S(1)} %get-tuple-element.122), channel_id=1, source_target_pairs={{4,8},{5,9},{6,10},{7,11},{8,4},{9,5},{10,6},{11,7},{0,1},{1,0},{2... | collective-permute-start | bytes 786440 | tf_op jit(solution)/shard_map/ppermute | solution.py:375
  24.8 7.6 %collective-permute-start.12 = (f32[4,128,128]{2,1,0:T(8,128)S(1)}, f32[4,128,128]{2,1,0:T(8,128)S(1)}, u32[]{:S(2)}, u32[]{:S(2)}) collective-permute-start(f32[4,128,128]{2,1,0:T(8,128)S(1)} %get-tuple-element.99), channel_id=1, source_target_pairs={{0,1},{1,0},{2,3},{3,2},{4,5},{5,4},{6,7},{7,6},{8,9},{9,8},{10,11... | collective-permute-start | bytes 786440 | tf_op jit(solution)/shard_map/ppermute | solution.py:375
  25.4 9.0 %collective-permute-start.11 = (f32[4,128,128]{2,1,0:T(8,128)S(1)}, f32[4,128,128]{2,1,0:T(8,128)S(1)}, u32[]{:S(2)}, u32[]{:S(2)}) collective-permute-start(f32[4,128,128]{2,1,0:T(8,128)S(1)} %get-tuple-element.84.refs_10_.refs_14_), channel_id=1, source_target_pairs={{0,2},{1,3},{2,0},{3,1},{4,6},{5,7},{6,4},{7,5},{8,10},{9,11},{10,... | collective-permute-start | bytes 786440 | tf_op jit(solution)/shard_map/ppermute | solution.py:375
  27.4 9.5 %collective-permute-start.7 = (f32[4,128,128]{2,1,0:T(8,128)S(1)}, f32[4,128,128]{2,1,0:T(8,128)S(1)}, u32[]{:S(2)}, u32[]{:S(2)}) collective-permute-start(f32[4,128,128]{2,1,0:T(8,128)S(1)} %collective-permute-done.6), channel_id=1, source_target_pairs={{0,4},{1,5},{2,6},{3,7},{4,0},{5,1},{6,2},{7,3},{8,12},{9,13},{10,... | collective-permute-start | bytes 786440 | tf_op jit(solution)/shard_map/ppermute | solution.py:375
  34.4 3.9 %collective-permute-start.13 = (f32[4,128,128]{2,1,0:T(8,128)S(1)}, f32[4,128,128]{2,1,0:T(8,128)S(1)}, u32[]{:S(2)}, u32[]{:S(2)}) collective-permute-start(f32[4,128,128]{2,1,0:T(8,128)S(1)} %get-tuple-element.132), channel_id=1, source_target_pairs={{0,1},{1,0},{2,3},{3,2},{4,5},{5,4},{6,7},{7,6},{8,9},{9,8},{10,11... | collective-permute-start | bytes 786440 | tf_op jit(solution)/shard_map/ppermute | solution.py:375
  37.0 6.4 %collective-permute-start.8 = (f32[4,128,128]{2,1,0:T(8,128)S(1)}, f32[4,128,128]{2,1,0:T(8,128)S(1)}, u32[]{:S(2)}, u32[]{:S(2)}) collective-permute-start(f32[4,128,128]{2,1,0:T(8,128)S(1)} %get-tuple-element.120.refs_18_), channel_id=1, source_target_pairs={{0,2},{1,3},{2,0},{3,1},{4,6},{5,7},{6,4},{7,5},{8,10},{9,11},{10,... | collective-permute-start | bytes 786440 | tf_op jit(solution)/shard_map/ppermute | solution.py:375
  37.8 3.3 %collective-permute-start.10 = (f32[2,128,128]{2,1,0:T(8,128)S(1)}, f32[2,128,128]{2,1,0:T(8,128)S(1)}, u32[]{:S(2)}, u32[]{:S(2)}) collective-permute-start(f32[2,128,128]{2,1,0:T(8,128)S(1)} %get-tuple-element.126), channel_id=1, source_target_pairs={{0,1},{1,0},{2,3},{3,2},{4,5},{5,4},{6,7},{7,6},{8,9},{9,8},{10,11... | collective-permute-start | bytes 393224 | tf_op jit(solution)/shard_map/ppermute | solution.py:375
  37.8 3.2 %collective-permute-start.9 = (f32[2,128,128]{2,1,0:T(8,128)S(1)}, f32[2,128,128]{2,1,0:T(8,128)S(1)}, u32[]{:S(2)}, u32[]{:S(2)}) collective-permute-start(f32[2,128,128]{2,1,0:T(8,128)S(1)} %get-tuple-element.127), channel_id=1, source_target_pairs={{0,1},{1,0},{2,3},{3,2},{4,5},{5,4},{6,7},{7,6},{8,9},{9,8},{10,11... | collective-permute-start | bytes 393224 | tf_op jit(solution)/shard_map/ppermute | solution.py:375
  43.5 1.6 %collective-permute-start.14 = (f32[4,128,128]{2,1,0:T(8,128)S(1)}, f32[4,128,128]{2,1,0:T(8,128)S(1)}, u32[]{:S(2)}, u32[]{:S(2)}) collective-permute-start(f32[4,128,128]{2,1,0:T(8,128)S(1)} %get-tuple-element.130), channel_id=1, source_target_pairs={{0,1},{1,0},{2,3},{3,2},{4,5},{5,4},{6,7},{7,6},{8,9},{9,8},{10,11... | collective-permute-start | bytes 786440 | tf_op jit(solution)/shard_map/ppermute | solution.py:375

commit v7 on v6

--- a/solution.py
+++ b/solution.py
@@ -241,10 +241,11 @@
     n_states = len(kinds) * pieces
     state_refs, refs = refs[:n_states], refs[n_states + n_filled + n_after :]
     each = quarter // pieces
-    o_hbm, dq_hbm, dk_hbm, dv_hbm, zero, one, other, sems = refs
-    zero[...] = jnp.zeros_like(zero)
+    o_hbm, dq_hbm, dk_hbm, dv_hbm, *zero, one, other, sems = refs
+    for ref in zero:
+        ref[...] = jnp.zeros_like(ref)
     count = q.shape[0]
-    two = 4
+    two = 2
     is_kv = (info[EARLY_KV] == 1) if early else (info[EARLY_KV] != 1)
     steps = [(n, j) for n in range(len(kinds)) for j in range(quarter // two)]
     starts = [first_head(info, side, part, quarter) * DH for side, part in kinds]
@@ -304,7 +305,7 @@
             copy.wait()
 
 
-def apply_states(info, args, partials, early, kinds, arrays, outs, after=()):
+def apply_states(info, args, partials, early, kinds, arrays, outs, after=(), tells=False):
     count, width = args[0].shape
     quarter = width // DH // 4
     filled = () if outs is None else tuple(outs)
@@ -316,16 +317,16 @@
             apply_kernel, early, kinds, len(arrays) // len(kinds), quarter, len(filled), len(after)
         ),
         out_shape=[jax.ShapeDtypeStruct((count, width), BF16)] * 4
-        + [jax.ShapeDtypeStruct((quarter, DH, DH), F32)],
+        + [jax.ShapeDtypeStruct((quarter, DH, DH), F32)] * tells,
         in_specs=[IN_SMEM]
         + [IN_VMEM] * (4 + len(partials) + len(arrays))
         + [IN_HBM] * len(filled)
         + [IN_VMEM] * len(after),
-        out_specs=[IN_HBM] * 4 + [IN_VMEM],
+        out_specs=[IN_HBM] * 4 + [IN_VMEM] * tells,
         scratch_shapes=[
             pltpu.VMEM((count, columns), BF16),
             pltpu.VMEM((count, columns), BF16),
-            pltpu.SemaphoreType.DMA((columns // (4 * DH), 2)),
+            pltpu.SemaphoreType.DMA((columns // (2 * DH), 2)),
         ],
         input_output_aliases={first_out + n: n for n in range(len(filled))},
         compiler_params=pltpu.CompilerParams(vmem_limit_bytes=8 * MIB),
@@ -453,17 +454,17 @@
     t_other = send(across, row_swap)
     t_kept = mine, send(theirs, core_swap)
     late = prepare(info, False, near, f, s, (across,))
-    *outs, zero = finish(True, kept_heads, t_kept, None, (across, late[0]))
+    *outs, zero = finish(True, kept_heads, t_kept, None, (across, late[0]), True)
     t_rest = t_other + rest_mine + zero, send(t_other + rest_theirs, core_swap)
 
     across = coming + late[0]
     u_other = send(across, row_swap)
     u_kept = [coming[cut] + late[1][cut] for cut in cuts]
     u_kept += [send(coming[cut] + late[2][cut], core_swap) for cut in cuts]
-    *outs, _ = finish(True, other_heads, t_rest, outs, (across,))
-    *outs, zero = finish(False, kept_heads, u_kept, outs)
+    outs = finish(True, other_heads, t_rest, outs, (across,))
+    *outs, zero = finish(False, kept_heads, u_kept, outs, (), True)
     u_rest = u_other + late[3] + zero, send(u_other + late[4], core_swap)
-    *outs, _ = finish(False, other_heads, u_rest, outs)
+    outs = finish(False, other_heads, u_rest, outs)
     return tuple(outs)
 
 

time: 47.8 us -> 47.1 us (0.985)
  Pallas kernels: 25.5 us -> 23.9 us
  waiting for transfers between devices: 5.32 us -> 6.15 us
    pallas_call x4, Pallas kernels: 9.12 us -> 7.5 us  [apply_states(): pl.pallas_call(functools.partial(apply_kernel, early, kinds, len(arrays)...]
    ppermute x15, waiting for transfers between devices: 5.32 us -> 6.15 us  [send(): return lax.ppermute(array, 'seq', pairs)]
  transfers between devices with their start and end apart: 15 -> 15, of which waited for: 5 -> 5; matrix products, arithmetic and copies ran while one was open for 1% -> 1% of each run, Pallas kernels for 43% -> 42%
where the time goes in v7:
time: 47.1 us; the launch traced here: 46.9 us
  Pallas kernels  23.9 us (51%)
  starting transfers between devices  15.4 us (33%)
  waiting for transfers between devices  6.15 us (13%)
  between operations  0.91 us (2%)
    ppermute x15, starting transfers between devices, send(): return lax.ppermute(array, 'seq', pairs)  15.4 us
    pallas_call x2, Pallas kernels, local_part(): pl.pallas_call(functools.partial(local_kernel, kinds, quarter, mark, len(...  8.24 us
    pallas_call x4, Pallas kernels, apply_states(): pl.pallas_call(functools.partial(apply_kernel, early, kinds, len(arrays)...  7.5 us
    ppermute x15, waiting for transfers between devices, send(): return lax.ppermute(array, 'seq', pairs)  6.15 us
    pallas_call x1, Pallas kernels, second_states(): pl.pallas_call(functools.partial(second_kernel, heads // 4, rows, len(aft...  3.22 us
    pallas_call x1, Pallas kernels, first_state(): pl.pallas_call(functools.partial(first_kernel, heads // 4, rows), out_sha...  2.46 us
    pallas_call x2, Pallas kernels, prepare(): pl.pallas_call(functools.partial(prepare_kernel, early, len(after)), out_...  1.44 us
    pallas_call x1, Pallas kernels, own_state(): pl.pallas_call(functools.partial(own_kernel, heads // 4), out_shape=jax.S...  1.02 us
  transfers between devices with their start and end apart: 15, of which 5 were waited for; matrix products, arithmetic and copies ran while one was open for 1% of the time, Pallas kernels for 42%

profile of v7, /device:TPU:0, one launch (start us, length us, event | category | flops | bytes accessed | tf_op | source)
XLA Modules:
  0.0 46.9 jit_solution(11486617907016052577)
XLA Ops:
  0.7 0.1 stack.39.info
  0.8 2.5 %first.1 = (f32[4,128,128]{2,1,0:T(8,128)S(1)}, f32[4,128,128]{2,1,0:T(8,128)S(1)}, bf16[256,2048]{1,0:T(8,128)(2,1)S(1)}, bf16[256,2048]{1,0:T(8,128)(2,1)S(1)}) custom-call(s32[6]{0:T(128)S(1)} %stack.39.info, bf16[256,2048]{1,0:T(8,128)(2,1)} %q.3, bf16[256,2048]{1,0:T(8,128)(2,1)} %k.3, bf16[256,2048]{1,0:T(8,128)(2,1)} %v.3, bf16[256,2048]{1,0:T(8,128)(2,1)} %d.3), custom_call_target="tpu_custom_call" | custom-call | flops 1 | bytes 1 | tf_op jit(solution)/shard_map/first/pallas_call | solution.py:109
  3.2 0.5 %collective-permute-start = (f32[4,128,128]{2,1,0:T(8,128)S(1)}, f32[4,128,128]{2,1,0:T(8,128)S(1)}, u32[]{:S(2)}, u32[]{:S(2)}) collective-permute-start(f32[4,128,128]{2,1,0:T(8,128)S(1)} %get-tuple-element.60), channel_id=1, source_target_pairs={{0,1},{1,0},{2,3},{3,2},{4,5},{5,4},{6,7},{7,6},{8,9},{9,8},{10,11... | collective-permute-start | bytes 786440 | tf_op jit(solution)/shard_map/ppermute | solution.py:376
  3.8 0.1 collective-permute-start.2
  3.8 1.0 %own.1.refs_1_ = f32[8,128,128]{2,1,0:T(8,128)S(1)} custom-call(s32[6]{0:T(128)S(1)} %stack.39.info, bf16[256,2048]{1,0:T(8,128)(2,1)S(1)} %get-tuple-element.58.left, bf16[256,2048]{1,0:T(8,128)(2,1)S(1)} %get-tuple-element.59.right), custom_call_target="tpu_custom_call" | custom-call | flops 1 | bytes 1 | tf_op jit(solution)/shard_map/own/pallas_call | solution.py:129
  5.0 3.0 %collective-permute-start.3 = (f32[4,128,128]{2,1,0:T(8,128)S(1)}, f32[4,128,128]{2,1,0:T(8,128)S(1)}, u32[]{:S(2)}, u32[]{:S(2)}) collective-permute-start(f32[4,128,128]{2,1,0:T(8,128)S(1)} %slice_add_fusion.3.refs_0_), channel_id=1, source_target_pairs={{0,2},{1,3},{2,0},{3,1},{4,6},{5,7},{6,4},{7,5},{8,10},{9,11},{10,... | collective-permute-start | bytes 786440 | tf_op jit(solution)/shard_map/ppermute | solution.py:376
  7.9 3.2 %second.1 = (f32[8,128,128]{2,1,0:T(8,128)S(1)}, f32[8,128,128]{2,1,0:T(8,128)S(1)}, bf16[256,2048]{1,0:T(8,128)(2,1)S(1)}, bf16[256,2048]{1,0:T(8,128)(2,1)S(1)...) custom-call(s32[6]{0:T(128)S(1)} %stack.39.info, bf16[256,2048]{1,0:T(8,128)(2,1)} %q.3, ...), custom_call_target="tpu_custom_call" | custom-call | flops 1 | bytes 1 | tf_op jit(solution)/shard_map/second/pallas_call | solution.py:176
  11.2 0.1 collective-permute-start.1
  11.2 2.4 %local.2 = (f32[256,512]{1,0:T(8,128)S(1)}, f32[256,512]{1,0:T(8,128)S(1)}, f32[256,512]{1,0:T(8,128)S(1)}, f32[256,512]{1,0:T(8,128)S(1)}, f32[4,128,128]{2,1,0:T(8,128)S(1)}) custom-call(s32[6]{0:T(128)S(1)} %stack.39.info, bf16[256,2048]{1,0:T(8,128)(2,1)S(1)} %get-tuple-element.61.q.refs_0_, bf16[256,2048]{1,0:T(8,128)(2,1)S(1)} %get-tuple-element.62.k.refs_1_, ...), custom_call_target="tpu_custom_call" | custom-call | flops 1 | bytes 1 | tf_op jit(solution)/shard_map/local/pallas_call | solution.py:223
  13.6 0.9 %collective-permute-done.3.refs_5_ = f32[4,128,128]{2,1,0:T(8,128)S(1)} collective-permute-done((f32[4,128,128]{2,1,0:T(8,128)S(1)}, f32[4,128,128]{2,1,0:T(8,128)S(1)}, u32[]{:S(2)}, u32[]{:S(2)}) %collective-permute-start.3) | collective-permute-done | bytes 262176 | tf_op jit(solution)/shard_map/ppermute | solution.py:376
  14.6 1.9 %collective-permute-start.5 = (f32[4,128,128]{2,1,0:T(8,128)S(1)}, f32[4,128,128]{2,1,0:T(8,128)S(1)}, u32[]{:S(2)}, u32[]{:S(2)}) collective-permute-start(f32[4,128,128]{2,1,0:T(8,128)S(1)} %get-tuple-element.79), channel_id=1, source_target_pairs={{0,4},{1,5},{2,6},{3,7},{4,0},{5,1},{6,2},{7,3},{8,12},{9,13},{10,... | collective-permute-start | bytes 786440 | tf_op jit(solution)/shard_map/ppermute | solution.py:376
  16.6 1.5 %collective-permute-start.4 = (f32[4,128,128]{2,1,0:T(8,128)S(1)}, f32[4,128,128]{2,1,0:T(8,128)S(1)}, u32[]{:S(2)}, u32[]{:S(2)}) collective-permute-start(f32[4,128,128]{2,1,0:T(8,128)S(1)} %slice_add_fusion.2.refs_0_), channel_id=1, source_target_pairs={{0,2},{1,3},{2,0},{3,1},{4,6},{5,7},{6,4},{7,5},{8,10},{9,11},{10,... | collective-permute-start | bytes 786440 | tf_op jit(solution)/shard_map/ppermute | solution.py:376
  18.1 5.8 %local.3 = (f32[256,512]{1,0:T(8,128)S(1)}, f32[256,512]{1,0:T(8,128)S(1)}, f32[256,512]{1,0:T(8,128)S(1)}, f32[256,512]{1,0:T(8,128)S(1)}, f32[256,512]{1,0:T(8...) custom-call(s32[6]{0:T(128)S(1)} %stack.39.info, ...), custom_call_target="tpu_custom_call" | custom-call | flops 1 | bytes 1 | tf_op jit(solution)/shard_map/local/pallas_call | solution.py:223
  24.0 0.1 add_select_fusion
  24.0 0.1 collective-permute-start.6
  24.1 0.7 %prepare.2 = (f32[4,128,128]{2,1,0:T(8,128)S(1)}, f32[4,128,128]{2,1,0:T(8,128)S(1)}, f32[4,128,128]{2,1,0:T(8,128)S(1)}, f32[4,128,128]{2,1,0:T(8,128)S(1)}, f32[4,128,128]{2,1,0:T(8,128)S(1)}) custom-call(s32[6]{0:T(128)S(1)} %stack.39.info, f32[4,128,128]{2,1,0:T(8,128)S(1)} %collective-permute-done.5.refs_0_, f32[8,128,128]{2,1,0:T(8,128)S(1)} %own.1.refs_1_, ...), custom_call_target="tpu_custom_call" | custom-call | flops 1 | bytes 1 | tf_op jit(solution)/shard_map/prepare/pallas_call | solution.py:364
  24.8 0.6 %collective-permute-start.12 = (f32[4,128,128]{2,1,0:T(8,128)S(1)}, f32[4,128,128]{2,1,0:T(8,128)S(1)}, u32[]{:S(2)}, u32[]{:S(2)}) collective-permute-start(f32[4,128,128]{2,1,0:T(8,128)S(1)} %get-tuple-element.95), channel_id=1, source_target_pairs={{0,1},{1,0},{2,3},{3,2},{4,5},{5,4},{6,7},{7,6},{8,9},{9,8},{10,11... | collective-permute-start | bytes 786440 | tf_op jit(solution)/shard_map/ppermute | solution.py:376
  25.4 1.3 %collective-permute-start.11 = (f32[4,128,128]{2,1,0:T(8,128)S(1)}, f32[4,128,128]{2,1,0:T(8,128)S(1)}, u32[]{:S(2)}, u32[]{:S(2)}) collective-permute-start(f32[4,128,128]{2,1,0:T(8,128)S(1)} %get-tuple-element.80.refs_10_.refs_14_), channel_id=1, source_target_pairs={{0,2},{1,3},{2,0},{3,1},{4,6},{5,7},{6,4},{7,5},{8,10},{9,11},{10,... | collective-permute-start | bytes 786440 | tf_op jit(solution)/shard_map/ppermute | solution.py:376
  26.7 0.7 %prepare.3 = (f32[4,128,128]{2,1,0:T(8,128)S(1)}, f32[4,128,128]{2,1,0:T(8,128)S(1)}, f32[4,128,128]{2,1,0:T(8,128)S(1)}, f32[4,128,128]{2,1,0:T(8,128)S(1)}, f32[4,128,128]{2,1,0:T(8,128)S(1)}) custom-call(s32[6]{0:T(128)S(1)} %stack.39.info, f32[4,128,128]{2,1,0:T(8,128)S(1)} %collective-permute-done.5.refs_0_, f32[8,128,128]{2,1,0:T(8,128)S(1)} %own.1.refs_1_, ...), custom_call_target="tpu_custom_call" | custom-call | flops 1 | bytes 1 | tf_op jit(solution)/shard_map/prepare/pallas_call | solution.py:364
  27.4 5.0 %collective-permute-start.7 = (f32[4,128,128]{2,1,0:T(8,128)S(1)}, f32[4,128,128]{2,1,0:T(8,128)S(1)}, u32[]{:S(2)}, u32[]{:S(2)}) collective-permute-start(f32[4,128,128]{2,1,0:T(8,128)S(1)} %collective-permute-done.6), channel_id=1, source_target_pairs={{0,4},{1,5},{2,6},{3,7},{4,0},{5,1},{6,2},{7,3},{8,12},{9,13},{10,... | collective-permute-start | bytes 786440 | tf_op jit(solution)/shard_map/ppermute | solution.py:376
  32.4 1.9 %apply.4 = (bf16[256,2048]{1,0:T(8,128)(2,1)}, bf16[256,2048]{1,0:T(8,128)(2,1)}, bf16[256,2048]{1,0:T(8,128)(2,1)}, bf16[256,2048]{1,0:T(8,128)(2,1)}, f32[4,128,128]{2,1,0:T(8,128)S(1)}) custom-call(s32[6]{0:T(128)S(1)} %stack.39.info, bf16[256,2048]{1,0:T(8,128)(2,1)S(1)} %get-tuple-element.61.q.refs_0_, ...), custom_call_target="tpu_custom_call" | custom-call | flops 1 | bytes 1 | tf_op jit(solution)/shard_map/apply/pallas_call | solution.py:315
  34.3 0.1 fusion.2
  34.5 2.4 %collective-permute-done.7 = f32[4,128,128]{2,1,0:T(8,128)S(1)} collective-permute-done((f32[4,128,128]{2,1,0:T(8,128)S(1)}, f32[4,128,128]{2,1,0:T(8,128)S(1)}, u32[]{:S(2)}, u32[]{:S(2)}) %collective-permute-start.7) | collective-permute-done | bytes 262176 | tf_op jit(solution)/shard_map/ppermute | solution.py:376
  37.0 0.8 %collective-permute-start.8 = (f32[4,128,128]{2,1,0:T(8,128)S(1)}, f32[4,128,128]{2,1,0:T(8,128)S(1)}, u32[]{:S(2)}, u32[]{:S(2)}) collective-permute-start(f32[4,128,128]{2,1,0:T(8,128)S(1)} %get-tuple-element.112.refs_18_), channel_id=1, source_target_pairs={{0,2},{1,3},{2,0},{3,1},{4,6},{5,7},{6,4},{7,5},{8,10},{9,11},{10,... | collective-permute-start | bytes 786440 | tf_op jit(solution)/shard_map/ppermute | solution.py:376
  37.8 0.1 collective-permute-start.10
  37.8 0.5 %collective-permute-start.9 = (f32[2,128,128]{2,1,0:T(8,128)S(1)}, f32[2,128,128]{2,1,0:T(8,128)S(1)}, u32[]{:S(2)}, u32[]{:S(2)}) collective-permute-start(f32[2,128,128]{2,1,0:T(8,128)S(1)} %get-tuple-element.119), channel_id=1, source_target_pairs={{0,1},{1,0},{2,3},{3,2},{4,5},{5,4},{6,7},{7,6},{8,9},{9,8},{10,11... | collective-permute-start | bytes 393224 | tf_op jit(solution)/shard_map/ppermute | solution.py:376
  38.4 1.9 %apply.5 = (bf16[256,2048]{1,0:T(8,128)(2,1)}, bf16[256,2048]{1,0:T(8,128)(2,1)}, bf16[256,2048]{1,0:T(8,128)(2,1)}, bf16[256,2048]{1,0:T(8,128)(2,1)}) custom-call(s32[6]{0:T(128)S(1)} %stack.39.info, bf16[256,2048]{1,0:T(8,128)(2,1)S(1)} %get-tuple-element.61.q.refs_0_, ...), custom_call_target="tpu_custom_call", output_to_operand_aliasing={{0}: (15, {}), {1}: (16, {}), {2}: (17, {}), {3}: (18, {})} | custom-call | flops 1 | bytes 1 | tf_op jit(solution)/shard_map/apply/pallas_call | solution.py:315
  40.3 1.8 %apply.6 = (bf16[256,2048]{1,0:T(8,128)(2,1)}, bf16[256,2048]{1,0:T(8,128)(2,1)}, bf16[256,2048]{1,0:T(8,128)(2,1)}, bf16[256,2048]{1,0:T(8,128)(2,1)}, f32[4,128,128]{2,1,0:T(8,128)S(1)}) custom-call(s32[6]{0:T(128)S(1)} %stack.39.info, ...), custom_call_target="tpu_custom_call", output_to_operand_aliasing={{0}: (17, {}), {1}: (18, {}), {2}: (19, {}), {3}: (20, {})} | custom-call | flops 1 | bytes 1 | tf_op jit(solution)/shard_map/apply/pallas_call | solution.py:315
  42.1 1.3 %collective-permute-done.8 = f32[4,128,128]{2,1,0:T(8,128)S(1)} collective-permute-done((f32[4,128,128]{2,1,0:T(8,128)S(1)}, f32[4,128,128]{2,1,0:T(8,128)S(1)}, u32[]{:S(2)}, u32[]{:S(2)}) %collective-permute-start.8) | collective-permute-done | bytes 262176 | tf_op jit(solution)/shard_map/ppermute | solution.py:376
  43.5 0.1 collective-permute-start.14
  43.5 1.5 %collective-permute-done.14.refs_13_ = f32[4,128,128]{2,1,0:T(8,128)S(1)} collective-permute-done((f32[4,128,128]{2,1,0:T(8,128)S(1)}, f32[4,128,128]{2,1,0:T(8,128)S(1)}, u32[]{:S(2)}, u32[]{:S(2)}) %collective-permute-start.14) | collective-permute-done | bytes 262176 | tf_op jit(solution)/shard_map/ppermute | solution.py:376
  45.1 1.9 %apply.7 = (bf16[256,2048]{1,0:T(8,128)(2,1)}, bf16[256,2048]{1,0:T(8,128)(2,1)}, bf16[256,2048]{1,0:T(8,128)(2,1)}, bf16[256,2048]{1,0:T(8,128)(2,1)}) custom-call(s32[6]{0:T(128)S(1)} %stack.39.info, bf16[256,2048]{1,0:T(8,128)(2,1)S(1)} %get-tuple-element.61.q.refs_0_, ...), custom_call_target="tpu_custom_call", output_to_operand_aliasing={{0}: (15, {}), {1}: (16, {}), {2}: (17, {}), {3}: (18, {})} | custom-call | flops 1 | bytes 1 | tf_op jit(solution)/shard_map/apply/pallas_call | solution.py:315
  (18 shorter events, 0.4 us)
Async XLA Ops:
  3.2 1.7 %collective-permute-start = (f32[4,128,128]{2,1,0:T(8,128)S(1)}, f32[4,128,128]{2,1,0:T(8,128)S(1)}, u32[]{:S(2)}, u32[]{:S(2)}) collective-permute-start(f32[4,128,128]{2,1,0:T(8,128)S(1)} %get-tuple-element.60), channel_id=1, source_target_pairs={{0,1},{1,0},{2,3},{3,2},{4,5},{5,4},{6,7},{7,6},{8,9},{9,8},{10,11... | collective-permute-start | bytes 786440 | tf_op jit(solution)/shard_map/ppermute | solution.py:376
  3.8 9.9 %collective-permute-start.2 = (f32[4,128,128]{2,1,0:T(8,128)S(1)}, f32[4,128,128]{2,1,0:T(8,128)S(1)}, u32[]{:S(2)}, u32[]{:S(2)}) collective-permute-start(f32[4,128,128]{2,1,0:T(8,128)S(1)} %get-tuple-element.67), channel_id=1, source_target_pairs={{0,1},{1,0},{2,3},{3,2},{4,5},{5,4},{6,7},{7,6},{8,9},{9,8},{10,11... | collective-permute-start | bytes 786440 | tf_op jit(solution)/shard_map/ppermute | solution.py:376
  5.0 9.6 %collective-permute-start.3 = (f32[4,128,128]{2,1,0:T(8,128)S(1)}, f32[4,128,128]{2,1,0:T(8,128)S(1)}, u32[]{:S(2)}, u32[]{:S(2)}) collective-permute-start(f32[4,128,128]{2,1,0:T(8,128)S(1)} %slice_add_fusion.3.refs_0_), channel_id=1, source_target_pairs={{0,2},{1,3},{2,0},{3,1},{4,6},{5,7},{6,4},{7,5},{8,10},{9,11},{10,... | collective-permute-start | bytes 786440 | tf_op jit(solution)/shard_map/ppermute | solution.py:376
  11.2 3.4 %collective-permute-start.1 = (f32[8,128,128]{2,1,0:T(8,128)S(1)}, f32[8,128,128]{2,1,0:T(8,128)S(1)}, u32[]{:S(2)}, u32[]{:S(2)}) collective-permute-start(f32[8,128,128]{2,1,0:T(8,128)S(1)} %get-tuple-element.66), channel_id=1, source_target_pairs={{0,1},{1,0},{2,3},{3,2},{4,5},{5,4},{6,7},{7,6},{8,9},{9,8},{10,11... | collective-permute-start | bytes 1572872 | tf_op jit(solution)/shard_map/ppermute | solution.py:376
  14.6 9.3 %collective-permute-start.5 = (f32[4,128,128]{2,1,0:T(8,128)S(1)}, f32[4,128,128]{2,1,0:T(8,128)S(1)}, u32[]{:S(2)}, u32[]{:S(2)}) collective-permute-start(f32[4,128,128]{2,1,0:T(8,128)S(1)} %get-tuple-element.79), channel_id=1, source_target_pairs={{0,4},{1,5},{2,6},{3,7},{4,0},{5,1},{6,2},{7,3},{8,12},{9,13},{10,... | collective-permute-start | bytes 786440 | tf_op jit(solution)/shard_map/ppermute | solution.py:376
  16.6 7.4 %collective-permute-start.4 = (f32[4,128,128]{2,1,0:T(8,128)S(1)}, f32[4,128,128]{2,1,0:T(8,128)S(1)}, u32[]{:S(2)}, u32[]{:S(2)}) collective-permute-start(f32[4,128,128]{2,1,0:T(8,128)S(1)} %slice_add_fusion.2.refs_0_), channel_id=1, source_target_pairs={{0,2},{1,3},{2,0},{3,1},{4,6},{5,7},{6,4},{7,5},{8,10},{9,11},{10,... | collective-permute-start | bytes 786440 | tf_op jit(solution)/shard_map/ppermute | solution.py:376
  24.0 3.4 %collective-permute-start.6 = (f32[4,128,128]{2,1,0:T(8,128)S(1)}, f32[4,128,128]{2,1,0:T(8,128)S(1)}, u32[]{:S(2)}, u32[]{:S(2)}) collective-permute-start(f32[4,128,128]{2,1,0:T(8,128)S(1)} %get-tuple-element.114), channel_id=1, source_target_pairs={{4,8},{5,9},{6,10},{7,11},{8,4},{9,5},{10,6},{11,7},{0,1},{1,0},{2... | collective-permute-start | bytes 786440 | tf_op jit(solution)/shard_map/ppermute | solution.py:376
  24.8 7.6 %collective-permute-start.12 = (f32[4,128,128]{2,1,0:T(8,128)S(1)}, f32[4,128,128]{2,1,0:T(8,128)S(1)}, u32[]{:S(2)}, u32[]{:S(2)}) collective-permute-start(f32[4,128,128]{2,1,0:T(8,128)S(1)} %get-tuple-element.95), channel_id=1, source_target_pairs={{0,1},{1,0},{2,3},{3,2},{4,5},{5,4},{6,7},{7,6},{8,9},{9,8},{10,11... | collective-permute-start | bytes 786440 | tf_op jit(solution)/shard_map/ppermute | solution.py:376
  25.4 8.9 %collective-permute-start.11 = (f32[4,128,128]{2,1,0:T(8,128)S(1)}, f32[4,128,128]{2,1,0:T(8,128)S(1)}, u32[]{:S(2)}, u32[]{:S(2)}) collective-permute-start(f32[4,128,128]{2,1,0:T(8,128)S(1)} %get-tuple-element.80.refs_10_.refs_14_), channel_id=1, source_target_pairs={{0,2},{1,3},{2,0},{3,1},{4,6},{5,7},{6,4},{7,5},{8,10},{9,11},{10,... | collective-permute-start | bytes 786440 | tf_op jit(solution)/shard_map/ppermute | solution.py:376
  27.4 9.5 %collective-permute-start.7 = (f32[4,128,128]{2,1,0:T(8,128)S(1)}, f32[4,128,128]{2,1,0:T(8,128)S(1)}, u32[]{:S(2)}, u32[]{:S(2)}) collective-permute-start(f32[4,128,128]{2,1,0:T(8,128)S(1)} %collective-permute-done.6), channel_id=1, source_target_pairs={{0,4},{1,5},{2,6},{3,7},{4,0},{5,1},{6,2},{7,3},{8,12},{9,13},{10,... | collective-permute-start | bytes 786440 | tf_op jit(solution)/shard_map/ppermute | solution.py:376
  34.4 3.9 %collective-permute-start.13 = (f32[4,128,128]{2,1,0:T(8,128)S(1)}, f32[4,128,128]{2,1,0:T(8,128)S(1)}, u32[]{:S(2)}, u32[]{:S(2)}) collective-permute-start(f32[4,128,128]{2,1,0:T(8,128)S(1)} %get-tuple-element.124), channel_id=1, source_target_pairs={{0,1},{1,0},{2,3},{3,2},{4,5},{5,4},{6,7},{7,6},{8,9},{9,8},{10,11... | collective-permute-start | bytes 786440 | tf_op jit(solution)/shard_map/ppermute | solution.py:376
  37.0 6.4 %collective-permute-start.8 = (f32[4,128,128]{2,1,0:T(8,128)S(1)}, f32[4,128,128]{2,1,0:T(8,128)S(1)}, u32[]{:S(2)}, u32[]{:S(2)}) collective-permute-start(f32[4,128,128]{2,1,0:T(8,128)S(1)} %get-tuple-element.112.refs_18_), channel_id=1, source_target_pairs={{0,2},{1,3},{2,0},{3,1},{4,6},{5,7},{6,4},{7,5},{8,10},{9,11},{10,... | collective-permute-start | bytes 786440 | tf_op jit(solution)/shard_map/ppermute | solution.py:376
  37.8 2.5 %collective-permute-start.10 = (f32[2,128,128]{2,1,0:T(8,128)S(1)}, f32[2,128,128]{2,1,0:T(8,128)S(1)}, u32[]{:S(2)}, u32[]{:S(2)}) collective-permute-start(f32[2,128,128]{2,1,0:T(8,128)S(1)} %get-tuple-element.118), channel_id=1, source_target_pairs={{0,1},{1,0},{2,3},{3,2},{4,5},{5,4},{6,7},{7,6},{8,9},{9,8},{10,11... | collective-permute-start | bytes 393224 | tf_op jit(solution)/shard_map/ppermute | solution.py:376
  37.8 2.4 %collective-permute-start.9 = (f32[2,128,128]{2,1,0:T(8,128)S(1)}, f32[2,128,128]{2,1,0:T(8,128)S(1)}, u32[]{:S(2)}, u32[]{:S(2)}) collective-permute-start(f32[2,128,128]{2,1,0:T(8,128)S(1)} %get-tuple-element.119), channel_id=1, source_target_pairs={{0,1},{1,0},{2,3},{3,2},{4,5},{5,4},{6,7},{7,6},{8,9},{9,8},{10,11... | collective-permute-start | bytes 393224 | tf_op jit(solution)/shard_map/ppermute | solution.py:376
  43.5 1.6 %collective-permute-start.14 = (f32[4,128,128]{2,1,0:T(8,128)S(1)}, f32[4,128,128]{2,1,0:T(8,128)S(1)}, u32[]{:S(2)}, u32[]{:S(2)}) collective-permute-start(f32[4,128,128]{2,1,0:T(8,128)S(1)} %get-tuple-element.122), channel_id=1, source_target_pairs={{0,1},{1,0},{2,3},{3,2},{4,5},{5,4},{6,7},{7,6},{8,9},{9,8},{10,11... | collective-permute-start | bytes 786440 | tf_op jit(solution)/shard_map/ppermute | solution.py:376

commit v8 on v7

--- a/solution.py
+++ b/solution.py
@@ -105,7 +105,7 @@
 def first_state(info, args):
     count, width = args[0].shape
     heads = width // DH
-    rows = count // 4
+    rows = count // 1
     return pl.pallas_call(
         functools.partial(first_kernel, heads // 4, rows),
         out_shape=[jax.ShapeDtypeStruct((heads // 4, DH, DH), F32)] * 2
@@ -172,7 +172,7 @@
 def second_states(info, args, after):
     count, width = args[0].shape
     heads = width // DH
-    rows = count // 4
+    rows = count // 1
     return pl.pallas_call(
         functools.partial(second_kernel, heads // 4, rows, len(after)),
         out_shape=[jax.ShapeDtypeStruct((heads // 2, DH, DH), F32)] * 2
@@ -190,6 +190,7 @@
     *parts, flag = refs[n_after:]
     flag[...] = jnp.full(flag.shape, jnp.where(info[INNER] == 1, mark, 0.0), F32)
     count = q.shape[0]
+    half = count // 2
     two = 2
     scale = rows_scale(info[START], count)
     lower = lax.broadcasted_iota(jnp.int32, (count, count), 1) <= lax.broadcasted_iota(
@@ -206,12 +207,19 @@
                 cols = pl.ds(pl.multiple_of((first + g * two + i) * DH, DH), DH)
                 qh, kh, vh = q[:, cols], k[:, cols], v[:, cols]
                 ph = (d[:, cols].astype(F32) * scale).astype(BF16)
-                scores = jnp.where(lower, dot(qh, kh, 1, 1), 0.0).astype(BF16)
-                back = jnp.where(lower, dot(ph, vh, 1, 1), 0.0).astype(BF16)
-                o_ref[:, to] = dot(scores, vh, 1, 0)
-                dq_ref[:, to] = dot(back, kh, 1, 0)
-                dk_ref[:, to] = dot(back, qh, 0, 0)
-                dv_ref[:, to] = dot(scores, ph, 0, 0)
+                top, bottom = slice(0, half), slice(half, count)
+                s0 = jnp.where(lower[top, top], dot(qh[top], kh[top], 1, 1), 0.0).astype(BF16)
+                s1 = jnp.where(lower[bottom], dot(qh[bottom], kh, 1, 1), 0.0).astype(BF16)
+                b0 = jnp.where(lower[top, top], dot(ph[top], vh[top], 1, 1), 0.0).astype(BF16)
+                b1 = jnp.where(lower[bottom], dot(ph[bottom], vh, 1, 1), 0.0).astype(BF16)
+                o_ref[top, to] = dot(s0, vh[top], 1, 0)
+                o_ref[bottom, to] = dot(s1, vh, 1, 0)
+                dq_ref[top, to] = dot(b0, kh[top], 1, 0)
+                dq_ref[bottom, to] = dot(b1, kh, 1, 0)
+                dk_ref[top, to] = dot(b0, qh[top], 0, 0) + dot(b1[:, top], qh[bottom], 0, 0)
+                dk_ref[bottom, to] = dot(b1[:, bottom], qh[bottom], 0, 0)
+                dv_ref[top, to] = dot(s0, ph[top], 0, 0) + dot(s1[:, top], ph[bottom], 0, 0)
+                dv_ref[bottom, to] = dot(s1[:, bottom], ph[bottom], 0, 0)
             return carry
 
         lax.fori_loop(0, quarter // two, step, 0)

time: 47.1 us -> 46.8 us (level)
  Pallas kernels: 23.9 us -> 22.9 us
  waiting for transfers between devices: 6.15 us -> 7.12 us
    ppermute x15, waiting for transfers between devices: 6.15 us -> 7.12 us  [send(): return lax.ppermute(array, 'seq', pairs)]
  transfers between devices with their start and end apart: 15 -> 15, of which waited for: 5 -> 6; matrix products, arithmetic and copies ran while one was open for 1% -> 1% of each run, Pallas kernels for 42% -> 40%
where the time goes in v8:
time: 46.8 us; the launch traced here: 46.7 us
  Pallas kernels  22.9 us (49%)
  starting transfers between devices  15.2 us (32%)
  waiting for transfers between devices  7.12 us (15%)
  between operations  0.9 us (2%)
    ppermute x15, starting transfers between devices, send(): return lax.ppermute(array, 'seq', pairs)  15.2 us
    pallas_call x2, Pallas kernels, local_part(): pl.pallas_call(functools.partial(local_kernel, kinds, quarter, mark, len(...  7.78 us
    pallas_call x4, Pallas kernels, apply_states(): pl.pallas_call(functools.partial(apply_kernel, early, kinds, len(arrays)...  7.5 us
    ppermute x15, waiting for transfers between devices, send(): return lax.ppermute(array, 'seq', pairs)  7.12 us
    pallas_call x1, Pallas kernels, second_states(): pl.pallas_call(functools.partial(second_kernel, heads // 4, rows, len(aft...  2.89 us
    pallas_call x1, Pallas kernels, first_state(): pl.pallas_call(functools.partial(first_kernel, heads // 4, rows), out_sha...  2.26 us
    pallas_call x2, Pallas kernels, prepare(): pl.pallas_call(functools.partial(prepare_kernel, early, len(after)), out_...  1.44 us
    pallas_call x1, Pallas kernels, own_state(): pl.pallas_call(functools.partial(own_kernel, heads // 4), out_shape=jax.S...  1.02 us
  transfers between devices with their start and end apart: 15, of which 6 were waited for; matrix products, arithmetic and copies ran while one was open for 1% of the time, Pallas kernels for 40%

profile of v8, /device:TPU:0, one launch (start us, length us, event | category | flops | bytes accessed | tf_op | source)
XLA Modules:
  0.0 46.7 jit_solution(6366314492220314599)
XLA Ops:
  0.7 0.1 stack.39.info
  0.8 2.3 %first.1 = (f32[4,128,128]{2,1,0:T(8,128)S(1)}, f32[4,128,128]{2,1,0:T(8,128)S(1)}, bf16[256,2048]{1,0:T(8,128)(2,1)S(1)}, bf16[256,2048]{1,0:T(8,128)(2,1)S(1)}) custom-call(s32[6]{0:T(128)S(1)} %stack.39.info, bf16[256,2048]{1,0:T(8,128)(2,1)} %q.3, bf16[256,2048]{1,0:T(8,128)(2,1)} %k.3, bf16[256,2048]{1,0:T(8,128)(2,1)} %v.3, bf16[256,2048]{1,0:T(8,128)(2,1)} %d.3), custom_call_target="tpu_custom_call" | custom-call | flops 1 | bytes 1 | tf_op jit(solution)/shard_map/first/pallas_call | solution.py:109
  3.0 0.5 %collective-permute-start = (f32[4,128,128]{2,1,0:T(8,128)S(1)}, f32[4,128,128]{2,1,0:T(8,128)S(1)}, u32[]{:S(2)}, u32[]{:S(2)}) collective-permute-start(f32[4,128,128]{2,1,0:T(8,128)S(1)} %get-tuple-element.60), channel_id=1, source_target_pairs={{0,1},{1,0},{2,3},{3,2},{4,5},{5,4},{6,7},{7,6},{8,9},{9,8},{10,11... | collective-permute-start | bytes 786440 | tf_op jit(solution)/shard_map/ppermute | solution.py:384
  3.6 0.1 collective-permute-start.2
  3.6 1.0 %own.1.refs_1_ = f32[8,128,128]{2,1,0:T(8,128)S(1)} custom-call(s32[6]{0:T(128)S(1)} %stack.39.info, bf16[256,2048]{1,0:T(8,128)(2,1)S(1)} %get-tuple-element.58.left, bf16[256,2048]{1,0:T(8,128)(2,1)S(1)} %get-tuple-element.59.right), custom_call_target="tpu_custom_call" | custom-call | flops 1 | bytes 1 | tf_op jit(solution)/shard_map/own/pallas_call | solution.py:129
  4.8 3.0 %collective-permute-start.3 = (f32[4,128,128]{2,1,0:T(8,128)S(1)}, f32[4,128,128]{2,1,0:T(8,128)S(1)}, u32[]{:S(2)}, u32[]{:S(2)}) collective-permute-start(f32[4,128,128]{2,1,0:T(8,128)S(1)} %slice_add_fusion.3.refs_0_), channel_id=1, source_target_pairs={{0,2},{1,3},{2,0},{3,1},{4,6},{5,7},{6,4},{7,5},{8,10},{9,11},{10,... | collective-permute-start | bytes 786440 | tf_op jit(solution)/shard_map/ppermute | solution.py:384
  7.7 2.9 %second.1 = (f32[8,128,128]{2,1,0:T(8,128)S(1)}, f32[8,128,128]{2,1,0:T(8,128)S(1)}, bf16[256,2048]{1,0:T(8,128)(2,1)S(1)}, bf16[256,2048]{1,0:T(8,128)(2,1)S(1)...) custom-call(s32[6]{0:T(128)S(1)} %stack.39.info, bf16[256,2048]{1,0:T(8,128)(2,1)} %q.3, ...), custom_call_target="tpu_custom_call" | custom-call | flops 1 | bytes 1 | tf_op jit(solution)/shard_map/second/pallas_call | solution.py:176
  10.6 0.1 collective-permute-start.1
  10.7 2.3 %local.2 = (f32[256,512]{1,0:T(8,128)S(1)}, f32[256,512]{1,0:T(8,128)S(1)}, f32[256,512]{1,0:T(8,128)S(1)}, f32[256,512]{1,0:T(8,128)S(1)}, f32[4,128,128]{2,1,0:T(8,128)S(1)}) custom-call(s32[6]{0:T(128)S(1)} %stack.39.info, bf16[256,2048]{1,0:T(8,128)(2,1)S(1)} %get-tuple-element.61.q.refs_0_, bf16[256,2048]{1,0:T(8,128)(2,1)S(1)} %get-tuple-element.62.k.refs_1_, ...), custom_call_target="tpu_custom_call" | custom-call | flops 1 | bytes 1 | tf_op jit(solution)/shard_map/local/pallas_call | solution.py:231
  13.0 1.3 %collective-permute-done.3.refs_5_ = f32[4,128,128]{2,1,0:T(8,128)S(1)} collective-permute-done((f32[4,128,128]{2,1,0:T(8,128)S(1)}, f32[4,128,128]{2,1,0:T(8,128)S(1)}, u32[]{:S(2)}, u32[]{:S(2)}) %collective-permute-start.3) | collective-permute-done | bytes 262176 | tf_op jit(solution)/shard_map/ppermute | solution.py:384
  14.4 1.9 %collective-permute-start.5 = (f32[4,128,128]{2,1,0:T(8,128)S(1)}, f32[4,128,128]{2,1,0:T(8,128)S(1)}, u32[]{:S(2)}, u32[]{:S(2)}) collective-permute-start(f32[4,128,128]{2,1,0:T(8,128)S(1)} %get-tuple-element.79), channel_id=1, source_target_pairs={{0,4},{1,5},{2,6},{3,7},{4,0},{5,1},{6,2},{7,3},{8,12},{9,13},{10,... | collective-permute-start | bytes 786440 | tf_op jit(solution)/shard_map/ppermute | solution.py:384
  16.4 1.5 %collective-permute-start.4 = (f32[4,128,128]{2,1,0:T(8,128)S(1)}, f32[4,128,128]{2,1,0:T(8,128)S(1)}, u32[]{:S(2)}, u32[]{:S(2)}) collective-permute-start(f32[4,128,128]{2,1,0:T(8,128)S(1)} %slice_add_fusion.2.refs_0_), channel_id=1, source_target_pairs={{0,2},{1,3},{2,0},{3,1},{4,6},{5,7},{6,4},{7,5},{8,10},{9,11},{10,... | collective-permute-start | bytes 786440 | tf_op jit(solution)/shard_map/ppermute | solution.py:384
  17.9 5.5 %local.3 = (f32[256,512]{1,0:T(8,128)S(1)}, f32[256,512]{1,0:T(8,128)S(1)}, f32[256,512]{1,0:T(8,128)S(1)}, f32[256,512]{1,0:T(8,128)S(1)}, f32[256,512]{1,0:T(8...) custom-call(s32[6]{0:T(128)S(1)} %stack.39.info, ...), custom_call_target="tpu_custom_call" | custom-call | flops 1 | bytes 1 | tf_op jit(solution)/shard_map/local/pallas_call | solution.py:231
  23.4 0.1 collective-permute-done.4.refs_9_
  23.6 0.1 collective-permute-start.6
  23.7 0.7 %prepare.2 = (f32[4,128,128]{2,1,0:T(8,128)S(1)}, f32[4,128,128]{2,1,0:T(8,128)S(1)}, f32[4,128,128]{2,1,0:T(8,128)S(1)}, f32[4,128,128]{2,1,0:T(8,128)S(1)}, f32[4,128,128]{2,1,0:T(8,128)S(1)}) custom-call(s32[6]{0:T(128)S(1)} %stack.39.info, f32[4,128,128]{2,1,0:T(8,128)S(1)} %collective-permute-done.5.refs_0_, f32[8,128,128]{2,1,0:T(8,128)S(1)} %own.1.refs_1_, ...), custom_call_target="tpu_custom_call" | custom-call | flops 1 | bytes 1 | tf_op jit(solution)/shard_map/prepare/pallas_call | solution.py:372
  24.4 0.6 %collective-permute-start.12 = (f32[4,128,128]{2,1,0:T(8,128)S(1)}, f32[4,128,128]{2,1,0:T(8,128)S(1)}, u32[]{:S(2)}, u32[]{:S(2)}) collective-permute-start(f32[4,128,128]{2,1,0:T(8,128)S(1)} %get-tuple-element.95), channel_id=1, source_target_pairs={{0,1},{1,0},{2,3},{3,2},{4,5},{5,4},{6,7},{7,6},{8,9},{9,8},{10,11... | collective-permute-start | bytes 786440 | tf_op jit(solution)/shard_map/ppermute | solution.py:384
  25.0 1.5 %collective-permute-start.11 = (f32[4,128,128]{2,1,0:T(8,128)S(1)}, f32[4,128,128]{2,1,0:T(8,128)S(1)}, u32[]{:S(2)}, u32[]{:S(2)}) collective-permute-start(f32[4,128,128]{2,1,0:T(8,128)S(1)} %get-tuple-element.80.refs_10_.refs_14_), channel_id=1, source_target_pairs={{0,2},{1,3},{2,0},{3,1},{4,6},{5,7},{6,4},{7,5},{8,10},{9,11},{10,... | collective-permute-start | bytes 786440 | tf_op jit(solution)/shard_map/ppermute | solution.py:384
  26.5 0.7 %prepare.3 = (f32[4,128,128]{2,1,0:T(8,128)S(1)}, f32[4,128,128]{2,1,0:T(8,128)S(1)}, f32[4,128,128]{2,1,0:T(8,128)S(1)}, f32[4,128,128]{2,1,0:T(8,128)S(1)}, f32[4,128,128]{2,1,0:T(8,128)S(1)}) custom-call(s32[6]{0:T(128)S(1)} %stack.39.info, f32[4,128,128]{2,1,0:T(8,128)S(1)} %collective-permute-done.5.refs_0_, f32[8,128,128]{2,1,0:T(8,128)S(1)} %own.1.refs_1_, ...), custom_call_target="tpu_custom_call" | custom-call | flops 1 | bytes 1 | tf_op jit(solution)/shard_map/prepare/pallas_call | solution.py:372
  27.2 4.7 %collective-permute-start.7 = (f32[4,128,128]{2,1,0:T(8,128)S(1)}, f32[4,128,128]{2,1,0:T(8,128)S(1)}, u32[]{:S(2)}, u32[]{:S(2)}) collective-permute-start(f32[4,128,128]{2,1,0:T(8,128)S(1)} %collective-permute-done.6), channel_id=1, source_target_pairs={{0,4},{1,5},{2,6},{3,7},{4,0},{5,1},{6,2},{7,3},{8,12},{9,13},{10,... | collective-permute-start | bytes 786440 | tf_op jit(solution)/shard_map/ppermute | solution.py:384
  31.9 1.9 %apply.4 = (bf16[256,2048]{1,0:T(8,128)(2,1)}, bf16[256,2048]{1,0:T(8,128)(2,1)}, bf16[256,2048]{1,0:T(8,128)(2,1)}, bf16[256,2048]{1,0:T(8,128)(2,1)}, f32[4,128,128]{2,1,0:T(8,128)S(1)}) custom-call(s32[6]{0:T(128)S(1)} %stack.39.info, bf16[256,2048]{1,0:T(8,128)(2,1)S(1)} %get-tuple-element.61.q.refs_0_, ...), custom_call_target="tpu_custom_call" | custom-call | flops 1 | bytes 1 | tf_op jit(solution)/shard_map/apply/pallas_call | solution.py:323
  33.8 0.1 fusion.2
  33.9 0.1 collective-permute-start.13
  34.0 2.7 %collective-permute-done.7 = f32[4,128,128]{2,1,0:T(8,128)S(1)} collective-permute-done((f32[4,128,128]{2,1,0:T(8,128)S(1)}, f32[4,128,128]{2,1,0:T(8,128)S(1)}, u32[]{:S(2)}, u32[]{:S(2)}) %collective-permute-start.7) | collective-permute-done | bytes 262176 | tf_op jit(solution)/shard_map/ppermute | solution.py:384
  36.7 0.6 %collective-permute-start.8 = (f32[4,128,128]{2,1,0:T(8,128)S(1)}, f32[4,128,128]{2,1,0:T(8,128)S(1)}, u32[]{:S(2)}, u32[]{:S(2)}) collective-permute-start(f32[4,128,128]{2,1,0:T(8,128)S(1)} %get-tuple-element.112.refs_18_), channel_id=1, source_target_pairs={{0,2},{1,3},{2,0},{3,1},{4,6},{5,7},{6,4},{7,5},{8,10},{9,11},{10,... | collective-permute-start | bytes 786440 | tf_op jit(solution)/shard_map/ppermute | solution.py:384
  37.4 0.1 collective-permute-start.10
  37.5 0.5 %collective-permute-start.9 = (f32[2,128,128]{2,1,0:T(8,128)S(1)}, f32[2,128,128]{2,1,0:T(8,128)S(1)}, u32[]{:S(2)}, u32[]{:S(2)}) collective-permute-start(f32[2,128,128]{2,1,0:T(8,128)S(1)} %get-tuple-element.119), channel_id=1, source_target_pairs={{0,1},{1,0},{2,3},{3,2},{4,5},{5,4},{6,7},{7,6},{8,9},{9,8},{10,11... | collective-permute-start | bytes 393224 | tf_op jit(solution)/shard_map/ppermute | solution.py:384
  38.0 1.9 %apply.5 = (bf16[256,2048]{1,0:T(8,128)(2,1)}, bf16[256,2048]{1,0:T(8,128)(2,1)}, bf16[256,2048]{1,0:T(8,128)(2,1)}, bf16[256,2048]{1,0:T(8,128)(2,1)}) custom-call(s32[6]{0:T(128)S(1)} %stack.39.info, bf16[256,2048]{1,0:T(8,128)(2,1)S(1)} %get-tuple-element.61.q.refs_0_, ...), custom_call_target="tpu_custom_call", output_to_operand_aliasing={{0}: (15, {}), {1}: (16, {}), {2}: (17, {}), {3}: (18, {})} | custom-call | flops 1 | bytes 1 | tf_op jit(solution)/shard_map/apply/pallas_call | solution.py:323
  39.9 1.8 %apply.6 = (bf16[256,2048]{1,0:T(8,128)(2,1)}, bf16[256,2048]{1,0:T(8,128)(2,1)}, bf16[256,2048]{1,0:T(8,128)(2,1)}, bf16[256,2048]{1,0:T(8,128)(2,1)}, f32[4,128,128]{2,1,0:T(8,128)S(1)}) custom-call(s32[6]{0:T(128)S(1)} %stack.39.info, ...), custom_call_target="tpu_custom_call", output_to_operand_aliasing={{0}: (17, {}), {1}: (18, {}), {2}: (19, {}), {3}: (20, {})} | custom-call | flops 1 | bytes 1 | tf_op jit(solution)/shard_map/apply/pallas_call | solution.py:323
  41.7 1.4 %collective-permute-done.8 = f32[4,128,128]{2,1,0:T(8,128)S(1)} collective-permute-done((f32[4,128,128]{2,1,0:T(8,128)S(1)}, f32[4,128,128]{2,1,0:T(8,128)S(1)}, u32[]{:S(2)}, u32[]{:S(2)}) %collective-permute-start.8) | collective-permute-done | bytes 262176 | tf_op jit(solution)/shard_map/ppermute | solution.py:384
  43.3 1.5 %collective-permute-done.14.refs_13_ = f32[4,128,128]{2,1,0:T(8,128)S(1)} collective-permute-done((f32[4,128,128]{2,1,0:T(8,128)S(1)}, f32[4,128,128]{2,1,0:T(8,128)S(1)}, u32[]{:S(2)}, u32[]{:S(2)}) %collective-permute-start.14) | collective-permute-done | bytes 262176 | tf_op jit(solution)/shard_map/ppermute | solution.py:384
  44.8 1.9 %apply.7 = (bf16[256,2048]{1,0:T(8,128)(2,1)}, bf16[256,2048]{1,0:T(8,128)(2,1)}, bf16[256,2048]{1,0:T(8,128)(2,1)}, bf16[256,2048]{1,0:T(8,128)(2,1)}) custom-call(s32[6]{0:T(128)S(1)} %stack.39.info, bf16[256,2048]{1,0:T(8,128)(2,1)S(1)} %get-tuple-element.61.q.refs_0_, ...), custom_call_target="tpu_custom_call", output_to_operand_aliasing={{0}: (15, {}), {1}: (16, {}), {2}: (17, {}), {3}: (18, {})} | custom-call | flops 1 | bytes 1 | tf_op jit(solution)/shard_map/apply/pallas_call | solution.py:323
  (18 shorter events, 0.5 us)
Async XLA Ops:
  3.0 1.7 %collective-permute-start = (f32[4,128,128]{2,1,0:T(8,128)S(1)}, f32[4,128,128]{2,1,0:T(8,128)S(1)}, u32[]{:S(2)}, u32[]{:S(2)}) collective-permute-start(f32[4,128,128]{2,1,0:T(8,128)S(1)} %get-tuple-element.60), channel_id=1, source_target_pairs={{0,1},{1,0},{2,3},{3,2},{4,5},{5,4},{6,7},{7,6},{8,9},{9,8},{10,11... | collective-permute-start | bytes 786440 | tf_op jit(solution)/shard_map/ppermute | solution.py:384
  3.6 9.4 %collective-permute-start.2 = (f32[4,128,128]{2,1,0:T(8,128)S(1)}, f32[4,128,128]{2,1,0:T(8,128)S(1)}, u32[]{:S(2)}, u32[]{:S(2)}) collective-permute-start(f32[4,128,128]{2,1,0:T(8,128)S(1)} %get-tuple-element.67), channel_id=1, source_target_pairs={{0,1},{1,0},{2,3},{3,2},{4,5},{5,4},{6,7},{7,6},{8,9},{9,8},{10,11... | collective-permute-start | bytes 786440 | tf_op jit(solution)/shard_map/ppermute | solution.py:384
  4.8 9.6 %collective-permute-start.3 = (f32[4,128,128]{2,1,0:T(8,128)S(1)}, f32[4,128,128]{2,1,0:T(8,128)S(1)}, u32[]{:S(2)}, u32[]{:S(2)}) collective-permute-start(f32[4,128,128]{2,1,0:T(8,128)S(1)} %slice_add_fusion.3.refs_0_), channel_id=1, source_target_pairs={{0,2},{1,3},{2,0},{3,1},{4,6},{5,7},{6,4},{7,5},{8,10},{9,11},{10,... | collective-permute-start | bytes 786440 | tf_op jit(solution)/shard_map/ppermute | solution.py:384
  10.6 3.8 %collective-permute-start.1 = (f32[8,128,128]{2,1,0:T(8,128)S(1)}, f32[8,128,128]{2,1,0:T(8,128)S(1)}, u32[]{:S(2)}, u32[]{:S(2)}) collective-permute-start(f32[8,128,128]{2,1,0:T(8,128)S(1)} %get-tuple-element.66), channel_id=1, source_target_pairs={{0,1},{1,0},{2,3},{3,2},{4,5},{5,4},{6,7},{7,6},{8,9},{9,8},{10,11... | collective-permute-start | bytes 1572872 | tf_op jit(solution)/shard_map/ppermute | solution.py:384
  14.4 9.0 %collective-permute-start.5 = (f32[4,128,128]{2,1,0:T(8,128)S(1)}, f32[4,128,128]{2,1,0:T(8,128)S(1)}, u32[]{:S(2)}, u32[]{:S(2)}) collective-permute-start(f32[4,128,128]{2,1,0:T(8,128)S(1)} %get-tuple-element.79), channel_id=1, source_target_pairs={{0,4},{1,5},{2,6},{3,7},{4,0},{5,1},{6,2},{7,3},{8,12},{9,13},{10,... | collective-permute-start | bytes 786440 | tf_op jit(solution)/shard_map/ppermute | solution.py:384
  16.4 7.2 %collective-permute-start.4 = (f32[4,128,128]{2,1,0:T(8,128)S(1)}, f32[4,128,128]{2,1,0:T(8,128)S(1)}, u32[]{:S(2)}, u32[]{:S(2)}) collective-permute-start(f32[4,128,128]{2,1,0:T(8,128)S(1)} %slice_add_fusion.2.refs_0_), channel_id=1, source_target_pairs={{0,2},{1,3},{2,0},{3,1},{4,6},{5,7},{6,4},{7,5},{8,10},{9,11},{10,... | collective-permute-start | bytes 786440 | tf_op jit(solution)/shard_map/ppermute | solution.py:384
  23.6 3.6 %collective-permute-start.6 = (f32[4,128,128]{2,1,0:T(8,128)S(1)}, f32[4,128,128]{2,1,0:T(8,128)S(1)}, u32[]{:S(2)}, u32[]{:S(2)}) collective-permute-start(f32[4,128,128]{2,1,0:T(8,128)S(1)} %get-tuple-element.114), channel_id=1, source_target_pairs={{4,8},{5,9},{6,10},{7,11},{8,4},{9,5},{10,6},{11,7},{0,1},{1,0},{2... | collective-permute-start | bytes 786440 | tf_op jit(solution)/shard_map/ppermute | solution.py:384
  24.4 7.5 %collective-permute-start.12 = (f32[4,128,128]{2,1,0:T(8,128)S(1)}, f32[4,128,128]{2,1,0:T(8,128)S(1)}, u32[]{:S(2)}, u32[]{:S(2)}) collective-permute-start(f32[4,128,128]{2,1,0:T(8,128)S(1)} %get-tuple-element.95), channel_id=1, source_target_pairs={{0,1},{1,0},{2,3},{3,2},{4,5},{5,4},{6,7},{7,6},{8,9},{9,8},{10,11... | collective-permute-start | bytes 786440 | tf_op jit(solution)/shard_map/ppermute | solution.py:384
  25.0 8.8 %collective-permute-start.11 = (f32[4,128,128]{2,1,0:T(8,128)S(1)}, f32[4,128,128]{2,1,0:T(8,128)S(1)}, u32[]{:S(2)}, u32[]{:S(2)}) collective-permute-start(f32[4,128,128]{2,1,0:T(8,128)S(1)} %get-tuple-element.80.refs_10_.refs_14_), channel_id=1, source_target_pairs={{0,2},{1,3},{2,0},{3,1},{4,6},{5,7},{6,4},{7,5},{8,10},{9,11},{10,... | collective-permute-start | bytes 786440 | tf_op jit(solution)/shard_map/ppermute | solution.py:384
  27.2 9.4 %collective-permute-start.7 = (f32[4,128,128]{2,1,0:T(8,128)S(1)}, f32[4,128,128]{2,1,0:T(8,128)S(1)}, u32[]{:S(2)}, u32[]{:S(2)}) collective-permute-start(f32[4,128,128]{2,1,0:T(8,128)S(1)} %collective-permute-done.6), channel_id=1, source_target_pairs={{0,4},{1,5},{2,6},{3,7},{4,0},{5,1},{6,2},{7,3},{8,12},{9,13},{10,... | collective-permute-start | bytes 786440 | tf_op jit(solution)/shard_map/ppermute | solution.py:384
  33.9 4.1 %collective-permute-start.13 = (f32[4,128,128]{2,1,0:T(8,128)S(1)}, f32[4,128,128]{2,1,0:T(8,128)S(1)}, u32[]{:S(2)}, u32[]{:S(2)}) collective-permute-start(f32[4,128,128]{2,1,0:T(8,128)S(1)} %get-tuple-element.124), channel_id=1, source_target_pairs={{0,1},{1,0},{2,3},{3,2},{4,5},{5,4},{6,7},{7,6},{8,9},{9,8},{10,11... | collective-permute-start | bytes 786440 | tf_op jit(solution)/shard_map/ppermute | solution.py:384
  36.7 6.4 %collective-permute-start.8 = (f32[4,128,128]{2,1,0:T(8,128)S(1)}, f32[4,128,128]{2,1,0:T(8,128)S(1)}, u32[]{:S(2)}, u32[]{:S(2)}) collective-permute-start(f32[4,128,128]{2,1,0:T(8,128)S(1)} %get-tuple-element.112.refs_18_), channel_id=1, source_target_pairs={{0,2},{1,3},{2,0},{3,1},{4,6},{5,7},{6,4},{7,5},{8,10},{9,11},{10,... | collective-permute-start | bytes 786440 | tf_op jit(solution)/shard_map/ppermute | solution.py:384
  37.4 2.5 %collective-permute-start.10 = (f32[2,128,128]{2,1,0:T(8,128)S(1)}, f32[2,128,128]{2,1,0:T(8,128)S(1)}, u32[]{:S(2)}, u32[]{:S(2)}) collective-permute-start(f32[2,128,128]{2,1,0:T(8,128)S(1)} %get-tuple-element.118), channel_id=1, source_target_pairs={{0,1},{1,0},{2,3},{3,2},{4,5},{5,4},{6,7},{7,6},{8,9},{9,8},{10,11... | collective-permute-start | bytes 393224 | tf_op jit(solution)/shard_map/ppermute | solution.py:384
  37.5 2.4 %collective-permute-start.9 = (f32[2,128,128]{2,1,0:T(8,128)S(1)}, f32[2,128,128]{2,1,0:T(8,128)S(1)}, u32[]{:S(2)}, u32[]{:S(2)}) collective-permute-start(f32[2,128,128]{2,1,0:T(8,128)S(1)} %get-tuple-element.119), channel_id=1, source_target_pairs={{0,1},{1,0},{2,3},{3,2},{4,5},{5,4},{6,7},{7,6},{8,9},{9,8},{10,11... | collective-permute-start | bytes 393224 | tf_op jit(solution)/shard_map/ppermute | solution.py:384
  43.2 1.6 %collective-permute-start.14 = (f32[4,128,128]{2,1,0:T(8,128)S(1)}, f32[4,128,128]{2,1,0:T(8,128)S(1)}, u32[]{:S(2)}, u32[]{:S(2)}) collective-permute-start(f32[4,128,128]{2,1,0:T(8,128)S(1)} %get-tuple-element.122), channel_id=1, source_target_pairs={{0,1},{1,0},{2,3},{3,2},{4,5},{5,4},{6,7},{7,6},{8,9},{9,8},{10,11... | collective-permute-start | bytes 786440 | tf_op jit(solution)/shard_map/ppermute | solution.py:384

commit v9 on v8

--- a/solution.py
+++ b/solution.py
@@ -41,7 +41,7 @@
     return pl.multiple_of(core * half, half)
 
 
-def state_products(is_kv, side, quarter, info, q, k, v, d, out):
+def state_products(is_kv, side, quarter, info, q, k, v, d, out, parts=(0, 1)):
     count = q.shape[0]
     pieces = out if isinstance(out, tuple) else (out,)
     each = pieces[0].shape[0]
@@ -51,7 +51,7 @@
 
     @pl.when(is_kv)
     def _():
-        for part in range(2):
+        for part in parts:
             head = first_head(info, side, part, quarter)
             for i in range(quarter):
                 cols = pl.ds(pl.multiple_of((head + i) * DH, DH), DH)
@@ -60,7 +60,7 @@
     @pl.when(jnp.logical_not(is_kv))
     def _():
         scale = rows_scale(info[START], count)
-        for part in range(2):
+        for part in parts:
             head = first_head(info, side, part, quarter)
             for i in range(quarter):
                 cols = pl.ds(pl.multiple_of((head + i) * DH, DH), DH)
@@ -68,11 +68,10 @@
                 at(part * quarter + i)[...] = dot(q[:, cols], scaled, 0, 0)
 
 
-def pair_copies(info, side, width, rows, sems, *pair):
-    half = width // 2
+def pair_copies(start, columns, rows, sems, *pair):
     for n, (there, here) in enumerate(pair):
         for step in range(there.shape[0] // rows):
-            at = pl.ds(step * rows, rows), pl.ds(half_cols(info, side, width), half)
+            at = pl.ds(step * rows, rows), pl.ds(start, columns)
             yield pltpu.make_async_copy(there.at[at], here.at[at], sems.at[n, step])
 
 
@@ -81,7 +80,11 @@
     is_kv = info[EVEN] == 1
 
     def copies(side, a, b):
-        return pair_copies(info, side, width, rows, sems.at[side], (a, left), (b, right))
+        start, columns = half_cols(info, side, width), width // 2
+        if side == 0:
+            columns = quarter * DH
+            start = pl.multiple_of(first_head(info, side, 1, quarter) * DH, columns)
+        return pair_copies(start, columns, rows, sems.at[side], (a, left), (b, right))
 
     @pl.when(is_kv)
     def _():
@@ -120,7 +123,7 @@
 
 
 def own_kernel(quarter, info, left, right, out):
-    state_products(info[EVEN] == 1, 0, quarter, info, left, left, right, right, out)
+    state_products(info[EVEN] == 1, 0, quarter, info, left, left, right, right, (out, out), (1,))
 
 
 def own_state(info, left, right):
@@ -128,7 +131,7 @@
     heads = width // DH
     return pl.pallas_call(
         functools.partial(own_kernel, heads // 4),
-        out_shape=jax.ShapeDtypeStruct((heads // 2, DH, DH), F32),
+        out_shape=jax.ShapeDtypeStruct((heads // 4, DH, DH), F32),
         in_specs=[IN_SMEM] + [IN_VMEM] * 2,
         out_specs=IN_VMEM,
         compiler_params=pltpu.CompilerParams(vmem_limit_bytes=4 * MIB),
@@ -138,12 +141,12 @@
 
 
 def second_kernel(quarter, rows, n_after, info, q, k, v, d, *refs):
-    sib, own, qv, kv, vv, dv, sems = refs[n_after:]
+    sib, own, kept, qv, kv, vv, dv, sems = refs[n_after:]
     width = q.shape[1]
     is_kv = info[EVEN] != 1
 
     def copies(n, side, *pair):
-        return pair_copies(info, side, width, rows, sems.at[n], *pair)
+        return pair_copies(half_cols(info, side, width), width // 2, rows, sems.at[n], *pair)
 
     keys, queries = ((k, kv), (v, vv)), ((q, qv), (d, dv))
 
@@ -167,6 +170,8 @@
     for n in (2, 3):
         for copy in copies(n, 1 - n % 2, *keys):
             copy.wait()
+    is_first = jnp.logical_not(is_kv)
+    state_products(is_first, 0, quarter, info, qv, kv, vv, dv, (kept, kept), (0,))
 
 
 def second_states(info, args, after):
@@ -176,9 +181,10 @@
     return pl.pallas_call(
         functools.partial(second_kernel, heads // 4, rows, len(after)),
         out_shape=[jax.ShapeDtypeStruct((heads // 2, DH, DH), F32)] * 2
+        + [jax.ShapeDtypeStruct((heads // 4, DH, DH), F32)]
         + [jax.ShapeDtypeStruct((count, width), BF16)] * 4,
         in_specs=[IN_SMEM] + [IN_HBM] * 4 + [IN_VMEM] * len(after),
-        out_specs=[IN_VMEM] * 6,
+        out_specs=[IN_VMEM] * 7,
         scratch_shapes=[pltpu.SemaphoreType.DMA((4, 2, count // rows))],
         compiler_params=pltpu.CompilerParams(vmem_limit_bytes=4 * MIB),
         cost_estimate=SMALL,
@@ -344,8 +350,9 @@
 
 
 def prepare_kernel(early, n_after, info, *refs):
-    near, f_own, f_got, f_got_give, f_keep, f_other, s_own, s_got, s_keep, s_other = refs[:10]
-    across, mine, theirs, rest_mine, rest_theirs = refs[10 + n_after :]
+    near, f_own, f_give, f_got, f_got_give, f_keep, f_other = refs[:7]
+    s_own, s_got, s_keep, s_other = refs[7:11]
+    across, mine, theirs, rest_mine, rest_theirs = refs[11 + n_after :]
     quarter = near.shape[0]
     is_kv = (info[EARLY_KV] == 1) if early else (info[EARLY_KV] != 1)
     is_first = (info[EVEN] == 1) == is_kv
@@ -362,7 +369,7 @@
         here = val + jnp.where(after_row, other, 0.0)
         mine[i] = here + jnp.where(after_core, got, 0.0)
         theirs[i] = here + jnp.where(after_core, 0.0, own)
-        own = jnp.where(is_first, f_own[quarter + i], s_own[quarter + i])
+        own = jnp.where(is_first, f_give[i], s_own[quarter + i])
         got = jnp.where(is_first, f_got_give[i], s_got[quarter + i])
         rest_mine[i] = jnp.where(after_core, got, 0.0)
         rest_theirs[i] = jnp.where(after_core, 0.0, own)
@@ -372,7 +379,7 @@
     return pl.pallas_call(
         functools.partial(prepare_kernel, early, len(after)),
         out_shape=[jax.ShapeDtypeStruct(near.shape, F32)] * 5,
-        in_specs=[IN_SMEM] + [IN_VMEM] * (10 + len(after)),
+        in_specs=[IN_SMEM] + [IN_VMEM] * (11 + len(after)),
         out_specs=[IN_VMEM] * 5,
         compiler_params=pltpu.CompilerParams(vmem_limit_bytes=4 * MIB),
         cost_estimate=SMALL,
@@ -427,18 +434,18 @@
     sib_keep, sib_give, left, right = first_state(info, far_args)
     got_give = send(sib_give, core_swap)
     got_keep = send(sib_keep, core_swap)
-    f_own = own_state(info, left, right)
-    f_give = f_own[quarter:] + got_give
-    f_keep = f_own[:quarter] + got_keep
+    own_give = own_state(info, left, right)
+    f_give = own_give + got_give
     f_other = send(f_give, row_swap)
-    s_sib, s_own, *args = second_states(info, far_args, (f_give,))
+    s_sib, s_own, f_own, *args = second_states(info, far_args, (f_give,))
+    f_keep = f_own + got_keep
     part_a, zero = local_part(info, args, kinds[:1], 0.0, (s_own,))
     s_got = send(s_sib, core_swap)
     s_keep, s_give = halves(s_own, s_got)
     f_total = f_keep + f_other + zero
     s_give, f_total = lax.optimization_barrier((s_give, f_total))
     s_other = send(s_give, row_swap)
-    f = f_own, got_keep, got_give, f_keep, f_other
+    f = f_own, own_give, got_keep, got_give, f_keep, f_other
     s = s_own, s_got, s_keep, s_other
     part_b, inside = local_part(info, args, kinds[1:], 1.0, (s_give,))
     partials = part_a | part_b

time: 46.8 us -> 46.9 us (level)
  transfers between devices with their start and end apart: 15 -> 15, of which waited for: 6 -> 6; matrix products, arithmetic and copies ran while one was open for 1% -> 1% of each run, Pallas kernels for 40% -> 41%
where the time goes in v9:
time: 46.9 us; the launch traced here: 46.7 us
  Pallas kernels  23.1 us (49%)
  starting transfers between devices  15.2 us (32%)
  waiting for transfers between devices  6.99 us (15%)
  between operations  0.9 us (2%)
    ppermute x15, starting transfers between devices, send(): return lax.ppermute(array, 'seq', pairs)  15.2 us
    pallas_call x2, Pallas kernels, local_part(): pl.pallas_call(functools.partial(local_kernel, kinds, quarter, mark, len(...  7.78 us
    pallas_call x4, Pallas kernels, apply_states(): pl.pallas_call(functools.partial(apply_kernel, early, kinds, len(arrays)...  7.5 us
    ppermute x15, waiting for transfers between devices, send(): return lax.ppermute(array, 'seq', pairs)  6.99 us
    pallas_call x1, Pallas kernels, second_states(): pl.pallas_call(functools.partial(second_kernel, heads // 4, rows, len(aft...  3.21 us
    pallas_call x1, Pallas kernels, first_state(): pl.pallas_call(functools.partial(first_kernel, heads // 4, rows), out_sha...  2.26 us
    pallas_call x2, Pallas kernels, prepare(): pl.pallas_call(functools.partial(prepare_kernel, early, len(after)), out_...  1.45 us
  transfers between devices with their start and end apart: 15, of which 6 were waited for; matrix products, arithmetic and copies ran while one was open for 1% of the time, Pallas kernels for 41%

profile of v9, /device:TPU:0, one launch (start us, length us, event | category | flops | bytes accessed | tf_op | source)
XLA Modules:
  0.0 46.7 jit_solution(14672519193887876792)
XLA Ops:
  0.7 0.1 stack.39.info
  0.8 2.3 %first.1 = (f32[4,128,128]{2,1,0:T(8,128)S(1)}, f32[4,128,128]{2,1,0:T(8,128)S(1)}, bf16[256,2048]{1,0:T(8,128)(2,1)S(1)}, bf16[256,2048]{1,0:T(8,128)(2,1)S(1)}) custom-call(s32[6]{0:T(128)S(1)} %stack.39.info, bf16[256,2048]{1,0:T(8,128)(2,1)} %q.3, bf16[256,2048]{1,0:T(8,128)(2,1)} %k.3, bf16[256,2048]{1,0:T(8,128)(2,1)} %v.3, bf16[256,2048]{1,0:T(8,128)(2,1)} %d.3), custom_call_target="tpu_custom_call" | custom-call | flops 1 | bytes 1 | tf_op jit(solution)/shard_map/first/pallas_call | solution.py:112
  3.0 0.5 %collective-permute-start = (f32[4,128,128]{2,1,0:T(8,128)S(1)}, f32[4,128,128]{2,1,0:T(8,128)S(1)}, u32[]{:S(2)}, u32[]{:S(2)}) collective-permute-start(f32[4,128,128]{2,1,0:T(8,128)S(1)} %get-tuple-element.61), channel_id=1, source_target_pairs={{0,1},{1,0},{2,3},{3,2},{4,5},{5,4},{6,7},{7,6},{8,9},{9,8},{10,11... | collective-permute-start | bytes 786440 | tf_op jit(solution)/shard_map/ppermute | solution.py:391
  3.6 0.1 collective-permute-start.2
  3.6 0.9 %own.1.refs_2_ = f32[4,128,128]{2,1,0:T(8,128)S(1)} custom-call(s32[6]{0:T(128)S(1)} %stack.39.info, bf16[256,2048]{1,0:T(8,128)(2,1)S(1)} %get-tuple-element.59.left, bf16[256,2048]{1,0:T(8,128)(2,1)S(1)} %get-tuple-element.60.right), custom_call_target="tpu_custom_call" | custom-call | flops 1 | bytes 1 | tf_op jit(solution)/shard_map/own/pallas_call | solution.py:132
  4.5 0.2 collective-permute-done.refs_4_
  4.8 3.0 %collective-permute-start.3 = (f32[4,128,128]{2,1,0:T(8,128)S(1)}, f32[4,128,128]{2,1,0:T(8,128)S(1)}, u32[]{:S(2)}, u32[]{:S(2)}) collective-permute-start(f32[4,128,128]{2,1,0:T(8,128)S(1)} %add.75.refs_0_), channel_id=1, source_target_pairs={{0,2},{1,3},{2,0},{3,1},{4,6},{5,7},{6,4},{7,5},{8,10},{9,11},{10,... | collective-permute-start | bytes 786440 | tf_op jit(solution)/shard_map/ppermute | solution.py:391
  7.7 3.2 %second.1 = (f32[8,128,128]{2,1,0:T(8,128)S(1)}, f32[8,128,128]{2,1,0:T(8,128)S(1)}, f32[4,128,128]{2,1,0:T(8,128)S(1)}, bf16[256,2048]{1,0:T(8,128)(2,1)S(1)}, ...) custom-call(s32[6]{0:T(128)S(1)} %stack.39.info, bf16[256,2048]{1,0:T(8,128)(2,1)} %q.3, ...), custom_call_target="tpu_custom_call" | custom-call | flops 1 | bytes 1 | tf_op jit(solution)/shard_map/second/pallas_call | solution.py:181
  10.9 0.1 collective-permute-start.1
  11.0 2.3 %local.2 = (f32[256,512]{1,0:T(8,128)S(1)}, f32[256,512]{1,0:T(8,128)S(1)}, f32[256,512]{1,0:T(8,128)S(1)}, f32[256,512]{1,0:T(8,128)S(1)}, f32[4,128,128]{2,1,0:T(8,128)S(1)}) custom-call(s32[6]{0:T(128)S(1)} %stack.39.info, bf16[256,2048]{1,0:T(8,128)(2,1)S(1)} %get-tuple-element.62.q.refs_0_, bf16[256,2048]{1,0:T(8,128)(2,1)S(1)} %get-tuple-element.63.k.refs_1_, ...), custom_call_target="tpu_custom_call" | custom-call | flops 1 | bytes 1 | tf_op jit(solution)/shard_map/local/pallas_call | solution.py:237
  13.3 1.0 %collective-permute-done.3.refs_6_ = f32[4,128,128]{2,1,0:T(8,128)S(1)} collective-permute-done((f32[4,128,128]{2,1,0:T(8,128)S(1)}, f32[4,128,128]{2,1,0:T(8,128)S(1)}, u32[]{:S(2)}, u32[]{:S(2)}) %collective-permute-start.3) | collective-permute-done | bytes 262176 | tf_op jit(solution)/shard_map/ppermute | solution.py:391
  14.4 1.9 %collective-permute-start.5 = (f32[4,128,128]{2,1,0:T(8,128)S(1)}, f32[4,128,128]{2,1,0:T(8,128)S(1)}, u32[]{:S(2)}, u32[]{:S(2)}) collective-permute-start(f32[4,128,128]{2,1,0:T(8,128)S(1)} %get-tuple-element.81), channel_id=1, source_target_pairs={{0,4},{1,5},{2,6},{3,7},{4,0},{5,1},{6,2},{7,3},{8,12},{9,13},{10,... | collective-permute-start | bytes 786440 | tf_op jit(solution)/shard_map/ppermute | solution.py:391
  16.3 1.5 %collective-permute-start.4 = (f32[4,128,128]{2,1,0:T(8,128)S(1)}, f32[4,128,128]{2,1,0:T(8,128)S(1)}, u32[]{:S(2)}, u32[]{:S(2)}) collective-permute-start(f32[4,128,128]{2,1,0:T(8,128)S(1)} %slice_add_fusion.1.refs_0_), channel_id=1, source_target_pairs={{0,2},{1,3},{2,0},{3,1},{4,6},{5,7},{6,4},{7,5},{8,10},{9,11},{10,... | collective-permute-start | bytes 786440 | tf_op jit(solution)/shard_map/ppermute | solution.py:391
  17.9 5.5 %local.3 = (f32[256,512]{1,0:T(8,128)S(1)}, f32[256,512]{1,0:T(8,128)S(1)}, f32[256,512]{1,0:T(8,128)S(1)}, f32[256,512]{1,0:T(8,128)S(1)}, f32[256,512]{1,0:T(8...) custom-call(s32[6]{0:T(128)S(1)} %stack.39.info, ...), custom_call_target="tpu_custom_call" | custom-call | flops 1 | bytes 1 | tf_op jit(solution)/shard_map/local/pallas_call | solution.py:237
  23.4 0.2 collective-permute-done.4.refs_10_
  23.7 0.1 collective-permute-start.6
  23.7 0.7 %prepare.2 = (f32[4,128,128]{2,1,0:T(8,128)S(1)}, f32[4,128,128]{2,1,0:T(8,128)S(1)}, f32[4,128,128]{2,1,0:T(8,128)S(1)}, f32[4,128,128]{2,1,0:T(8,128)S(1)}, f32[4,128,128]{2,1,0:T(8,128)S(1)}) custom-call(s32[6]{0:T(128)S(1)} %stack.39.info, f32[4,128,128]{2,1,0:T(8,128)S(1)} %collective-permute-done.5.refs_0_, ...), custom_call_target="tpu_custom_call" | custom-call | flops 1 | bytes 1 | tf_op jit(solution)/shard_map/prepare/pallas_call | solution.py:379
  24.5 0.6 %collective-permute-start.12 = (f32[4,128,128]{2,1,0:T(8,128)S(1)}, f32[4,128,128]{2,1,0:T(8,128)S(1)}, u32[]{:S(2)}, u32[]{:S(2)}) collective-permute-start(f32[4,128,128]{2,1,0:T(8,128)S(1)} %get-tuple-element.97), channel_id=1, source_target_pairs={{0,1},{1,0},{2,3},{3,2},{4,5},{5,4},{6,7},{7,6},{8,9},{9,8},{10,11... | collective-permute-start | bytes 786440 | tf_op jit(solution)/shard_map/ppermute | solution.py:391
  25.0 1.5 %collective-permute-start.11 = (f32[4,128,128]{2,1,0:T(8,128)S(1)}, f32[4,128,128]{2,1,0:T(8,128)S(1)}, u32[]{:S(2)}, u32[]{:S(2)}) collective-permute-start(f32[4,128,128]{2,1,0:T(8,128)S(1)} %get-tuple-element.82.refs_11_.refs_14_), channel_id=1, source_target_pairs={{0,2},{1,3},{2,0},{3,1},{4,6},{5,7},{6,4},{7,5},{8,10},{9,11},{10,... | collective-permute-start | bytes 786440 | tf_op jit(solution)/shard_map/ppermute | solution.py:391
  26.5 0.7 %prepare.3 = (f32[4,128,128]{2,1,0:T(8,128)S(1)}, f32[4,128,128]{2,1,0:T(8,128)S(1)}, f32[4,128,128]{2,1,0:T(8,128)S(1)}, f32[4,128,128]{2,1,0:T(8,128)S(1)}, f32[4,128,128]{2,1,0:T(8,128)S(1)}) custom-call(s32[6]{0:T(128)S(1)} %stack.39.info, f32[4,128,128]{2,1,0:T(8,128)S(1)} %collective-permute-done.5.refs_0_, ...), custom_call_target="tpu_custom_call" | custom-call | flops 1 | bytes 1 | tf_op jit(solution)/shard_map/prepare/pallas_call | solution.py:379
  27.3 4.6 %collective-permute-start.7 = (f32[4,128,128]{2,1,0:T(8,128)S(1)}, f32[4,128,128]{2,1,0:T(8,128)S(1)}, u32[]{:S(2)}, u32[]{:S(2)}) collective-permute-start(f32[4,128,128]{2,1,0:T(8,128)S(1)} %collective-permute-done.6), channel_id=1, source_target_pairs={{0,4},{1,5},{2,6},{3,7},{4,0},{5,1},{6,2},{7,3},{8,12},{9,13},{10,... | collective-permute-start | bytes 786440 | tf_op jit(solution)/shard_map/ppermute | solution.py:391
  31.9 1.9 %apply.4 = (bf16[256,2048]{1,0:T(8,128)(2,1)}, bf16[256,2048]{1,0:T(8,128)(2,1)}, bf16[256,2048]{1,0:T(8,128)(2,1)}, bf16[256,2048]{1,0:T(8,128)(2,1)}, f32[4,128,128]{2,1,0:T(8,128)S(1)}) custom-call(s32[6]{0:T(128)S(1)} %stack.39.info, bf16[256,2048]{1,0:T(8,128)(2,1)S(1)} %get-tuple-element.62.q.refs_0_, ...), custom_call_target="tpu_custom_call" | custom-call | flops 1 | bytes 1 | tf_op jit(solution)/shard_map/apply/pallas_call | solution.py:329
  33.8 0.1 fusion.2
  34.0 2.7 %collective-permute-done.7 = f32[4,128,128]{2,1,0:T(8,128)S(1)} collective-permute-done((f32[4,128,128]{2,1,0:T(8,128)S(1)}, f32[4,128,128]{2,1,0:T(8,128)S(1)}, u32[]{:S(2)}, u32[]{:S(2)}) %collective-permute-start.7) | collective-permute-done | bytes 262176 | tf_op jit(solution)/shard_map/ppermute | solution.py:391
  36.8 0.7 %collective-permute-start.8 = (f32[4,128,128]{2,1,0:T(8,128)S(1)}, f32[4,128,128]{2,1,0:T(8,128)S(1)}, u32[]{:S(2)}, u32[]{:S(2)}) collective-permute-start(f32[4,128,128]{2,1,0:T(8,128)S(1)} %get-tuple-element.114.refs_18_), channel_id=1, source_target_pairs={{0,2},{1,3},{2,0},{3,1},{4,6},{5,7},{6,4},{7,5},{8,10},{9,11},{10,... | collective-permute-start | bytes 786440 | tf_op jit(solution)/shard_map/ppermute | solution.py:391
  37.5 0.1 collective-permute-start.10
  37.6 0.5 %collective-permute-start.9 = (f32[2,128,128]{2,1,0:T(8,128)S(1)}, f32[2,128,128]{2,1,0:T(8,128)S(1)}, u32[]{:S(2)}, u32[]{:S(2)}) collective-permute-start(f32[2,128,128]{2,1,0:T(8,128)S(1)} %get-tuple-element.121), channel_id=1, source_target_pairs={{0,1},{1,0},{2,3},{3,2},{4,5},{5,4},{6,7},{7,6},{8,9},{9,8},{10,11... | collective-permute-start | bytes 393224 | tf_op jit(solution)/shard_map/ppermute | solution.py:391
  38.1 1.9 %apply.5 = (bf16[256,2048]{1,0:T(8,128)(2,1)}, bf16[256,2048]{1,0:T(8,128)(2,1)}, bf16[256,2048]{1,0:T(8,128)(2,1)}, bf16[256,2048]{1,0:T(8,128)(2,1)}) custom-call(s32[6]{0:T(128)S(1)} %stack.39.info, bf16[256,2048]{1,0:T(8,128)(2,1)S(1)} %get-tuple-element.62.q.refs_0_, ...), custom_call_target="tpu_custom_call", output_to_operand_aliasing={{0}: (15, {}), {1}: (16, {}), {2}: (17, {}), {3}: (18, {})} | custom-call | flops 1 | bytes 1 | tf_op jit(solution)/shard_map/apply/pallas_call | solution.py:329
  40.0 1.8 %apply.6 = (bf16[256,2048]{1,0:T(8,128)(2,1)}, bf16[256,2048]{1,0:T(8,128)(2,1)}, bf16[256,2048]{1,0:T(8,128)(2,1)}, bf16[256,2048]{1,0:T(8,128)(2,1)}, f32[4,128,128]{2,1,0:T(8,128)S(1)}) custom-call(s32[6]{0:T(128)S(1)} %stack.39.info, ...), custom_call_target="tpu_custom_call", output_to_operand_aliasing={{0}: (17, {}), {1}: (18, {}), {2}: (19, {}), {3}: (20, {})} | custom-call | flops 1 | bytes 1 | tf_op jit(solution)/shard_map/apply/pallas_call | solution.py:329
  41.9 1.3 %collective-permute-done.8 = f32[4,128,128]{2,1,0:T(8,128)S(1)} collective-permute-done((f32[4,128,128]{2,1,0:T(8,128)S(1)}, f32[4,128,128]{2,1,0:T(8,128)S(1)}, u32[]{:S(2)}, u32[]{:S(2)}) %collective-permute-start.8) | collective-permute-done | bytes 262176 | tf_op jit(solution)/shard_map/ppermute | solution.py:391
  43.4 1.5 %collective-permute-done.14.refs_13_ = f32[4,128,128]{2,1,0:T(8,128)S(1)} collective-permute-done((f32[4,128,128]{2,1,0:T(8,128)S(1)}, f32[4,128,128]{2,1,0:T(8,128)S(1)}, u32[]{:S(2)}, u32[]{:S(2)}) %collective-permute-start.14) | collective-permute-done | bytes 262176 | tf_op jit(solution)/shard_map/ppermute | solution.py:391
  44.9 1.9 %apply.7 = (bf16[256,2048]{1,0:T(8,128)(2,1)}, bf16[256,2048]{1,0:T(8,128)(2,1)}, bf16[256,2048]{1,0:T(8,128)(2,1)}, bf16[256,2048]{1,0:T(8,128)(2,1)}) custom-call(s32[6]{0:T(128)S(1)} %stack.39.info, bf16[256,2048]{1,0:T(8,128)(2,1)S(1)} %get-tuple-element.62.q.refs_0_, ...), custom_call_target="tpu_custom_call", output_to_operand_aliasing={{0}: (15, {}), {1}: (16, {}), {2}: (17, {}), {3}: (18, {})} | custom-call | flops 1 | bytes 1 | tf_op jit(solution)/shard_map/apply/pallas_call | solution.py:329
  (18 shorter events, 0.5 us)
Async XLA Ops:
  3.0 1.7 %collective-permute-start = (f32[4,128,128]{2,1,0:T(8,128)S(1)}, f32[4,128,128]{2,1,0:T(8,128)S(1)}, u32[]{:S(2)}, u32[]{:S(2)}) collective-permute-start(f32[4,128,128]{2,1,0:T(8,128)S(1)} %get-tuple-element.61), channel_id=1, source_target_pairs={{0,1},{1,0},{2,3},{3,2},{4,5},{5,4},{6,7},{7,6},{8,9},{9,8},{10,11... | collective-permute-start | bytes 786440 | tf_op jit(solution)/shard_map/ppermute | solution.py:391
  3.6 9.7 %collective-permute-start.2 = (f32[4,128,128]{2,1,0:T(8,128)S(1)}, f32[4,128,128]{2,1,0:T(8,128)S(1)}, u32[]{:S(2)}, u32[]{:S(2)}) collective-permute-start(f32[4,128,128]{2,1,0:T(8,128)S(1)} %get-tuple-element.69), channel_id=1, source_target_pairs={{0,1},{1,0},{2,3},{3,2},{4,5},{5,4},{6,7},{7,6},{8,9},{9,8},{10,11... | collective-permute-start | bytes 786440 | tf_op jit(solution)/shard_map/ppermute | solution.py:391
  4.8 9.6 %collective-permute-start.3 = (f32[4,128,128]{2,1,0:T(8,128)S(1)}, f32[4,128,128]{2,1,0:T(8,128)S(1)}, u32[]{:S(2)}, u32[]{:S(2)}) collective-permute-start(f32[4,128,128]{2,1,0:T(8,128)S(1)} %add.75.refs_0_), channel_id=1, source_target_pairs={{0,2},{1,3},{2,0},{3,1},{4,6},{5,7},{6,4},{7,5},{8,10},{9,11},{10,... | collective-permute-start | bytes 786440 | tf_op jit(solution)/shard_map/ppermute | solution.py:391
  10.9 3.4 %collective-permute-start.1 = (f32[8,128,128]{2,1,0:T(8,128)S(1)}, f32[8,128,128]{2,1,0:T(8,128)S(1)}, u32[]{:S(2)}, u32[]{:S(2)}) collective-permute-start(f32[8,128,128]{2,1,0:T(8,128)S(1)} %get-tuple-element.67), channel_id=1, source_target_pairs={{0,1},{1,0},{2,3},{3,2},{4,5},{5,4},{6,7},{7,6},{8,9},{9,8},{10,11... | collective-permute-start | bytes 1572872 | tf_op jit(solution)/shard_map/ppermute | solution.py:391
  14.4 9.0 %collective-permute-start.5 = (f32[4,128,128]{2,1,0:T(8,128)S(1)}, f32[4,128,128]{2,1,0:T(8,128)S(1)}, u32[]{:S(2)}, u32[]{:S(2)}) collective-permute-start(f32[4,128,128]{2,1,0:T(8,128)S(1)} %get-tuple-element.81), channel_id=1, source_target_pairs={{0,4},{1,5},{2,6},{3,7},{4,0},{5,1},{6,2},{7,3},{8,12},{9,13},{10,... | collective-permute-start | bytes 786440 | tf_op jit(solution)/shard_map/ppermute | solution.py:391
  16.3 7.2 %collective-permute-start.4 = (f32[4,128,128]{2,1,0:T(8,128)S(1)}, f32[4,128,128]{2,1,0:T(8,128)S(1)}, u32[]{:S(2)}, u32[]{:S(2)}) collective-permute-start(f32[4,128,128]{2,1,0:T(8,128)S(1)} %slice_add_fusion.1.refs_0_), channel_id=1, source_target_pairs={{0,2},{1,3},{2,0},{3,1},{4,6},{5,7},{6,4},{7,5},{8,10},{9,11},{10,... | collective-permute-start | bytes 786440 | tf_op jit(solution)/shard_map/ppermute | solution.py:391
  23.7 3.6 %collective-permute-start.6 = (f32[4,128,128]{2,1,0:T(8,128)S(1)}, f32[4,128,128]{2,1,0:T(8,128)S(1)}, u32[]{:S(2)}, u32[]{:S(2)}) collective-permute-start(f32[4,128,128]{2,1,0:T(8,128)S(1)} %get-tuple-element.116), channel_id=1, source_target_pairs={{4,8},{5,9},{6,10},{7,11},{8,4},{9,5},{10,6},{11,7},{0,1},{1,0},{2... | collective-permute-start | bytes 786440 | tf_op jit(solution)/shard_map/ppermute | solution.py:391
  24.5 7.5 %collective-permute-start.12 = (f32[4,128,128]{2,1,0:T(8,128)S(1)}, f32[4,128,128]{2,1,0:T(8,128)S(1)}, u32[]{:S(2)}, u32[]{:S(2)}) collective-permute-start(f32[4,128,128]{2,1,0:T(8,128)S(1)} %get-tuple-element.97), channel_id=1, source_target_pairs={{0,1},{1,0},{2,3},{3,2},{4,5},{5,4},{6,7},{7,6},{8,9},{9,8},{10,11... | collective-permute-start | bytes 786440 | tf_op jit(solution)/shard_map/ppermute | solution.py:391
  25.0 8.8 %collective-permute-start.11 = (f32[4,128,128]{2,1,0:T(8,128)S(1)}, f32[4,128,128]{2,1,0:T(8,128)S(1)}, u32[]{:S(2)}, u32[]{:S(2)}) collective-permute-start(f32[4,128,128]{2,1,0:T(8,128)S(1)} %get-tuple-element.82.refs_11_.refs_14_), channel_id=1, source_target_pairs={{0,2},{1,3},{2,0},{3,1},{4,6},{5,7},{6,4},{7,5},{8,10},{9,11},{10,... | collective-permute-start | bytes 786440 | tf_op jit(solution)/shard_map/ppermute | solution.py:391
  27.3 9.4 %collective-permute-start.7 = (f32[4,128,128]{2,1,0:T(8,128)S(1)}, f32[4,128,128]{2,1,0:T(8,128)S(1)}, u32[]{:S(2)}, u32[]{:S(2)}) collective-permute-start(f32[4,128,128]{2,1,0:T(8,128)S(1)} %collective-permute-done.6), channel_id=1, source_target_pairs={{0,4},{1,5},{2,6},{3,7},{4,0},{5,1},{6,2},{7,3},{8,12},{9,13},{10,... | collective-permute-start | bytes 786440 | tf_op jit(solution)/shard_map/ppermute | solution.py:391
  33.9 4.1 %collective-permute-start.13 = (f32[4,128,128]{2,1,0:T(8,128)S(1)}, f32[4,128,128]{2,1,0:T(8,128)S(1)}, u32[]{:S(2)}, u32[]{:S(2)}) collective-permute-start(f32[4,128,128]{2,1,0:T(8,128)S(1)} %get-tuple-element.126), channel_id=1, source_target_pairs={{0,1},{1,0},{2,3},{3,2},{4,5},{5,4},{6,7},{7,6},{8,9},{9,8},{10,11... | collective-permute-start | bytes 786440 | tf_op jit(solution)/shard_map/ppermute | solution.py:391
  36.8 6.4 %collective-permute-start.8 = (f32[4,128,128]{2,1,0:T(8,128)S(1)}, f32[4,128,128]{2,1,0:T(8,128)S(1)}, u32[]{:S(2)}, u32[]{:S(2)}) collective-permute-start(f32[4,128,128]{2,1,0:T(8,128)S(1)} %get-tuple-element.114.refs_18_), channel_id=1, source_target_pairs={{0,2},{1,3},{2,0},{3,1},{4,6},{5,7},{6,4},{7,5},{8,10},{9,11},{10,... | collective-permute-start | bytes 786440 | tf_op jit(solution)/shard_map/ppermute | solution.py:391
  37.5 2.5 %collective-permute-start.10 = (f32[2,128,128]{2,1,0:T(8,128)S(1)}, f32[2,128,128]{2,1,0:T(8,128)S(1)}, u32[]{:S(2)}, u32[]{:S(2)}) collective-permute-start(f32[2,128,128]{2,1,0:T(8,128)S(1)} %get-tuple-element.120), channel_id=1, source_target_pairs={{0,1},{1,0},{2,3},{3,2},{4,5},{5,4},{6,7},{7,6},{8,9},{9,8},{10,11... | collective-permute-start | bytes 393224 | tf_op jit(solution)/shard_map/ppermute | solution.py:391
  37.6 2.4 %collective-permute-start.9 = (f32[2,128,128]{2,1,0:T(8,128)S(1)}, f32[2,128,128]{2,1,0:T(8,128)S(1)}, u32[]{:S(2)}, u32[]{:S(2)}) collective-permute-start(f32[2,128,128]{2,1,0:T(8,128)S(1)} %get-tuple-element.121), channel_id=1, source_target_pairs={{0,1},{1,0},{2,3},{3,2},{4,5},{5,4},{6,7},{7,6},{8,9},{9,8},{10,11... | collective-permute-start | bytes 393224 | tf_op jit(solution)/shard_map/ppermute | solution.py:391
  43.3 1.6 %collective-permute-start.14 = (f32[4,128,128]{2,1,0:T(8,128)S(1)}, f32[4,128,128]{2,1,0:T(8,128)S(1)}, u32[]{:S(2)}, u32[]{:S(2)}) collective-permute-start(f32[4,128,128]{2,1,0:T(8,128)S(1)} %get-tuple-element.124), channel_id=1, source_target_pairs={{0,1},{1,0},{2,3},{3,2},{4,5},{5,4},{6,7},{7,6},{8,9},{9,8},{10,11... | collective-permute-start | bytes 786440 | tf_op jit(solution)/shard_map/ppermute | solution.py:391
